TPU v7x, 768 devices: a whole 4x8x12 slice. The times are simulated.
768 devices in a mesh: dom: 12 (over z), inner: 64 (over x, y, core).
Axes of the slice: x: 4, y: 8, z: 12, core: 2. Of those that a mesh axis runs over, the one named last changes fastest.
Arguments:
- features: bfloat16 [786432, 256], P(('dom', 'inner')), may hold values from -6 to 6
- tiles: bfloat16 [6144, 8, 128, 128], P(('dom', 'inner')), may hold values from 0 to 1, as said below
- pair_source: int32 [6144, 8], P(('dom', 'inner')), may hold values from 0 to 21, as said below
- in_degree: int32 [786432], P(('dom', 'inner')), may hold values from 1 to 1056, as said below
- send_blocks: int32 [768, 12], P(('dom', 'inner')), may hold values from 0 to 7
- w_self: bfloat16 [256, 256], replicated, may hold values from -0.375 to 0.375
- w_neigh: bfloat16 [256, 256], replicated, may hold values from -3 to 3
- bias: float32 [256], replicated, may hold values from -3 to 3
- cotangent: bfloat16 [786432, 256], P(('dom', 'inner')), may hold values from -6 to 6
Outputs:
- layer_out: bfloat16 [786432, 256], P(('dom', 'inner'))
- grad_features: bfloat16 [786432, 256], P(('dom', 'inner'))
- grad_self: float32 [256, 256], replicated
- grad_neigh: float32 [256, 256], replicated
- grad_bias: float32 [256], replicated
Inputs may be any that keep to these rules, and one draw needn't show every extreme that they name: `pair_source`: every device's 8 * 8 pairs name each of its 22 table entries at least once. `in_degree`: each node's in-degree is at least one more than the number of ones in its rows of its block's tiles. `tiles`: entries are 0 or 1.
All inputs are finite; a program needn't handle non-finite values.
Results may differ from a plain program's by a relative error of at most 0.0075.
Values may be sent and summed in bfloat16 or wider, within the bound.
No kernel may reach another device: no remote copies, remote signals or barrier semaphores. Data moves between devices by JAX's collectives and lax.ppermute only.
A program may use at most 64 MiB of HBM per device.

v0:
```python
import math

import jax
import jax.numpy as jnp
from jax import lax
from jax.sharding import PartitionSpec as P


def with_halo(block, sides, width):
    for axis, dim in sides:
        count = lax.axis_size(axis)
        forward = [(i, i + 1) for i in range(count - 1)]
        backward = [(target, source) for source, target in forward]
        low = lax.ppermute(
            lax.slice_in_dim(block, block.shape[dim] - width, None, axis=dim), axis, forward
        )
        high = lax.ppermute(lax.slice_in_dim(block, 0, width, axis=dim), axis, backward)
        block = jnp.concatenate([low, block, high], axis=dim)
    return block


def per_device(
    features, tiles, pair_source, in_degree, send_blocks, w_self, w_neigh, bias, cotangent
):
    rows_dev, width = features.shape
    nblocks = tiles.shape[0]
    npairs = tiles.shape[1]
    block_rows = tiles.shape[2]
    dom_size = lax.axis_size("dom")
    entries = nblocks + 2 + dom_size
    blocks = features.reshape(nblocks, block_rows, width)
    padded = with_halo(features, (("inner", 0),), block_rows)
    left_rim = padded[:block_rows]
    right_rim = padded[rows_dev + block_rows :]
    block_range = jnp.arange(nblocks, dtype=jnp.int32)
    chosen = (send_blocks[0][:, None] == block_range[None, :]).astype(jnp.bfloat16)
    outgoing = jnp.einsum("jb,brf->jrf", chosen, blocks, preferred_element_type=jnp.float32).astype(
        jnp.bfloat16
    )
    received = lax.all_to_all(outgoing, "dom", split_axis=0, concat_axis=0, tiled=True)
    source_table = jnp.concatenate([blocks, left_rim[None], right_rim[None], received], axis=0)
    flat_pairs = pair_source.reshape(nblocks * npairs)
    selector = flat_pairs[:, None] == jnp.arange(entries, dtype=jnp.int32)[None, :]
    sources = jnp.einsum(
        "nt,tjf->njf",
        selector.astype(jnp.bfloat16),
        source_table,
        preferred_element_type=jnp.float32,
    ).astype(jnp.bfloat16)
    sources = sources.reshape(nblocks, npairs, block_rows, width)
    summed = jnp.einsum("bpij,bpjf->bif", tiles, sources, preferred_element_type=jnp.float32)
    degree = in_degree.astype(jnp.float32)[:, None]
    mean_agg = (summed.reshape(rows_dev, width) / degree).astype(jnp.bfloat16)
    preact = (
        jnp.dot(features, w_self, preferred_element_type=jnp.float32)
        + jnp.dot(mean_agg, w_neigh, preferred_element_type=jnp.float32)
        + bias
    )
    sigma = jax.nn.sigmoid(preact)
    layer_out = (preact * sigma).astype(jnp.bfloat16)
    grad_pre = (cotangent.astype(jnp.float32) * sigma * (1.0 + preact * (1.0 - sigma))).astype(
        jnp.bfloat16
    )
    contract_rows = (((0,), (0,)), ((), ()))
    contract_cols = (((1,), (1,)), ((), ()))
    local_self = lax.dot_general(
        features, grad_pre, contract_rows, preferred_element_type=jnp.float32
    )
    local_neigh = lax.dot_general(
        mean_agg, grad_pre, contract_rows, preferred_element_type=jnp.float32
    )
    local_bias = jnp.sum(grad_pre.astype(jnp.float32), axis=0)
    grad_mean = (
        lax.dot_general(grad_pre, w_neigh, contract_cols, preferred_element_type=jnp.float32)
        / degree
    )
    grad_mean = grad_mean.astype(jnp.bfloat16).reshape(nblocks, block_rows, width)
    pair_grads = jnp.einsum("bpij,bif->bpjf", tiles, grad_mean, preferred_element_type=jnp.float32)
    pair_grads = pair_grads.reshape(nblocks * npairs, block_rows, width)
    entry_grads = jax.ops.segment_sum(pair_grads, flat_pairs, num_segments=entries)
    rim_grads = jnp.concatenate([entry_grads[nblocks], entry_grads[nblocks + 1]], axis=0)
    returned_rims = with_halo(rim_grads.astype(jnp.bfloat16), (("inner", 0),), block_rows).astype(
        rim_grads.dtype
    )
    slot_grads = entry_grads[nblocks + 2 :].astype(jnp.bfloat16)
    returned = lax.all_to_all(slot_grads, "dom", split_axis=0, concat_axis=0, tiled=True)
    sent_map = (send_blocks[0][:, None] == block_range[None, :]).astype(jnp.bfloat16)
    returned_sum = jnp.einsum("jb,jrf->brf", sent_map, returned, preferred_element_type=jnp.float32)
    self_part = lax.dot_general(grad_pre, w_self, contract_cols, preferred_element_type=jnp.float32)
    total = self_part.reshape(nblocks, block_rows, width) + entry_grads[:nblocks] + returned_sum
    total = total.at[0].add(returned_rims[:block_rows])
    total = total.at[nblocks - 1].add(returned_rims[3 * block_rows :])
    sum_self, sum_neigh, sum_bias = lax.psum(
        (local_self, local_neigh, local_bias), ("dom", "inner")
    )
    grad_scale = 1.0 / math.sqrt(rows_dev * dom_size * lax.axis_size("inner"))
    grad_features = total.reshape(rows_dev, width).astype(jnp.bfloat16)
    return (
        layer_out,
        grad_features,
        sum_self * grad_scale,
        sum_neigh * grad_scale,
        sum_bias * grad_scale,
    )


def solution(mesh):
    return jax.shard_map(
        per_device,
        mesh=mesh,
        in_specs=(
            P(("dom", "inner"), None),
            P(("dom", "inner"), None, None, None),
            P(("dom", "inner"), None),
            P(("dom", "inner")),
            P(("dom", "inner"), None),
            P(),
            P(),
            P(),
            P(("dom", "inner"), None),
        ),
        out_specs=(P(("dom", "inner"), None), P(("dom", "inner"), None), P(), P(), P()),
        check_vma=False,
    )
```

profile of v0, /device:TPU:1, one launch (start us, length us, event | category | flops | bytes accessed | tf_op | source)
XLA Modules:
  0.0 602.2 jit_solution(5114425694367850396)
XLA Ops:
  7.2 0.0 copy-start
  7.2 0.0 copy-start.1
  7.2 1.6 convolution_convert_fusion
  8.8 0.0 copy-start.7
  8.8 0.0 copy-start.2
  8.9 1.1 copy.66
  10.0 15.7 %all-to-all-start = ((bf16[12,128,256]{2,1,0:T(8,128)(2,1)}), bf16[12,128,256]{2,1,0:T(8,128)(2,1)S(1)}, u32[]{:S(2)}, u32[]{:S(2)}) async-start(bf16[12,128,256]{2,1,0:T(8,128)(2,1)} %copy.66), calls=%async_computation | async-start | bytes 1572864 | tf_op jit(solution)/shard_map/all_to_all | solution.py:40
  25.7 0.7 fusion.38
  26.4 4.0 collective-permute-start
  30.4 1.9 collective-permute-start.1
  32.4 2.2 fusion.39
  34.5 1.1 copy.67
  35.6 0.0 copy-done.7
  35.6 0.1 eq.16
  35.7 0.0 copy-done.2
  35.7 2.9 copy.71
  38.6 0.0 copy-done.8
  38.6 0.0 collective-permute-done
  38.6 1.6 copy.68
  40.2 0.0 collective-permute-done.1
  40.2 1.6 copy.69
  41.8 12.0 %all-to-all-done = bf16[12,128,256]{2,1,0:T(8,128)(2,1)S(1)} async-done(((bf16[12,128,256]{2,1,0:T(8,128)(2,1)}), bf16[12,128,256]{2,1,0:T(8,128)(2,1)S(1)}, u32[]{:S(2)}, u32[]{:S(2)}) %all-to-all-start) | async-done | bytes 786464 | tf_op jit(solution)/shard_map/all_to_all | solution.py:40
  53.8 1.5 copy.70
  55.3 5.2 fusion
  60.5 1.4 fusion.21
  62.0 2.9 convert_reduce_fusion
  64.9 0.8 copy-done.3
  65.7 0.3 fusion.20
  66.0 4.5 fusion.41
  70.5 9.0 %copy.73 = f32[64,128,256]{2,1,0:T(8,128)} copy(f32[64,128,256]{1,2,0:T(8,128)} %bitcast.58) | data formatting | bytes 16777216 | tf_op jit(solution)/shard_map/reshape | solution.py:79
  79.5 0.3 broadcast_in_dim.16
  79.8 12.5 %scatter_fusion = f32[22,128,256]{2,1,0:T(8,128)S(1)} fusion(f32[22,128,256]{2,1,0:T(8,128)S(1)} %broadcast_in_dim.16, s32[64]{0:T(128)S(1)} %eq.16, f32[64,128,256]{2,1,0:T(8,128)} %copy.73), kind=kCustom, calls=%fused_computation | custom fusion | flops 2097152 | bytes 25166080 | tf_op jit(solution)/shard_map/scatter-add | solution.py:80
  92.3 0.2 convert.9
  92.5 1.1 copy-done.5
  93.6 0.9 slice.84
  94.5 7.6 %all-to-all-start.1 = ((bf16[12,128,256]{2,1,0:T(8,128)(2,1)}), bf16[12,128,256]{2,1,0:T(8,128)(2,1)}, u32[]{:S(2)}, u32[]{:S(2)}) async-start(bf16[12,128,256]{2,1,0:T(8,128)(2,1)} %slice.84), calls=%async_computation.1 | async-start | bytes 1572864 | tf_op jit(solution)/shard_map/all_to_all | solution.py:86
  102.1 0.0 all-reduce.3.cloned.1.call-start
  102.2 1.5 slice_bitcast_fusion.1
  103.7 4.1 collective-permute-start.2
  107.8 1.9 collective-permute-start.3
  109.7 2.2 fusion.42
  112.0 2.1 convolution_bitcast_fusion
  114.0 0.0 all-reduce.3.cloned.1.call-update
  114.1 112.9 %psum.23 = f32[256]{0:T(256)S(1)} all-reduce(f32[256]{0:T(256)S(1)} %get-tuple-element.56), channel_id=1, replica_groups=mesh['dom'=12,'inner'=64] {'dom','inner'}, use_global_device_ids=true, to_apply=%region_4.0 | all-reduce | flops 256 | bytes 2048 | tf_op jit(solution)/shard_map/psum | solution.py:93
  226.9 2.4 fusion.40
  229.3 0.6 broadcast_multiply_fusion.2
  229.9 1.1 slice.83
  231.0 0.0 collective-permute-done.2
  231.0 0.0 collective-permute-done.3
  231.0 0.9 fusion.24
  232.0 351.9 %all-reduce.3.cloned.1.call-done = (f32[256,256]{0,1:T(8,128)}, f32[256,256]{0,1:T(8,128)}) async-done(((f32[256,256]{0,1:T(8,128)}, f32[256,256]{0,1:T(8,128)}), (f32[256,256]{0,1:T(8,128)}, f32[256,256]{0,1:T(8,128)})) %all-reduce.3.cloned.1.call-update) | async-done | bytes 524304 | tf_op jit(solution)/shard_map/psum | solution.py:93
  583.8 1.1 broadcast_multiply_fusion
  584.9 0.8 copy.81
  585.8 0.8 copy.82
  586.6 0.0 all-to-all-done.1
  586.6 3.0 convolution_add_fusion.1
  589.6 0.1 slice.85
  589.7 0.9 fusion.23
  590.6 0.1 copy.78
  590.7 1.7 scatter-add.18
  592.5 0.2 slice_add_fusion
  592.6 1.7 scatter-add.19
  594.4 0.1 convert_element_type.50
  594.4 0.9 copy.79
  (16 shorter events, 0.0 us)
Async XLA Ops:
  7.2 54.8 %copy-start = (bf16[256,256]{1,0:T(8,128)(2,1)S(1)}, bf16[256,256]{1,0:T(8,128)(2,1)}, u32[]{:S(2)}) copy-start(bf16[256,256]{1,0:T(8,128)(2,1)} %param.19) | copy-start | bytes 393220
  7.2 18.5 %copy-start.1 = (bf16[1024,256]{1,0:T(8,128)(2,1)S(1)}, bf16[1024,256]{1,0:T(8,128)(2,1)}, u32[]{:S(2)}) copy-start(bf16[1024,256]{1,0:T(8,128)(2,1)} %param.13) | copy-start | bytes 1572868
  8.8 26.8 %copy-start.7 = (s32[8,8]{1,0:T(8,128)S(1)}, s32[8,8]{1,0:T(8,128)}, u32[]{:S(2)}) copy-start(s32[8,8]{1,0:T(8,128)} %param.15) | copy-start | bytes 772
  8.8 26.9 %copy-start.2 = (bf16[8,8,128,128]{3,2,1,0:T(8,128)(2,1)S(1)}, bf16[8,8,128,128]{3,2,1,0:T(8,128)(2,1)}, u32[]{:S(2)}) copy-start(bf16[8,8,128,128]{3,2,1,0:T(8,128)(2,1)} %param.14) | copy-start | bytes 6291460
  10.0 43.9 %all-to-all-start = ((bf16[12,128,256]{2,1,0:T(8,128)(2,1)}), bf16[12,128,256]{2,1,0:T(8,128)(2,1)S(1)}, u32[]{:S(2)}, u32[]{:S(2)}) async-start(bf16[12,128,256]{2,1,0:T(8,128)(2,1)} %copy.66), calls=%async_computation | async-start | bytes 1572864 | tf_op jit(solution)/shard_map/all_to_all | solution.py:40
  26.4 12.2 %collective-permute-start = (bf16[128,256]{1,0:T(8,128)(2,1)}, bf16[128,256]{1,0:T(8,128)(2,1)}, u32[]{:S(2)}, u32[]{:S(2)}) collective-permute-start(bf16[128,256]{1,0:T(8,128)(2,1)} %get-tuple-element.61), channel_id=1, source_target_pairs={{0,1},{1,2},{2,3},{3,4},{4,5},{5,6},{6,7},{7,8},{8,9},{9,10},{10,1... | collective-permute-start | bytes 196616 | tf_op jit(solution)/shard_map/ppermute | solution.py:14
  30.4 9.8 %collective-permute-start.1 = (bf16[128,256]{1,0:T(8,128)(2,1)}, bf16[128,256]{1,0:T(8,128)(2,1)}, u32[]{:S(2)}, u32[]{:S(2)}) collective-permute-start(bf16[128,256]{1,0:T(8,128)(2,1)} %get-tuple-element.62), channel_id=1, source_target_pairs={{1,0},{2,1},{3,2},{4,3},{5,4},{6,5},{7,6},{8,7},{9,8},{10,9},{11,1... | collective-permute-start | bytes 196616 | tf_op jit(solution)/shard_map/ppermute | solution.py:17
  34.5 4.1 copy-start.8
  55.3 6.6 %copy-start.10 = (bf16[1024,256]{1,0:T(8,128)(2,1)S(1)}, bf16[1024,256]{1,0:T(8,128)(2,1)}, u32[]{:S(2)}) copy-start(bf16[1024,256]{1,0:T(8,128)(2,1)} %param.21) | copy-start | bytes 1572868
  55.3 6.6 %copy-start.11 = (f32[256]{0:T(256)S(1)}, f32[256]{0:T(256)}, u32[]{:S(2)}) copy-start(f32[256]{0:T(256)} %param.20) | copy-start | bytes 3076
  62.0 2.9 copy-start.6
  64.9 0.8 copy-start.3
  92.5 1.1 copy-start.5
  94.5 492.1 %all-to-all-start.1 = ((bf16[12,128,256]{2,1,0:T(8,128)(2,1)}), bf16[12,128,256]{2,1,0:T(8,128)(2,1)}, u32[]{:S(2)}, u32[]{:S(2)}) async-start(bf16[12,128,256]{2,1,0:T(8,128)(2,1)} %slice.84), calls=%async_computation.1 | async-start | bytes 1572864 | tf_op jit(solution)/shard_map/all_to_all | solution.py:86
  102.1 481.7 %all-reduce.3.cloned.1.call-start = ((), (), s32[]{:S(2)}) async-start(), calls=%async_computation.2 | async-start | bytes 1048576 | tf_op jit(solution)/shard_map/psum | solution.py:93
  103.7 127.3 %collective-permute-start.2 = (bf16[128,256]{1,0:T(8,128)(2,1)}, bf16[128,256]{1,0:T(8,128)(2,1)}, u32[]{:S(2)}, u32[]{:S(2)}) collective-permute-start(bf16[128,256]{1,0:T(8,128)(2,1)} %get-tuple-element.58), channel_id=1, source_target_pairs={{0,1},{1,2},{2,3},{3,4},{4,5},{5,6},{6,7},{7,8},{8,9},{9,10},{10,1... | collective-permute-start | bytes 196616 | tf_op jit(solution)/shard_map/ppermute | solution.py:14
  107.8 123.2 %collective-permute-start.3 = (bf16[128,256]{1,0:T(8,128)(2,1)}, bf16[128,256]{1,0:T(8,128)(2,1)}, u32[]{:S(2)}, u32[]{:S(2)}) collective-permute-start(bf16[128,256]{1,0:T(8,128)(2,1)} %get-tuple-element.59), channel_id=1, source_target_pairs={{1,0},{2,1},{3,2},{4,3},{5,4},{6,5},{7,6},{8,7},{9,8},{10,9},{11,1... | collective-permute-start | bytes 196616 | tf_op jit(solution)/shard_map/ppermute | solution.py:17
  226.9 359.7 %copy-start.9 = (s32[1,12]{1,0:T(1,128)S(1)}, s32[1,12]{1,0:T(1,128)}, u32[]{:S(2)}) copy-start(s32[1,12]{1,0:T(1,128)} %param.17) | copy-start | bytes 148
  231.0 355.6 %copy-start.4 = (f32[8,128,256]{2,1,0:T(8,128)S(1)}, f32[8,128,256]{2,1,0:T(8,128)}, u32[]{:S(2)}) copy-start(f32[8,128,256]{2,1,0:T(8,128)} %slice.83) | copy-start | bytes 3145732
Sparse Core Ops, SparseCore 0:
  114.2 469.6 all-reduce.2
where the time goes:
time: 603 us; the launch traced here: 602 us
  waiting for transfers between devices  364 us (60%)
  blocking collectives  113 us (19%)
  starting transfers between devices  35.3 us (6%)
  local copies, waits for them, and re-layouts  31.5 us (5%)
  matrix products  26.5 us (4%)
  other arithmetic  17.7 us (3%)
  between operations  14.3 us (2%)
    psum x1, waiting for transfers between devices, per_device(): lax.psum((local_self, local_neigh, local_bias), ('dom', 'inner'))  352 us
    psum x1, blocking collectives, per_device(): lax.psum((local_self, local_neigh, local_bias), ('dom', 'inner'))  113 us
    all_to_all x1, starting transfers between devices, per_device(): lax.all_to_all(outgoing, 'dom', split_axis=0, concat_axis=0, tiled=True)  15.7 us
    scatter-add x1, other arithmetic, per_device(): jax.ops.segment_sum(pair_grads, flat_pairs, num_segments=entries)  12.5 us
  transfers between devices with their start and end apart: 7, of which 2 were waited for; matrix products, arithmetic and copies ran while one was open for 4% of the time, Pallas kernels for 0%

commit v1 on v0

--- a/solution.py
+++ b/solution.py
@@ -17,6 +17,31 @@
         high = lax.ppermute(lax.slice_in_dim(block, 0, width, axis=dim), axis, backward)
         block = jnp.concatenate([low, block, high], axis=dim)
     return block
+
+
+LANES = 128
+
+
+def reduce_grads(local_self, local_neigh, local_bias, scale):
+    dom_size = lax.axis_size("dom")
+    inner_size = lax.axis_size("inner")
+    width, hidden = local_self.shape
+    both = jnp.concatenate([local_self, local_neigh], axis=0).astype(jnp.bfloat16)
+    rows = both.size // (inner_size * LANES)
+    chunks = both.reshape(inner_size, rows, LANES)
+    pieces = lax.all_to_all(chunks, "inner", split_axis=0, concat_axis=0, tiled=True)
+    piece = jnp.sum(pieces.astype(jnp.float32), axis=0)
+    bias_rows = hidden // LANES
+    spare = jnp.zeros((8 - bias_rows, LANES), jnp.float32)
+    piece = jnp.concatenate([piece, local_bias.reshape(bias_rows, LANES), spare], axis=0)
+    spread = jnp.broadcast_to(piece[None], (dom_size,) + piece.shape)
+    spread = lax.all_to_all(spread, "dom", split_axis=0, concat_axis=0, tiled=True)
+    piece = (jnp.sum(spread, axis=0) * scale).astype(jnp.bfloat16)
+    spread = jnp.broadcast_to(piece[None], (inner_size,) + piece.shape)
+    spread = lax.all_to_all(spread, "inner", split_axis=0, concat_axis=0, tiled=True)
+    whole = spread[:, :rows].astype(jnp.float32).reshape(2, width, hidden)
+    sum_bias = jnp.sum(spread[:, rows : rows + bias_rows].astype(jnp.float32), axis=0)
+    return whole[0], whole[1], sum_bias.reshape(hidden)
 
 
 def per_device(
@@ -90,17 +115,15 @@
     total = self_part.reshape(nblocks, block_rows, width) + entry_grads[:nblocks] + returned_sum
     total = total.at[0].add(returned_rims[:block_rows])
     total = total.at[nblocks - 1].add(returned_rims[3 * block_rows :])
-    sum_self, sum_neigh, sum_bias = lax.psum(
-        (local_self, local_neigh, local_bias), ("dom", "inner")
-    )
     grad_scale = 1.0 / math.sqrt(rows_dev * dom_size * lax.axis_size("inner"))
+    sum_self, sum_neigh, sum_bias = reduce_grads(local_self, local_neigh, local_bias, grad_scale)
     grad_features = total.reshape(rows_dev, width).astype(jnp.bfloat16)
     return (
         layer_out,
         grad_features,
-        sum_self * grad_scale,
-        sum_neigh * grad_scale,
-        sum_bias * grad_scale,
+        sum_self,
+        sum_neigh,
+        sum_bias,
     )
 
 

time: 603 us -> 186 us (0.31)
  the two profiles are of different devices: /device:TPU:1 before, /device:TPU:6 now
where the time goes in v1:
time: 186 us; the launch traced here: 185 us
  starting transfers between devices  52.1 us (28%)
  waiting for transfers between devices  43.2 us (23%)
  local copies, waits for them, and re-layouts  31.7 us (17%)
  matrix products  22.3 us (12%)
  blocking collectives  17.4 us (9%)
  other arithmetic  17.2 us (9%)
    all_to_all x1, waiting for transfers between devices, per_device(): lax.all_to_all(slot_grads, 'dom', split_axis=0, concat_axis=0, tiled=True)  18.2 us
    all_to_all x1, blocking collectives, reduce_grads(): lax.all_to_all(spread, 'dom', split_axis=0, concat_axis=0, tiled=True)  17.4 us
    all_to_all x1, starting transfers between devices, per_device(): lax.all_to_all(outgoing, 'dom', split_axis=0, concat_axis=0, tiled=True)  15.2 us
    all_to_all x1, waiting for transfers between devices, per_device(): lax.all_to_all(outgoing, 'dom', split_axis=0, concat_axis=0, tiled=True)  13.5 us
    scatter-add x1, other arithmetic, per_device(): jax.ops.segment_sum(pair_grads, flat_pairs, num_segments=entries)  12.5 us
    all_to_all x1, waiting for transfers between devices, reduce_grads(): lax.all_to_all(chunks, 'inner', split_axis=0, concat_axis=0, tiled=True)  11.5 us
    ppermute x2, starting transfers between devices, with_halo(): lax.ppermute(lax.slice_in_dim(block, 0, width, axis=dim), axis, backward)  11.3 us
    all_to_all x1, starting transfers between devices, reduce_grads(): lax.all_to_all(chunks, 'inner', split_axis=0, concat_axis=0, tiled=True)  10.8 us
  transfers between devices with their start and end apart: 8, of which 3 were waited for; matrix products, arithmetic and copies ran while one was open for 25% of the time, Pallas kernels for 0%

profile of v1, /device:TPU:6, one launch (start us, length us, event | category | flops | bytes accessed | tf_op | source)
XLA Modules:
  0.0 184.9 jit_solution(6197337339160689700)
XLA Ops:
  0.6 0.0 copy-start
  0.7 1.6 convolution_convert_fusion
  2.3 0.0 copy-start.14
  2.3 0.0 copy-start.2
  2.3 1.1 copy.69
  3.5 15.2 %all-to-all-start = ((bf16[12,128,256]{2,1,0:T(8,128)(2,1)}), bf16[12,128,256]{2,1,0:T(8,128)(2,1)S(1)}, u32[]{:S(2)}, u32[]{:S(2)}) async-start(bf16[12,128,256]{2,1,0:T(8,128)(2,1)} %copy.69), calls=%async_computation | async-start | bytes 1572864 | tf_op jit(solution)/shard_map/all_to_all | solution.py:65
  18.6 0.7 fusion.40
  19.3 1.9 %collective-permute-start = (bf16[128,256]{1,0:T(8,128)(2,1)}, bf16[128,256]{1,0:T(8,128)(2,1)}, u32[]{:S(2)}, u32[]{:S(2)}) collective-permute-start(bf16[128,256]{1,0:T(8,128)(2,1)} %get-tuple-element.36), channel_id=1, source_target_pairs={{0,1},{1,2},{2,3},{3,4},{4,5},{5,6},{6,7},{7,8},{8,9},{9,10},{10,1... | collective-permute-start | bytes 196616 | tf_op jit(solution)/shard_map/ppermute | solution.py:14
  21.2 5.8 %collective-permute-start.1 = (bf16[128,256]{1,0:T(8,128)(2,1)}, bf16[128,256]{1,0:T(8,128)(2,1)}, u32[]{:S(2)}, u32[]{:S(2)}) collective-permute-start(bf16[128,256]{1,0:T(8,128)(2,1)} %get-tuple-element.37), channel_id=1, source_target_pairs={{1,0},{2,1},{3,2},{4,3},{5,4},{6,5},{7,6},{8,7},{9,8},{10,9},{11,1... | collective-permute-start | bytes 196616 | tf_op jit(solution)/shard_map/ppermute | solution.py:17
  27.0 2.2 %fusion.41 = f32[1024,256]{1,0:T(8,128)} fusion(bf16[1024,256]{1,0:T(8,128)(2,1)S(1)} %copy-done.1, bf16[256,256]{1,0:T(8,128)(2,1)} %param.18), kind=kOutput, calls=%fused_computation.55 | convolution fusion | flops 134217728 | bytes 1703936 | tf_op jit(solution)/shard_map/dot_general | solution.py:80
  29.1 1.1 copy.70
  30.2 0.1 eq.16
  30.3 2.9 %copy.74 = bf16[8,8,128,128]{2,1,0,3:T(8,128)(2,1)} copy(bf16[8,8,128,128]{3,2,1,0:T(8,128)(2,1)S(1)} %copy-done.2) | data formatting | bytes 4194304 | tf_op args[1]
  33.2 0.0 collective-permute-done
  33.2 1.6 copy.71
  34.8 0.0 collective-permute-done.1
  34.8 1.6 copy.72
  36.4 13.5 %all-to-all-done = bf16[12,128,256]{2,1,0:T(8,128)(2,1)S(1)} async-done(((bf16[12,128,256]{2,1,0:T(8,128)(2,1)}), bf16[12,128,256]{2,1,0:T(8,128)(2,1)S(1)}, u32[]{:S(2)}, u32[]{:S(2)}) %all-to-all-start) | async-done | bytes 786464 | tf_op jit(solution)/shard_map/all_to_all | solution.py:65
  50.0 1.4 copy.73
  51.4 5.1 %fusion = f32[8,256,128,1]{1,2,0,3:T(8,128)} fusion(bf16[8,8,128,128]{2,1,0,3:T(8,128)(2,1)} %copy.74, bf16[12,128,256]{2,0,1:T(8,128)(2,1)} %copy.73, bf16[1,128,256]{2,0,1:T(2,128)(2,1)} %copy.72, bf16[1,128,256]{2,0,1:T(2,128)(2,1)} %copy.71, bf16[8,128,256]{2,0,1:T(8,128)(2,1)} %copy.70, s32[64]{0:T(128)S(1)} %eq.16), kind=kOutput, calls=%fused_computation.1 | convolution fusion | flops 637011328 | bytes 4587776 | tf_op jit(solution)/shard_map/bpij,bpjf->bif/dot_general | solution.py:76
  56.5 1.4 fusion.22
  58.0 2.9 %convert_reduce_fusion = (f32[256]{0:T(256)S(1)}, bf16[1024,256]{1,0:T(8,128)(2,1)S(1)}, bf16[1024,256]{1,0:T(8,128)(2,1)}) fusion(bf16[1024,256]{1,0:T(8,128)(2,1)} %param.21, f32[256]{0:T(256)S(1)} %copy-done.17, f32[1024,256]{1,0:T(8,128)} %fusion.41, bf16[1024,256]{1,0:T(8,128)(2,1)S(1)} %fusion.22, bf16[256,256]{1,0:T(8,128)(2,1)S(1)} %copy-done), kind=kOutput, calls=%fused_computation.25 | convolution fusion | flops 138411776 | bytes 3278848 | tf_op jit(solution)/shard_map/dot_general | solution.py:81
  60.9 0.3 convolution_convert_fusion.1
  61.2 0.3 fusion.21
  61.6 0.8 convert_element_type.73
  62.4 10.8 %all-to-all-start.2 = ((bf16[64,16,128]{2,1,0:T(8,128)(2,1)}), bf16[64,16,128]{2,1,0:T(8,128)(2,1)S(1)}, u32[]{:S(2)}, u32[]{:S(2)}) async-start(bf16[64,16,128]{2,1,0:T(8,128)(2,1)} %convert_element_type.73), calls=%async_computation.2 | async-start | bytes 524288 | tf_op jit(solution)/shard_map/all_to_all | solution.py:32
  73.2 0.1 pad.6.clone
  73.3 11.5 %all-to-all-done.2 = bf16[64,16,128]{2,1,0:T(8,128)(2,1)S(1)} async-done(((bf16[64,16,128]{2,1,0:T(8,128)(2,1)}), bf16[64,16,128]{2,1,0:T(8,128)(2,1)S(1)}, u32[]{:S(2)}, u32[]{:S(2)}) %all-to-all-start.2) | async-done | bytes 262176 | tf_op jit(solution)/shard_map/all_to_all | solution.py:32
  84.8 0.1 convert_reduce_fusion.1
  84.9 0.1 maximum_maximum_fusion
  84.9 17.4 %all_to_all.25 = f32[12,24,128]{2,1,0:T(8,128)S(1)} all-to-all(f32[12,24,128]{2,1,0:T(8,128)S(1)} %broadcast_in_dim.16), channel_id=1, replica_groups=mesh['dom'=12,'inner'=64] {'dom'}, dimensions={0} | all-to-all | bytes 294912 | tf_op jit(solution)/shard_map/all_to_all | solution.py:38
  102.4 0.8 broadcast_in_dim.34
  103.2 6.5 %all-to-all-start.4 = ((bf16[64,24,128]{2,1,0:T(8,128)(2,1)}), bf16[64,24,128]{2,1,0:T(8,128)(2,1)}, u32[]{:S(2)}, u32[]{:S(2)}) async-start(bf16[64,24,128]{2,1,0:T(8,128)(2,1)} %broadcast_in_dim.34), calls=%async_computation.4 | async-start | bytes 786432 | tf_op jit(solution)/shard_map/all_to_all | solution.py:41
  109.6 0.3 fusion.20
  110.0 4.5 %fusion.43 = f32[8,256,8,128]{3,1,2,0:T(8,128)} fusion(bf16[8,128,256,1]{2,1,3,0:T(8,128)(2,1)S(1)} %bitcast.65, bf16[8,8,128,128]{3,2,1,0:T(8,128)(2,1)S(1)} %copy-done.2), kind=kOutput, calls=%fused_computation.57 | convolution fusion | flops 536870912 | bytes 11010048 | tf_op jit(solution)/shard_map/bpij,bif->bpjf/dot_general | solution.py:103
  114.5 9.0 %copy.76 = f32[64,128,256]{2,1,0:T(8,128)} copy(f32[64,128,256]{1,2,0:T(8,128)} %bitcast.60) | data formatting | bytes 16777216 | tf_op jit(solution)/shard_map/reshape | solution.py:104
  123.5 0.3 broadcast_in_dim.14
  123.8 12.5 %scatter_fusion = f32[22,128,256]{2,1,0:T(8,128)S(1)} fusion(f32[22,128,256]{2,1,0:T(8,128)S(1)} %broadcast_in_dim.14, s32[64]{0:T(128)S(1)} %eq.16, f32[64,128,256]{2,1,0:T(8,128)} %copy.76), kind=kCustom, calls=%fused_computation | custom fusion | flops 2097152 | bytes 25166080 | tf_op jit(solution)/shard_map/scatter-add | solution.py:105
  136.3 0.2 convert.16
  136.5 1.1 copy-done.5
  137.6 0.9 slice.102
  138.5 0.0 all-to-all-done.4
  138.5 4.3 %all-to-all-start.1 = ((bf16[12,128,256]{2,1,0:T(8,128)(2,1)}), bf16[12,128,256]{2,1,0:T(8,128)(2,1)}, u32[]{:S(2)}, u32[]{:S(2)}) async-start(bf16[12,128,256]{2,1,0:T(8,128)(2,1)} %slice.102), calls=%async_computation.1 | async-start | bytes 1572864 | tf_op jit(solution)/shard_map/all_to_all | solution.py:111
  142.8 0.9 slice_bitcast_fusion.1
  143.7 2.1 %collective-permute-start.2 = (bf16[128,256]{1,0:T(8,128)(2,1)S(1)}, bf16[128,256]{1,0:T(8,128)(2,1)S(1)}, u32[]{:S(2)}, u32[]{:S(2)}) collective-permute-start(bf16[128,256]{1,0:T(8,128)(2,1)S(1)} %get-tuple-element.31), channel_id=1, source_target_pairs={{0,1},{1,2},{2,3},{3,4},{4,5},{5,6},{6,7},{7,8},{8,9},{9,10},{10,1... | collective-permute-start | bytes 196616 | tf_op jit(solution)/shard_map/ppermute | solution.py:14
  145.8 5.6 %collective-permute-start.3 = (bf16[128,256]{1,0:T(8,128)(2,1)S(1)}, bf16[128,256]{1,0:T(8,128)(2,1)S(1)}, u32[]{:S(2)}, u32[]{:S(2)}) collective-permute-start(bf16[128,256]{1,0:T(8,128)(2,1)S(1)} %get-tuple-element.32), channel_id=1, source_target_pairs={{1,0},{2,1},{3,2},{4,3},{5,4},{6,5},{7,6},{8,7},{9,8},{10,9},{11,1... | collective-permute-start | bytes 196616 | tf_op jit(solution)/shard_map/ppermute | solution.py:17
  151.4 2.2 %fusion.42 = f32[1024,256]{1,0:T(8,128)} fusion(bf16[1024,256]{1,0:T(8,128)(2,1)S(1)} %get-tuple-element.30, bf16[256,256]{1,0:T(8,128)(2,1)} %param.18), kind=kOutput, calls=%fused_computation.56 | convolution fusion | flops 134217728 | bytes 1703936 | tf_op jit(solution)/shard_map/dot_general | solution.py:114
  153.6 1.1 slice.101
  154.7 0.0 collective-permute-done.2
  154.7 0.0 collective-permute-done.3
  154.8 0.0 copy-start.12
  154.8 1.1 slice_convert_fusion
  156.0 0.8 squeeze.16
  156.8 0.8 squeeze.17
  157.6 1.5 convert_reduce_fusion.2
  159.1 18.2 %all-to-all-done.1 = bf16[12,128,256]{2,1,0:T(8,128)(2,1)} async-done(((bf16[12,128,256]{2,1,0:T(8,128)(2,1)}), bf16[12,128,256]{2,1,0:T(8,128)(2,1)}, u32[]{:S(2)}, u32[]{:S(2)}) %all-to-all-start.1) | async-done | bytes 786464 | tf_op jit(solution)/shard_map/all_to_all | solution.py:111
  177.3 2.7 %convolution_add_fusion.1 = f32[8,128,256]{2,0,1:T(8,128)S(1)} fusion(f32[8,128,256]{2,1,0:T(8,128)S(1)} %copy-done.3, bf16[12,128,256]{2,1,0:T(8,128)(2,1)} %all-to-all-done.1, f32[8,128,256]{2,1,0:T(8,128)S(1)} %bitcast.63, s32[12]{0:T(128)S(1)} %bitcast.67), kind=kOutput, calls=%fused_computation.16 | convolution fusion | flops 6815840 | bytes 3932208 | tf_op jit(solution)/shard_map/jb,jrf->brf/dot_general | solution.py:113
  180.1 0.1 slice.103
  180.2 0.1 copy.81
  180.3 1.7 scatter-add.18
  182.1 0.2 slice_add_fusion
  182.3 1.7 scatter-add.19
  184.0 0.1 convert_element_type.71
  184.1 0.9 copy.82
  (40 shorter events, 0.2 us)
Async XLA Ops:
  0.6 57.4 %copy-start = (bf16[256,256]{1,0:T(8,128)(2,1)S(1)}, bf16[256,256]{1,0:T(8,128)(2,1)}, u32[]{:S(2)}) copy-start(bf16[256,256]{1,0:T(8,128)(2,1)} %param.19) | copy-start | bytes 393220
  0.6 18.0 %copy-start.1 = (bf16[1024,256]{1,0:T(8,128)(2,1)S(1)}, bf16[1024,256]{1,0:T(8,128)(2,1)}, u32[]{:S(2)}) copy-start(bf16[1024,256]{1,0:T(8,128)(2,1)} %param.13) | copy-start | bytes 1572868
  2.3 27.9 %copy-start.14 = (s32[8,8]{1,0:T(8,128)S(1)}, s32[8,8]{1,0:T(8,128)}, u32[]{:S(2)}) copy-start(s32[8,8]{1,0:T(8,128)} %param.15) | copy-start | bytes 772
  2.3 28.0 %copy-start.2 = (bf16[8,8,128,128]{3,2,1,0:T(8,128)(2,1)S(1)}, bf16[8,8,128,128]{3,2,1,0:T(8,128)(2,1)}, u32[]{:S(2)}) copy-start(bf16[8,8,128,128]{3,2,1,0:T(8,128)(2,1)} %param.14) | copy-start | bytes 6291460
  3.5 46.5 %all-to-all-start = ((bf16[12,128,256]{2,1,0:T(8,128)(2,1)}), bf16[12,128,256]{2,1,0:T(8,128)(2,1)S(1)}, u32[]{:S(2)}, u32[]{:S(2)}) async-start(bf16[12,128,256]{2,1,0:T(8,128)(2,1)} %copy.69), calls=%async_computation | async-start | bytes 1572864 | tf_op jit(solution)/shard_map/all_to_all | solution.py:65
  19.3 13.9 %collective-permute-start = (bf16[128,256]{1,0:T(8,128)(2,1)}, bf16[128,256]{1,0:T(8,128)(2,1)}, u32[]{:S(2)}, u32[]{:S(2)}) collective-permute-start(bf16[128,256]{1,0:T(8,128)(2,1)} %get-tuple-element.36), channel_id=1, source_target_pairs={{0,1},{1,2},{2,3},{3,4},{4,5},{5,6},{6,7},{7,8},{8,9},{9,10},{10,1... | collective-permute-start | bytes 196616 | tf_op jit(solution)/shard_map/ppermute | solution.py:14
  21.2 13.6 %collective-permute-start.1 = (bf16[128,256]{1,0:T(8,128)(2,1)}, bf16[128,256]{1,0:T(8,128)(2,1)}, u32[]{:S(2)}, u32[]{:S(2)}) collective-permute-start(bf16[128,256]{1,0:T(8,128)(2,1)} %get-tuple-element.37), channel_id=1, source_target_pairs={{1,0},{2,1},{3,2},{4,3},{5,4},{6,5},{7,6},{8,7},{9,8},{10,9},{11,1... | collective-permute-start | bytes 196616 | tf_op jit(solution)/shard_map/ppermute | solution.py:17
  29.1 4.1 %copy-start.15 = (s32[1024]{0:T(1024)S(1)}, s32[1024]{0:T(1024)}, u32[]{:S(2)}) copy-start(s32[1024]{0:T(1024)} %param.16) | copy-start | bytes 12292
  51.4 6.6 %copy-start.17 = (f32[256]{0:T(256)S(1)}, f32[256]{0:T(256)}, u32[]{:S(2)}) copy-start(f32[256]{0:T(256)} %param.20) | copy-start | bytes 3076
  62.4 22.4 %all-to-all-start.2 = ((bf16[64,16,128]{2,1,0:T(8,128)(2,1)}), bf16[64,16,128]{2,1,0:T(8,128)(2,1)S(1)}, u32[]{:S(2)}, u32[]{:S(2)}) async-start(bf16[64,16,128]{2,1,0:T(8,128)(2,1)} %convert_element_type.73), calls=%async_computation.2 | async-start | bytes 524288 | tf_op jit(solution)/shard_map/all_to_all | solution.py:32
  103.2 35.3 %all-to-all-start.4 = ((bf16[64,24,128]{2,1,0:T(8,128)(2,1)}), bf16[64,24,128]{2,1,0:T(8,128)(2,1)}, u32[]{:S(2)}, u32[]{:S(2)}) async-start(bf16[64,24,128]{2,1,0:T(8,128)(2,1)} %broadcast_in_dim.34), calls=%async_computation.4 | async-start | bytes 786432 | tf_op jit(solution)/shard_map/all_to_all | solution.py:41
  136.4 1.1 copy-start.5
  138.5 38.8 %all-to-all-start.1 = ((bf16[12,128,256]{2,1,0:T(8,128)(2,1)}), bf16[12,128,256]{2,1,0:T(8,128)(2,1)}, u32[]{:S(2)}, u32[]{:S(2)}) async-start(bf16[12,128,256]{2,1,0:T(8,128)(2,1)} %slice.102), calls=%async_computation.1 | async-start | bytes 1572864 | tf_op jit(solution)/shard_map/all_to_all | solution.py:111
  143.7 12.3 %copy-start.6 = (bf16[128,256]{1,0:T(8,128)(2,1)}, bf16[128,256]{1,0:T(8,128)(2,1)S(1)}, u32[]{:S(2)}) copy-start(bf16[128,256]{1,0:T(8,128)(2,1)S(1)} %get-tuple-element.31) | copy-start | bytes 196612
  143.7 12.3 %copy-start.8 = (bf16[128,256]{1,0:T(8,128)(2,1)}, bf16[128,256]{1,0:T(8,128)(2,1)S(1)}, u32[]{:S(2)}) copy-start(bf16[128,256]{1,0:T(8,128)(2,1)S(1)} %get-tuple-element.32) | copy-start | bytes 196612
  143.7 11.0 %collective-permute-start.2 = (bf16[128,256]{1,0:T(8,128)(2,1)S(1)}, bf16[128,256]{1,0:T(8,128)(2,1)S(1)}, u32[]{:S(2)}, u32[]{:S(2)}) collective-permute-start(bf16[128,256]{1,0:T(8,128)(2,1)S(1)} %get-tuple-element.31), channel_id=1, source_target_pairs={{0,1},{1,2},{2,3},{3,4},{4,5},{5,6},{6,7},{7,8},{8,9},{9,10},{10,1... | collective-permute-start | bytes 196616 | tf_op jit(solution)/shard_map/ppermute | solution.py:14
  145.8 8.9 %collective-permute-start.3 = (bf16[128,256]{1,0:T(8,128)(2,1)S(1)}, bf16[128,256]{1,0:T(8,128)(2,1)S(1)}, u32[]{:S(2)}, u32[]{:S(2)}) collective-permute-start(bf16[128,256]{1,0:T(8,128)(2,1)S(1)} %get-tuple-element.32), channel_id=1, source_target_pairs={{1,0},{2,1},{3,2},{4,3},{5,4},{6,5},{7,6},{8,7},{9,8},{10,9},{11,1... | collective-permute-start | bytes 196616 | tf_op jit(solution)/shard_map/ppermute | solution.py:17
  153.6 23.7 %copy-start.16 = (s32[1,12]{1,0:T(1,128)S(1)}, s32[1,12]{1,0:T(1,128)}, u32[]{:S(2)}) copy-start(s32[1,12]{1,0:T(1,128)} %param.17) | copy-start | bytes 148
  154.7 22.6 %copy-start.3 = (f32[8,128,256]{2,1,0:T(8,128)S(1)}, f32[8,128,256]{2,1,0:T(8,128)}, u32[]{:S(2)}) copy-start(f32[8,128,256]{2,1,0:T(8,128)} %slice.101) | copy-start | bytes 3145732
  154.7 22.6 %copy-start.4 = (f32[1024,256]{1,0:T(8,128)S(1)}, f32[1024,256]{1,0:T(8,128)}, u32[]{:S(2)}) copy-start(f32[1024,256]{1,0:T(8,128)} %fusion.42) | copy-start | bytes 3145732
  154.7 1.3 copy-start.10
  154.8 1.2 copy-start.12
  156.0 24.1 %copy-start.7 = (bf16[128,256]{1,0:T(8,128)(2,1)S(1)}, bf16[128,256]{1,0:T(8,128)(2,1)}, u32[]{:S(2)}) copy-start(bf16[128,256]{1,0:T(8,128)(2,1)} %copy-done.6) | copy-start | bytes 196612
  156.0 24.1 %copy-start.9 = (bf16[128,256]{1,0:T(8,128)(2,1)S(1)}, bf16[128,256]{1,0:T(8,128)(2,1)}, u32[]{:S(2)}) copy-start(bf16[128,256]{1,0:T(8,128)(2,1)} %copy-done.8) | copy-start | bytes 196612
  177.3 2.9 %copy-start.11 = (bf16[128,256]{1,0:T(8,128)(2,1)S(1)}, bf16[128,256]{1,0:T(8,128)(2,1)}, u32[]{:S(2)}) copy-start(bf16[128,256]{1,0:T(8,128)(2,1)} %copy-done.10) | copy-start | bytes 196612
  177.3 2.9 %copy-start.13 = (bf16[128,256]{1,0:T(8,128)(2,1)S(1)}, bf16[128,256]{1,0:T(8,128)(2,1)}, u32[]{:S(2)}) copy-start(bf16[128,256]{1,0:T(8,128)(2,1)} %copy-done.12) | copy-start | bytes 196612

commit v2 on v0

v2 whole, which is shorter than its diff:
```python
import functools
import math

import jax
import jax.numpy as jnp
from jax import lax
from jax.experimental import pallas as pl
from jax.experimental.pallas import tpu as pltpu
from jax.sharding import PartitionSpec as P

LANES = 128
VMEM = pl.BlockSpec(memory_space=pltpu.VMEM)
SMEM = pl.BlockSpec(memory_space=pltpu.SMEM)
ANY = pl.BlockSpec(memory_space=pl.ANY)
F32 = jnp.float32
BF16 = jnp.bfloat16
CONTRACT_ROWS = (((0,), (0,)), ((), ()))
CONTRACT_COLS = (((1,), (1,)), ((), ()))


def params():
    return pltpu.CompilerParams(vmem_limit_bytes=32 * 1024 * 1024)


def pick_kernel(send_ref, blocks_ref, out_ref, sems):
    copies = []
    for j in range(out_ref.shape[0]):
        copies.append(
            pltpu.make_async_copy(blocks_ref.at[send_ref[0, j]], out_ref.at[j], sems.at[j])
        )
    for copy in copies:
        copy.start()
    for copy in copies:
        copy.wait()


def layer_kernel(
    pairs_ref,
    degree_ref,
    w_self_ref,
    w_neigh_ref,
    bias_ref,
    blocks_hbm,
    left_hbm,
    right_hbm,
    received_hbm,
    tiles_hbm,
    cot_hbm,
    out_hbm,
    own_ref,
    rims_ref,
    slots_ref,
    grads_ref,
    gbias_ref,
    table,
    tiles,
    cot,
    out,
    sources,
    mean,
    grad_pre,
    inverse,
    entries,
    sems,
    tile_sems,
):
    nblocks, npairs, rows, _ = tiles.shape
    width = table.shape[2]
    copies = [
        pltpu.make_async_copy(blocks_hbm, table.at[pl.ds(0, nblocks)], sems.at[0]),
        pltpu.make_async_copy(left_hbm, table.at[nblocks], sems.at[1]),
        pltpu.make_async_copy(right_hbm, table.at[nblocks + 1], sems.at[2]),
        pltpu.make_async_copy(
            received_hbm, table.at[pl.ds(nblocks + 2, received_hbm.shape[0])], sems.at[3]
        ),
    ]
    tile_copies = [
        pltpu.make_async_copy(tiles_hbm.at[b], tiles.at[b], tile_sems.at[b])
        for b in range(nblocks)
    ]
    cot_copy = pltpu.make_async_copy(cot_hbm, cot, sems.at[4])
    out_copy = pltpu.make_async_copy(out, out_hbm, sems.at[5])
    for copy in copies:
        copy.start()
    for copy in tile_copies:
        copy.start()
    cot_copy.start()

    for b in range(nblocks):
        row = 1.0 / degree_ref[b : b + 1, :].astype(F32)
        inverse[b] = jnp.broadcast_to(row, (rows, rows)).T
    entries[nblocks:] = jnp.zeros((entries.shape[0] - nblocks, rows, width), F32)

    for copy in copies:
        copy.wait()

    def tile_row(b):
        return jnp.concatenate([tiles[b, p] for p in range(npairs)], axis=1)

    def by_degree(values, b):
        return jnp.concatenate(
            [values[:, k : k + rows] * inverse[b] for k in range(0, width, rows)], axis=1
        )

    for b in range(nblocks):
        for p in range(npairs):
            sources[b % 2, pl.ds(p * rows, rows), :] = table[pairs_ref[b, p]]
        tile_copies[b].wait()
        summed = jnp.dot(tile_row(b), sources[b % 2], preferred_element_type=F32)
        mean[b] = by_degree(summed, b).astype(BF16)

    cot_copy.wait()
    w_self = w_self_ref[...]
    w_neigh = w_neigh_ref[...]
    gbias = jnp.zeros((1, width), F32)
    step = 2
    for b in range(0, nblocks, step):
        features = table[b : b + step].reshape(step * rows, width)
        means = mean[b : b + step].reshape(step * rows, width)
        preact = (
            jnp.dot(features, w_self, preferred_element_type=F32)
            + jnp.dot(means, w_neigh, preferred_element_type=F32)
            + bias_ref[...]
        )
        sigma = jax.nn.sigmoid(preact)
        out[b : b + step] = (preact * sigma).astype(BF16).reshape(step, rows, width)
        cots = cot[b : b + step].reshape(step * rows, width).astype(F32)
        grad = (cots * sigma * (1.0 + preact * (1.0 - sigma))).astype(BF16)
        grad_pre[pl.ds(b * rows, step * rows), :] = grad
        gbias = gbias + jnp.sum(grad.astype(F32), axis=0, keepdims=True)
        own = lax.dot_general(grad, w_self, CONTRACT_COLS, preferred_element_type=F32)
        entries[b : b + step] = own.reshape(step, rows, width)
    out_copy.start()
    gbias_ref[...] = gbias

    for b in range(nblocks):
        grad = grad_pre[pl.ds(b * rows, rows), :]
        grad_mean = lax.dot_general(grad, w_neigh, CONTRACT_COLS, preferred_element_type=F32)
        grad_mean = by_degree(grad_mean, b).astype(BF16)
        parts = lax.dot_general(
            tile_row(b), grad_mean, CONTRACT_ROWS, preferred_element_type=F32
        )
        for p in range(npairs):
            entry = pairs_ref[b, p]
            entries[entry] = entries[entry] + parts[p * rows : (p + 1) * rows]

    own_ref[...] = entries[:nblocks]
    rims_ref[...] = entries[nblocks : nblocks + 2].astype(BF16)
    slots_ref[...] = entries[nblocks + 2 :].astype(BF16)

    grads = grad_pre[...]
    features = table[:nblocks].reshape(nblocks * rows, width)
    means = mean[...].reshape(nblocks * rows, width)
    grads_ref[:width, :] = lax.dot_general(
        features, grads, CONTRACT_ROWS, preferred_element_type=F32
    ).astype(BF16)
    grads_ref[width:, :] = lax.dot_general(
        means, grads, CONTRACT_ROWS, preferred_element_type=F32
    ).astype(BF16)
    out_copy.wait()


def combine_kernel(send_ref, own_ref, returned_ref, low_ref, high_ref, out_ref, total):
    total[...] = own_ref[...]
    last = total.shape[0] - 1
    total[0] = total[0] + low_ref[...].astype(F32)
    total[last] = total[last] + high_ref[...].astype(F32)
    for j in range(returned_ref.shape[0]):
        block = send_ref[0, j]
        total[block] = total[block] + returned_ref[j].astype(F32)
    out_ref[...] = total[...].astype(BF16)


def call_layer(
    blocks, left, right, received, tiles, cot, pairs, degree, w_self, w_neigh, bias
):
    nblocks, npairs, rows, _ = tiles.shape
    width = blocks.shape[2]
    dom = received.shape[0]
    entries = nblocks + 2 + dom
    shape = jax.ShapeDtypeStruct
    return pl.pallas_call(
        layer_kernel,
        out_shape=(
            shape(blocks.shape, BF16),
            shape(blocks.shape, F32),
            shape((2, rows, width), BF16),
            shape((dom, rows, width), BF16),
            shape((2 * width, width), BF16),
            shape((1, width), F32),
        ),
        in_specs=[SMEM] + [VMEM] * 4 + [ANY] * 6,
        out_specs=(ANY,) + (VMEM,) * 5,
        scratch_shapes=[
            pltpu.VMEM((entries, rows, width), BF16),
            pltpu.VMEM(tiles.shape, BF16),
            pltpu.VMEM(blocks.shape, BF16),
            pltpu.VMEM(blocks.shape, BF16),
            pltpu.VMEM((2, npairs * rows, width), BF16),
            pltpu.VMEM(blocks.shape, BF16),
            pltpu.VMEM((nblocks * rows, width), BF16),
            pltpu.VMEM((nblocks, rows, rows), F32),
            pltpu.VMEM((entries, rows, width), F32),
            pltpu.SemaphoreType.DMA((6,)),
            pltpu.SemaphoreType.DMA((nblocks,)),
        ],
        compiler_params=params(),
        cost_estimate=pl.CostEstimate(
            flops=4 * 10**9, bytes_accessed=8 * 10**6, transcendentals=nblocks * rows * width
        ),
    )(pairs, degree, w_self, w_neigh, bias, blocks, left, right, received, tiles, cot)


def neighbours(low_source, high_source, axis):
    count = lax.axis_size(axis)
    forward = [(i, i + 1) for i in range(count - 1)]
    backward = [(target, source) for source, target in forward]
    return lax.ppermute(low_source, axis, forward), lax.ppermute(high_source, axis, backward)


def reduce_grads(grads, gbias, scale):
    dom_size = lax.axis_size("dom")
    inner_size = lax.axis_size("inner")
    hidden = grads.shape[1]
    rows = grads.shape[0] // inner_size
    chunks = grads.reshape(inner_size, rows, hidden)
    pieces = lax.all_to_all(chunks, "inner", split_axis=0, concat_axis=0, tiled=True)
    piece = jnp.sum(pieces.astype(F32), axis=0)
    piece = [piece[:, k : k + LANES] for k in range(0, hidden, LANES)]
    bias_rows = hidden // LANES
    spare = jnp.zeros((8 - bias_rows, LANES), F32)
    piece = jnp.concatenate(piece + [gbias.reshape(bias_rows, LANES), spare], axis=0)
    spread = jnp.broadcast_to(piece[None], (dom_size,) + piece.shape)
    spread = lax.all_to_all(spread, "dom", split_axis=0, concat_axis=0, tiled=True)
    piece = (jnp.sum(spread, axis=0) * scale).astype(BF16)
    spread = jnp.broadcast_to(piece[None], (inner_size,) + piece.shape)
    spread = lax.all_to_all(spread, "inner", split_axis=0, concat_axis=0, tiled=True)
    return pl.pallas_call(
        functools.partial(unpack_kernel, rows, bias_rows),
        out_shape=(
            jax.ShapeDtypeStruct((hidden, hidden), F32),
            jax.ShapeDtypeStruct((hidden, hidden), F32),
            jax.ShapeDtypeStruct((bias_rows, LANES), F32),
        ),
        in_specs=[VMEM],
        out_specs=(VMEM,) * 3,
        compiler_params=params(),
    )(spread)


def unpack_kernel(rows, bias_rows, spread_ref, self_ref, neigh_ref, bias_ref):
    spread = spread_ref[...].astype(F32)
    half = spread.shape[0] // 2
    for k in range(bias_rows):
        part = spread[:, k * rows : (k + 1) * rows]
        for ref, first in ((self_ref, 0), (neigh_ref, half)):
            ref[:, k * LANES : (k + 1) * LANES] = part[first : first + half].reshape(-1, LANES)
    tail = jnp.sum(spread[:, bias_rows * rows :], axis=0)
    bias_ref[...] = tail[:bias_rows]


def per_device(
    features, tiles, pair_source, in_degree, send_blocks, w_self, w_neigh, bias, cotangent
):
    rows_dev, width = features.shape
    nblocks, _, rows, _ = tiles.shape
    dom_size = lax.axis_size("dom")
    blocks = features.reshape(nblocks, rows, width)
    outgoing = pl.pallas_call(
        pick_kernel,
        out_shape=jax.ShapeDtypeStruct((dom_size, rows, width), BF16),
        in_specs=[SMEM, ANY],
        out_specs=ANY,
        scratch_shapes=[pltpu.SemaphoreType.DMA((dom_size,))],
    )(send_blocks, blocks)
    received = lax.all_to_all(outgoing, "dom", split_axis=0, concat_axis=0, tiled=True)
    left, right = neighbours(blocks[nblocks - 1], blocks[0], "inner")
    layer_out, own, rims, slots, grads, gbias = call_layer(
        blocks,
        left,
        right,
        received,
        tiles,
        cotangent.reshape(nblocks, rows, width),
        pair_source,
        in_degree.reshape(nblocks, rows),
        w_self,
        w_neigh,
        bias[None, :],
    )
    returned = lax.all_to_all(slots, "dom", split_axis=0, concat_axis=0, tiled=True)
    low, high = neighbours(rims[1], rims[0], "inner")
    grad_features = pl.pallas_call(
        combine_kernel,
        out_shape=jax.ShapeDtypeStruct(blocks.shape, BF16),
        in_specs=[SMEM] + [VMEM] * 4,
        out_specs=VMEM,
        scratch_shapes=[pltpu.VMEM(blocks.shape, F32)],
        compiler_params=params(),
        cost_estimate=pl.CostEstimate(
            flops=10**6, bytes_accessed=3 * 10**6, transcendentals=0
        ),
    )(send_blocks, own, returned, low, high)
    scale = 1.0 / math.sqrt(rows_dev * dom_size * lax.axis_size("inner"))
    sum_self, sum_neigh, sum_bias = reduce_grads(grads, gbias, scale)
    return (
        layer_out.reshape(rows_dev, width),
        grad_features.reshape(rows_dev, width),
        sum_self,
        sum_neigh,
        sum_bias.reshape(-1),
    )


def solution(mesh):
    return jax.shard_map(
        per_device,
        mesh=mesh,
        in_specs=(
            P(("dom", "inner"), None),
            P(("dom", "inner"), None, None, None),
            P(("dom", "inner"), None),
            P(("dom", "inner")),
            P(("dom", "inner"), None),
            P(),
            P(),
            P(),
            P(("dom", "inner"), None),
        ),
        out_specs=(P(("dom", "inner"), None), P(("dom", "inner"), None), P(), P(), P()),
        check_vma=False,
    )
```

time: 603 us -> 184 us (0.31)
  the two profiles are of different devices: /device:TPU:1 before, /device:TPU:6 now
where the time goes in v2:
time: 184 us
  waiting for transfers between devices  61.2 us (33%)
  starting transfers between devices  45 us (24%)
  blocking collectives  37.6 us (20%)
  Pallas kernels  37.3 us (20%)
    pallas_call x1, Pallas kernels, per_device(): pl.pallas_call(pick_kernel, out_shape=jax.ShapeDtypeStruct((dom_size, row...  25.8 us
    all_to_all x1, waiting for transfers between devices, per_device(): lax.all_to_all(slots, 'dom', split_axis=0, concat_axis=0, tiled=True)  25 us
    all_to_all x1, waiting for transfers between devices, per_device(): lax.all_to_all(outgoing, 'dom', split_axis=0, concat_axis=0, tiled=True)  21.7 us
    all_to_all x1, blocking collectives, reduce_grads(): lax.all_to_all(spread, 'inner', split_axis=0, concat_axis=0, tiled=True)  20.2 us
    all_to_all x1, blocking collectives, reduce_grads(): lax.all_to_all(spread, 'dom', split_axis=0, concat_axis=0, tiled=True)  17.4 us
    all_to_all x1, starting transfers between devices, per_device(): lax.all_to_all(outgoing, 'dom', split_axis=0, concat_axis=0, tiled=True)  15.2 us
    all_to_all x1, waiting for transfers between devices, reduce_grads(): lax.all_to_all(chunks, 'inner', split_axis=0, concat_axis=0, tiled=True)  11.5 us
    ppermute x2, starting transfers between devices, neighbours(): lax.ppermute(high_source, axis, backward)  11.1 us
  transfers between devices with their start and end apart: 7, of which 5 were waited for; matrix products, arithmetic and copies ran while one was open for 0% of the time, Pallas kernels for 0%

profile of v2, /device:TPU:6, one launch (start us, length us, event | category | flops | bytes accessed | tf_op | source)
XLA Modules:
  0.0 183.9 jit_solution(97520776811926886)
XLA Ops:
  0.6 0.0 copy-start
  0.6 0.0 copy-start.7
  0.7 0.0 copy-start.8
  0.7 0.0 copy-start.3
  0.7 0.0 copy-start.6
  0.7 0.0 copy-start.4
  0.7 0.0 copy-start.5
  0.7 25.8 %shard_map.128 = bf16[12,128,256]{2,1,0:T(8,128)(2,1)} custom-call(s32[1,12]{1,0:T(1,128)} %send_ref.3, bf16[8,128,256]{2,1,0:T(8,128)(2,1)} %bitcast.13), custom_call_target="tpu_custom_call" | custom-call | tf_op jit(solution)/shard_map/pallas_call | solution.py:269
  26.5 15.2 %all-to-all-start = ((bf16[12,128,256]{2,1,0:T(8,128)(2,1)}), bf16[12,128,256]{2,1,0:T(8,128)(2,1)S(1)}, u32[]{:S(2)}, u32[]{:S(2)}) async-start(bf16[12,128,256]{2,1,0:T(8,128)(2,1)} %shard_map.128), calls=%async_computation | async-start | bytes 1572864 | tf_op jit(solution)/shard_map/all_to_all | solution.py:276
  41.7 0.0 copy-done
  41.7 1.9 %collective-permute-start = (bf16[128,256]{1,0:T(8,128)(2,1)S(1)}, bf16[128,256]{1,0:T(8,128)(2,1)S(1)}, u32[]{:S(2)}, u32[]{:S(2)}) collective-permute-start(bf16[128,256]{1,0:T(8,128)(2,1)S(1)} %get-tuple-element.24), channel_id=1, source_target_pairs={{0,1},{1,2},{2,3},{3,4},{4,5},{5,6},{6,7},{7,8},{8,9},{9,10},{10,1... | collective-permute-start | bytes 196616 | tf_op jit(solution)/shard_map/ppermute | solution.py:218
  43.7 5.8 %collective-permute-start.1 = (bf16[128,256]{1,0:T(8,128)(2,1)S(1)}, bf16[128,256]{1,0:T(8,128)(2,1)S(1)}, u32[]{:S(2)}, u32[]{:S(2)}) collective-permute-start(bf16[128,256]{1,0:T(8,128)(2,1)S(1)} %get-tuple-element.23), channel_id=1, source_target_pairs={{1,0},{2,1},{3,2},{4,3},{5,4},{6,5},{7,6},{8,7},{9,8},{10,9},{11,1... | collective-permute-start | bytes 196616 | tf_op jit(solution)/shard_map/ppermute | solution.py:218
  49.4 0.0 collective-permute-done.left_hbm
  49.4 1.9 %collective-permute-done.1.right_hbm = bf16[128,256]{1,0:T(8,128)(2,1)S(1)} collective-permute-done((bf16[128,256]{1,0:T(8,128)(2,1)S(1)}, bf16[128,256]{1,0:T(8,128)(2,1)S(1)}, u32[]{:S(2)}, u32[]{:S(2)}) %collective-permute-start.1) | collective-permute-done | bytes 65568 | tf_op jit(solution)/shard_map/ppermute | solution.py:218
  51.3 21.7 %all-to-all-done.received_hbm = bf16[12,128,256]{2,1,0:T(8,128)(2,1)S(1)} async-done(((bf16[12,128,256]{2,1,0:T(8,128)(2,1)}), bf16[12,128,256]{2,1,0:T(8,128)(2,1)S(1)}, u32[]{:S(2)}, u32[]{:S(2)}) %all-to-all-start) | async-done | bytes 786464 | tf_op jit(solution)/shard_map/all_to_all | solution.py:276
  73.1 0.0 copy-done.7
  73.1 0.0 copy-done.8
  73.1 0.0 copy-done.3
  73.1 0.0 copy-done.6
  73.1 0.0 copy-done.4
  73.1 0.0 copy-done.5
  73.1 0.0 copy-start.2
  73.1 1.6 copy-done.2
  74.7 9.0 %shard_map.129 = (bf16[8,128,256]{2,1,0:T(8,128)(2,1)}, f32[8,128,256]{2,1,0:T(8,128)S(1)}, bf16[2,128,256]{2,1,0:T(8,128)(2,1)S(1)}, bf16[12,128,256]{2,1,0:T(8...) custom-call(s32[8,8]{1,0:T(8,128)S(1)} %copy-done.6, s32[8,128]{1,0:T(8,128)S(1)} %bitcast.17, ...), custom_call_target="tpu_custom_call" | custom-call | flops 4000000000 | bytes 8000000 | tf_op jit(solution)/shard_map/pallas_call | solution.py:182
  83.7 10.8 %all-to-all-start.2 = ((bf16[64,8,256]{2,1,0:T(8,128)(2,1)}), bf16[64,8,256]{2,1,0:T(8,128)(2,1)S(1)}, u32[]{:S(2)}, u32[]{:S(2)}) async-start(bf16[64,8,256]{2,1,0:T(8,128)(2,1)} %bitcast.8), calls=%async_computation.2 | async-start | bytes 524288 | tf_op jit(solution)/shard_map/all_to_all | solution.py:227
  94.6 0.1 pad.3.clone
  94.6 11.5 %all-to-all-done.2 = bf16[64,8,256]{2,1,0:T(8,128)(2,1)S(1)} async-done(((bf16[64,8,256]{2,1,0:T(8,128)(2,1)}), bf16[64,8,256]{2,1,0:T(8,128)(2,1)S(1)}, u32[]{:S(2)}, u32[]{:S(2)}) %all-to-all-start.2) | async-done | bytes 262176 | tf_op jit(solution)/shard_map/all_to_all | solution.py:227
  106.1 0.1 convert_reduce_fusion
  106.2 0.0 copy-start.1
  106.2 0.1 maximum_maximum_fusion
  106.3 17.4 %all_to_all.25 = f32[12,24,128]{2,1,0:T(8,128)S(1)} all-to-all(f32[12,24,128]{2,1,0:T(8,128)S(1)} %broadcast_in_dim.20), channel_id=1, replica_groups=mesh['dom'=12,'inner'=64] {'dom'}, dimensions={0} | all-to-all | bytes 294912 | tf_op jit(solution)/shard_map/all_to_all | solution.py:234
  123.7 0.1 broadcast_in_dim.21
  123.8 20.2 %all_to_all.26.spread_ref = bf16[64,24,128]{2,1,0:T(8,128)(2,1)S(1)} all-to-all(bf16[64,24,128]{2,1,0:T(8,128)(2,1)S(1)} %broadcast_in_dim.21), channel_id=1, replica_groups=mesh['dom'=12,'inner'=64] {'inner'}, dimensions={0} | all-to-all | bytes 786432 | tf_op jit(solution)/shard_map/all_to_all | solution.py:237
  144.0 3.6 %all-to-all-start.1 = ((bf16[12,128,256]{2,1,0:T(8,128)(2,1)}), bf16[12,128,256]{2,1,0:T(8,128)(2,1)S(1)}, u32[]{:S(2)}, u32[]{:S(2)}) async-start(bf16[12,128,256]{2,1,0:T(8,128)(2,1)} %get-tuple-element.16), calls=%async_computation.1 | async-start | bytes 1572864 | tf_op jit(solution)/shard_map/all_to_all | solution.py:291
  147.7 2.3 %collective-permute-start.2 = (bf16[128,256]{1,0:T(8,128)(2,1)S(1)}, bf16[128,256]{1,0:T(8,128)(2,1)S(1)}, u32[]{:S(2)}, u32[]{:S(2)}) collective-permute-start(bf16[128,256]{1,0:T(8,128)(2,1)S(1)} %get-tuple-element.26), channel_id=1, source_target_pairs={{0,1},{1,2},{2,3},{3,4},{4,5},{5,6},{6,7},{7,8},{8,9},{9,10},{10,1... | collective-permute-start | bytes 196616 | tf_op jit(solution)/shard_map/ppermute | solution.py:218
  150.0 5.4 %collective-permute-start.3 = (bf16[128,256]{1,0:T(8,128)(2,1)S(1)}, bf16[128,256]{1,0:T(8,128)(2,1)S(1)}, u32[]{:S(2)}, u32[]{:S(2)}) collective-permute-start(bf16[128,256]{1,0:T(8,128)(2,1)S(1)} %get-tuple-element.25), channel_id=1, source_target_pairs={{1,0},{2,1},{3,2},{4,3},{5,4},{6,5},{7,6},{8,7},{9,8},{10,9},{11,1... | collective-permute-start | bytes 196616 | tf_op jit(solution)/shard_map/ppermute | solution.py:218
  155.4 0.8 shard_map.131
  156.2 0.0 collective-permute-done.2.low_ref
  156.2 1.1 collective-permute-done.3.high_ref
  157.3 25.0 %all-to-all-done.1.returned_ref = bf16[12,128,256]{2,1,0:T(8,128)(2,1)S(1)} async-done(((bf16[12,128,256]{2,1,0:T(8,128)(2,1)}), bf16[12,128,256]{2,1,0:T(8,128)(2,1)S(1)}, u32[]{:S(2)}, u32[]{:S(2)}) %all-to-all-start.1) | async-done | bytes 786464 | tf_op jit(solution)/shard_map/all_to_all | solution.py:291
  182.3 0.0 copy-done.1
  182.3 1.6 shard_map.130
  (7 shorter events, 0.1 us)
Async XLA Ops:
  0.6 41.1 %copy-start = (bf16[1024,256]{1,0:T(8,128)(2,1)S(1)}, bf16[1024,256]{1,0:T(8,128)(2,1)}, u32[]{:S(2)}) copy-start(bf16[1024,256]{1,0:T(8,128)(2,1)} %param.9) | copy-start | bytes 1572868
  0.6 72.4 %copy-start.7 = (s32[1024]{0:T(1024)S(1)}, s32[1024]{0:T(1024)}, u32[]{:S(2)}) copy-start(s32[1024]{0:T(1024)} %param.12) | copy-start | bytes 12292
  0.7 72.4 %copy-start.8 = (f32[256]{0:T(256)S(1)}, f32[256]{0:T(256)}, u32[]{:S(2)}) copy-start(f32[256]{0:T(256)} %param.16) | copy-start | bytes 3076
  0.7 72.4 %copy-start.3 = (bf16[1024,256]{1,0:T(8,128)(2,1)S(1)}, bf16[1024,256]{1,0:T(8,128)(2,1)}, u32[]{:S(2)}) copy-start(bf16[1024,256]{1,0:T(8,128)(2,1)} %param.17) | copy-start | bytes 1572868
  0.7 72.4 %copy-start.6 = (s32[8,8]{1,0:T(8,128)S(1)}, s32[8,8]{1,0:T(8,128)}, u32[]{:S(2)}) copy-start(s32[8,8]{1,0:T(8,128)} %pairs_ref.1) | copy-start | bytes 772
  0.7 72.4 %copy-start.4 = (bf16[256,256]{1,0:T(8,128)(2,1)S(1)}, bf16[256,256]{1,0:T(8,128)(2,1)}, u32[]{:S(2)}) copy-start(bf16[256,256]{1,0:T(8,128)(2,1)} %w_self_ref.1) | copy-start | bytes 393220
  0.7 72.4 %copy-start.5 = (bf16[256,256]{1,0:T(8,128)(2,1)S(1)}, bf16[256,256]{1,0:T(8,128)(2,1)}, u32[]{:S(2)}) copy-start(bf16[256,256]{1,0:T(8,128)(2,1)} %w_neigh_ref.1) | copy-start | bytes 393220
  26.5 46.5 %all-to-all-start = ((bf16[12,128,256]{2,1,0:T(8,128)(2,1)}), bf16[12,128,256]{2,1,0:T(8,128)(2,1)S(1)}, u32[]{:S(2)}, u32[]{:S(2)}) async-start(bf16[12,128,256]{2,1,0:T(8,128)(2,1)} %shard_map.128), calls=%async_computation | async-start | bytes 1572864 | tf_op jit(solution)/shard_map/all_to_all | solution.py:276
  41.7 7.7 %collective-permute-start = (bf16[128,256]{1,0:T(8,128)(2,1)S(1)}, bf16[128,256]{1,0:T(8,128)(2,1)S(1)}, u32[]{:S(2)}, u32[]{:S(2)}) collective-permute-start(bf16[128,256]{1,0:T(8,128)(2,1)S(1)} %get-tuple-element.24), channel_id=1, source_target_pairs={{0,1},{1,2},{2,3},{3,4},{4,5},{5,6},{6,7},{7,8},{8,9},{9,10},{10,1... | collective-permute-start | bytes 196616 | tf_op jit(solution)/shard_map/ppermute | solution.py:218
  43.7 7.6 %collective-permute-start.1 = (bf16[128,256]{1,0:T(8,128)(2,1)S(1)}, bf16[128,256]{1,0:T(8,128)(2,1)S(1)}, u32[]{:S(2)}, u32[]{:S(2)}) collective-permute-start(bf16[128,256]{1,0:T(8,128)(2,1)S(1)} %get-tuple-element.23), channel_id=1, source_target_pairs={{1,0},{2,1},{3,2},{4,3},{5,4},{6,5},{7,6},{8,7},{9,8},{10,9},{11,1... | collective-permute-start | bytes 196616 | tf_op jit(solution)/shard_map/ppermute | solution.py:218
  73.1 1.6 copy-start.2
  83.7 22.4 %all-to-all-start.2 = ((bf16[64,8,256]{2,1,0:T(8,128)(2,1)}), bf16[64,8,256]{2,1,0:T(8,128)(2,1)S(1)}, u32[]{:S(2)}, u32[]{:S(2)}) async-start(bf16[64,8,256]{2,1,0:T(8,128)(2,1)} %bitcast.8), calls=%async_computation.2 | async-start | bytes 524288 | tf_op jit(solution)/shard_map/all_to_all | solution.py:227
  106.2 76.1 %copy-start.1 = (s32[1,12]{1,0:T(1,128)S(1)}, s32[1,12]{1,0:T(1,128)}, u32[]{:S(2)}) copy-start(s32[1,12]{1,0:T(1,128)} %send_ref.3) | copy-start | bytes 148
  144.0 38.3 %all-to-all-start.1 = ((bf16[12,128,256]{2,1,0:T(8,128)(2,1)}), bf16[12,128,256]{2,1,0:T(8,128)(2,1)S(1)}, u32[]{:S(2)}, u32[]{:S(2)}) async-start(bf16[12,128,256]{2,1,0:T(8,128)(2,1)} %get-tuple-element.16), calls=%async_computation.1 | async-start | bytes 1572864 | tf_op jit(solution)/shard_map/all_to_all | solution.py:291
  147.7 8.5 %collective-permute-start.2 = (bf16[128,256]{1,0:T(8,128)(2,1)S(1)}, bf16[128,256]{1,0:T(8,128)(2,1)S(1)}, u32[]{:S(2)}, u32[]{:S(2)}) collective-permute-start(bf16[128,256]{1,0:T(8,128)(2,1)S(1)} %get-tuple-element.26), channel_id=1, source_target_pairs={{0,1},{1,2},{2,3},{3,4},{4,5},{5,6},{6,7},{7,8},{8,9},{9,10},{10,1... | collective-permute-start | bytes 196616 | tf_op jit(solution)/shard_map/ppermute | solution.py:218
  150.0 7.3 %collective-permute-start.3 = (bf16[128,256]{1,0:T(8,128)(2,1)S(1)}, bf16[128,256]{1,0:T(8,128)(2,1)S(1)}, u32[]{:S(2)}, u32[]{:S(2)}) collective-permute-start(bf16[128,256]{1,0:T(8,128)(2,1)S(1)} %get-tuple-element.25), channel_id=1, source_target_pairs={{1,0},{2,1},{3,2},{4,3},{5,4},{6,5},{7,6},{8,7},{9,8},{10,9},{11,1... | collective-permute-start | bytes 196616 | tf_op jit(solution)/shard_map/ppermute | solution.py:218

commit v3 on v2

--- a/solution.py
+++ b/solution.py
@@ -12,6 +12,7 @@
 VMEM = pl.BlockSpec(memory_space=pltpu.VMEM)
 SMEM = pl.BlockSpec(memory_space=pltpu.SMEM)
 ANY = pl.BlockSpec(memory_space=pl.ANY)
+HBM = pl.BlockSpec(memory_space=pltpu.HBM)
 F32 = jnp.float32
 BF16 = jnp.bfloat16
 CONTRACT_ROWS = (((0,), (0,)), ((), ()))
@@ -22,12 +23,26 @@
     return pltpu.CompilerParams(vmem_limit_bytes=32 * 1024 * 1024)
 
 
-def pick_kernel(send_ref, blocks_ref, out_ref, sems):
-    copies = []
+def pick_kernel(send_ref, blocks_ref, out_ref):
     for j in range(out_ref.shape[0]):
-        copies.append(
-            pltpu.make_async_copy(blocks_ref.at[send_ref[0, j]], out_ref.at[j], sems.at[j])
+        out_ref[j] = blocks_ref[send_ref[0, j]]
+
+
+def merge_kernel(pieces_ref, gbias_ref, slots_ref, merged_ref, piece, sems):
+    rows = slots_ref.shape[1] - piece.shape[0]
+    summed = jnp.sum(pieces_ref[...].astype(F32), axis=0)
+    bias = gbias_ref[...]
+    high = bias.astype(BF16).astype(F32)
+    tail = jnp.concatenate(
+        [high, bias - high, jnp.zeros((6, bias.shape[1]), F32)], axis=0
+    )
+    piece[...] = jnp.concatenate([summed, tail], axis=0).astype(BF16)
+    copies = [
+        pltpu.make_async_copy(
+            piece, merged_ref.at[j, pl.ds(rows, piece.shape[0])], sems.at[j]
         )
+        for j in range(merged_ref.shape[0])
+    ]
     for copy in copies:
         copy.start()
     for copy in copies:
@@ -146,7 +161,10 @@
 
     own_ref[...] = entries[:nblocks]
     rims_ref[...] = entries[nblocks : nblocks + 2].astype(BF16)
-    slots_ref[...] = entries[nblocks + 2 :].astype(BF16)
+    slots_ref[:, :rows, :] = entries[nblocks + 2 :].astype(BF16)
+    slots_ref[:, rows:, :] = jnp.zeros(
+        (slots_ref.shape[0], slots_ref.shape[1] - rows, width), BF16
+    )
 
     grads = grad_pre[...]
     features = table[:nblocks].reshape(nblocks * rows, width)
@@ -167,7 +185,7 @@
     total[last] = total[last] + high_ref[...].astype(F32)
     for j in range(returned_ref.shape[0]):
         block = send_ref[0, j]
-        total[block] = total[block] + returned_ref[j].astype(F32)
+        total[block] = total[block] + returned_ref[j, : total.shape[1]].astype(F32)
     out_ref[...] = total[...].astype(BF16)
 
 
@@ -178,6 +196,7 @@
     width = blocks.shape[2]
     dom = received.shape[0]
     entries = nblocks + 2 + dom
+    extra = 2 * width // lax.axis_size("inner") + 8
     shape = jax.ShapeDtypeStruct
     return pl.pallas_call(
         layer_kernel,
@@ -185,11 +204,11 @@
             shape(blocks.shape, BF16),
             shape(blocks.shape, F32),
             shape((2, rows, width), BF16),
-            shape((dom, rows, width), BF16),
+            shape((dom, rows + extra, width), BF16),
             shape((2 * width, width), BF16),
             shape((1, width), F32),
         ),
-        in_specs=[SMEM] + [VMEM] * 4 + [ANY] * 6,
+        in_specs=[SMEM] + [VMEM] * 4 + [ANY] * 4 + [HBM] * 2,
         out_specs=(ANY,) + (VMEM,) * 5,
         scratch_shapes=[
             pltpu.VMEM((entries, rows, width), BF16),
@@ -218,21 +237,35 @@
     return lax.ppermute(low_source, axis, forward), lax.ppermute(high_source, axis, backward)
 
 
-def reduce_grads(grads, gbias, scale):
-    dom_size = lax.axis_size("dom")
+def merge_grads(grads, gbias, slots):
     inner_size = lax.axis_size("inner")
     hidden = grads.shape[1]
-    rows = grads.shape[0] // inner_size
-    chunks = grads.reshape(inner_size, rows, hidden)
+    chunks = grads.reshape(inner_size, grads.shape[0] // inner_size, hidden)
     pieces = lax.all_to_all(chunks, "inner", split_axis=0, concat_axis=0, tiled=True)
-    piece = jnp.sum(pieces.astype(F32), axis=0)
-    piece = [piece[:, k : k + LANES] for k in range(0, hidden, LANES)]
-    bias_rows = hidden // LANES
+    return pl.pallas_call(
+        merge_kernel,
+        out_shape=jax.ShapeDtypeStruct(slots.shape, BF16),
+        in_specs=[VMEM, VMEM, ANY],
+        out_specs=ANY,
+        scratch_shapes=[
+            pltpu.VMEM((chunks.shape[1] + 8, hidden), BF16),
+            pltpu.SemaphoreType.DMA((slots.shape[0],)),
+        ],
+        input_output_aliases={2: 0},
+        compiler_params=params(),
+    )(pieces, gbias, slots)
+
+
+def spread_grads(extra, scale):
+    inner_size = lax.axis_size("inner")
+    hidden = extra.shape[2]
+    rows = extra.shape[1] - 8
+    summed = jnp.sum(extra.astype(F32), axis=0) * scale
+    lanes = [summed[:rows, k : k + LANES] for k in range(0, hidden, LANES)]
+    bias = (summed[rows] + summed[rows + 1]).reshape(-1, LANES)
+    bias_rows = bias.shape[0]
     spare = jnp.zeros((8 - bias_rows, LANES), F32)
-    piece = jnp.concatenate(piece + [gbias.reshape(bias_rows, LANES), spare], axis=0)
-    spread = jnp.broadcast_to(piece[None], (dom_size,) + piece.shape)
-    spread = lax.all_to_all(spread, "dom", split_axis=0, concat_axis=0, tiled=True)
-    piece = (jnp.sum(spread, axis=0) * scale).astype(BF16)
+    piece = jnp.concatenate(lanes + [bias, spare], axis=0).astype(BF16)
     spread = jnp.broadcast_to(piece[None], (inner_size,) + piece.shape)
     spread = lax.all_to_all(spread, "inner", split_axis=0, concat_axis=0, tiled=True)
     return pl.pallas_call(
@@ -269,9 +302,9 @@
     outgoing = pl.pallas_call(
         pick_kernel,
         out_shape=jax.ShapeDtypeStruct((dom_size, rows, width), BF16),
-        in_specs=[SMEM, ANY],
-        out_specs=ANY,
-        scratch_shapes=[pltpu.SemaphoreType.DMA((dom_size,))],
+        in_specs=[SMEM, VMEM],
+        out_specs=VMEM,
+        compiler_params=params(),
     )(send_blocks, blocks)
     received = lax.all_to_all(outgoing, "dom", split_axis=0, concat_axis=0, tiled=True)
     left, right = neighbours(blocks[nblocks - 1], blocks[0], "inner")
@@ -288,7 +321,8 @@
         w_neigh,
         bias[None, :],
     )
-    returned = lax.all_to_all(slots, "dom", split_axis=0, concat_axis=0, tiled=True)
+    merged = merge_grads(grads, gbias, slots)
+    returned = lax.all_to_all(merged, "dom", split_axis=0, concat_axis=0, tiled=True)
     low, high = neighbours(rims[1], rims[0], "inner")
     grad_features = pl.pallas_call(
         combine_kernel,
@@ -302,7 +336,7 @@
         ),
     )(send_blocks, own, returned, low, high)
     scale = 1.0 / math.sqrt(rows_dev * dom_size * lax.axis_size("inner"))
-    sum_self, sum_neigh, sum_bias = reduce_grads(grads, gbias, scale)
+    sum_self, sum_neigh, sum_bias = spread_grads(returned[:, rows:], scale)
     return (
         layer_out.reshape(rows_dev, width),
         grad_features.reshape(rows_dev, width),

time: 184 us -> 150 us (0.82)
  the two profiles are of different devices: /device:TPU:6 before, /device:TPU:1 now
where the time goes in v3:
time: 150 us; the launch traced here: 149 us
  waiting for transfers between devices  63.1 us (42%)
  starting transfers between devices  41.7 us (28%)
  blocking collectives  26.1 us (17%)
  Pallas kernels  13.3 us (9%)
  local copies, waits for them, and re-layouts  4.22 us (3%)
    all_to_all x1, waiting for transfers between devices, per_device(): lax.all_to_all(merged, 'dom', split_axis=0, concat_axis=0, tiled=True)  33 us
    all_to_all x1, blocking collectives, merge_grads(): lax.all_to_all(chunks, 'inner', split_axis=0, concat_axis=0, tiled=True)  26.1 us
    all_to_all x1, waiting for transfers between devices, per_device(): lax.all_to_all(outgoing, 'dom', split_axis=0, concat_axis=0, tiled=True)  18.5 us
    all_to_all x1, starting transfers between devices, per_device(): lax.all_to_all(outgoing, 'dom', split_axis=0, concat_axis=0, tiled=True)  15.7 us
    all_to_all x1, starting transfers between devices, spread_grads(): lax.all_to_all(spread, 'inner', split_axis=0, concat_axis=0, tiled=True)  10.4 us
    pallas_call x1, Pallas kernels, call_layer(): pl.pallas_call(layer_kernel, out_shape=(shape(blocks.shape, BF16), shape(...  8.56 us
    ppermute x2, starting transfers between devices, neighbours(): lax.ppermute(low_source, axis, forward)  7.59 us
    ppermute x2, waiting for transfers between devices, neighbours(): lax.ppermute(high_source, axis, backward)  7 us
  transfers between devices with their start and end apart: 7, of which 6 were waited for; matrix products, arithmetic and copies ran while one was open for 0% of the time, Pallas kernels for 1%

profile of v3, /device:TPU:1, one launch (start us, length us, event | category | flops | bytes accessed | tf_op | source)
XLA Modules:
  0.0 149.4 jit_solution(29485464161604393)
XLA Ops:
  0.6 0.0 copy-start.10
  0.6 0.0 copy-start
  0.7 1.0 copy-done
  1.7 0.0 copy-start.2
  1.7 0.7 copy-done.2
  2.3 0.0 copy-start.1
  2.4 0.0 copy-start.5
  2.4 0.0 copy-start.6
  2.4 0.0 copy-start.7
  2.4 0.0 copy-start.8
  2.4 0.0 copy-start.9
  2.4 1.5 shard_map.128
  3.9 15.7 %all-to-all-start = ((bf16[12,128,256]{2,1,0:T(8,128)(2,1)}), bf16[12,128,256]{2,1,0:T(8,128)(2,1)S(1)}, u32[]{:S(2)}, u32[]{:S(2)}) async-start(bf16[12,128,256]{2,1,0:T(8,128)(2,1)} %shard_map.128), calls=%async_computation | async-start | bytes 1572864 | tf_op jit(solution)/shard_map/all_to_all | solution.py:309
  19.6 0.0 copy-done.1
  19.6 4.0 %collective-permute-start = (bf16[128,256]{1,0:T(8,128)(2,1)S(1)}, bf16[128,256]{1,0:T(8,128)(2,1)S(1)}, u32[]{:S(2)}, u32[]{:S(2)}) collective-permute-start(bf16[128,256]{1,0:T(8,128)(2,1)S(1)} %get-tuple-element.24), channel_id=1, source_target_pairs={{0,1},{1,2},{2,3},{3,4},{4,5},{5,6},{6,7},{7,8},{8,9},{9,10},{10,1... | collective-permute-start | bytes 196616 | tf_op jit(solution)/shard_map/ppermute | solution.py:237
  23.6 1.9 %collective-permute-start.1 = (bf16[128,256]{1,0:T(8,128)(2,1)S(1)}, bf16[128,256]{1,0:T(8,128)(2,1)S(1)}, u32[]{:S(2)}, u32[]{:S(2)}) collective-permute-start(bf16[128,256]{1,0:T(8,128)(2,1)S(1)} %get-tuple-element.23), channel_id=1, source_target_pairs={{1,0},{2,1},{3,2},{4,3},{5,4},{6,5},{7,6},{8,7},{9,8},{10,9},{11,1... | collective-permute-start | bytes 196616 | tf_op jit(solution)/shard_map/ppermute | solution.py:237
  25.6 0.0 collective-permute-done.left_hbm
  25.6 3.6 %collective-permute-done.1.right_hbm = bf16[128,256]{1,0:T(8,128)(2,1)S(1)} collective-permute-done((bf16[128,256]{1,0:T(8,128)(2,1)S(1)}, bf16[128,256]{1,0:T(8,128)(2,1)S(1)}, u32[]{:S(2)}, u32[]{:S(2)}) %collective-permute-start.1) | collective-permute-done | bytes 65568 | tf_op jit(solution)/shard_map/ppermute | solution.py:237
  29.2 18.5 %all-to-all-done.received_hbm = bf16[12,128,256]{2,1,0:T(8,128)(2,1)S(1)} async-done(((bf16[12,128,256]{2,1,0:T(8,128)(2,1)}), bf16[12,128,256]{2,1,0:T(8,128)(2,1)S(1)}, u32[]{:S(2)}, u32[]{:S(2)}) %all-to-all-start) | async-done | bytes 786464 | tf_op jit(solution)/shard_map/all_to_all | solution.py:309
  47.7 0.0 copy-done.10
  47.7 0.0 copy-done.5
  47.7 0.0 copy-done.6
  47.7 0.0 copy-done.7
  47.7 0.0 copy-done.8
  47.7 0.0 copy-done.9
  47.7 0.0 copy-start.4
  47.8 1.6 %copy-done.4 = bf16[8,8,128,128]{3,2,1,0:T(8,128)(2,1)S(1)} copy-done((bf16[8,8,128,128]{3,2,1,0:T(8,128)(2,1)S(1)}, bf16[8,8,128,128]{3,2,1,0:T(8,128)(2,1)}, u32[]{:S(2)}) %copy-start.4) | copy-done | bytes 2097176
  49.3 8.6 %shard_map.129 = (bf16[8,128,256]{2,1,0:T(8,128)(2,1)}, f32[8,128,256]{2,1,0:T(8,128)S(1)}, bf16[2,128,256]{2,1,0:T(8,128)(2,1)S(1)}, bf16[12,144,256]{2,1,0:T(8...) custom-call(s32[8,8]{1,0:T(8,128)S(1)} %copy-done.8, s32[8,128]{1,0:T(8,128)S(1)} %bitcast.17, ...), custom_call_target="tpu_custom_call" | custom-call | flops 4000000000 | bytes 8000000 | tf_op jit(solution)/shard_map/pallas_call | solution.py:201
  57.9 26.1 %all_to_all.20.pieces_ref = bf16[64,8,256]{2,1,0:T(8,128)(2,1)S(1)} all-to-all(bf16[64,8,256]{2,1,0:T(8,128)(2,1)S(1)} %bitcast.15), channel_id=1, replica_groups=mesh['dom'=12,'inner'=64] {'inner'}, dimensions={0} | all-to-all | bytes 524288 | tf_op jit(solution)/shard_map/all_to_all | solution.py:244
  84.0 0.8 shard_map.130
  84.8 0.0 copy-start.3
  84.8 4.2 %all-to-all-start.2 = ((bf16[12,144,256]{2,1,0:T(8,128)(2,1)}), bf16[12,144,256]{2,1,0:T(8,128)(2,1)S(1)}, u32[]{:S(2)}, u32[]{:S(2)}) async-start(bf16[12,144,256]{2,1,0:T(8,128)(2,1)} %shard_map.130), calls=%async_computation.2 | async-start | bytes 1769472 | tf_op jit(solution)/shard_map/all_to_all | solution.py:325
  89.0 0.1 pad.3.clone
  89.1 33.0 %all-to-all-done.2.returned_ref = bf16[12,144,256]{2,1,0:T(8,128)(2,1)S(1)} async-done(((bf16[12,144,256]{2,1,0:T(8,128)(2,1)}), bf16[12,144,256]{2,1,0:T(8,128)(2,1)S(1)}, u32[]{:S(2)}, u32[]{:S(2)}) %all-to-all-start.2) | async-done | bytes 884768 | tf_op jit(solution)/shard_map/all_to_all | solution.py:325
  122.2 0.1 maximum_maximum_fusion
  122.3 0.8 broadcast_in_dim.14
  123.1 10.4 %all-to-all-start.3 = ((bf16[64,24,128]{2,1,0:T(8,128)(2,1)}), bf16[64,24,128]{2,1,0:T(8,128)(2,1)S(1)}, u32[]{:S(2)}, u32[]{:S(2)}) async-start(bf16[64,24,128]{2,1,0:T(8,128)(2,1)} %broadcast_in_dim.14), calls=%async_computation.3 | async-start | bytes 786432 | tf_op jit(solution)/shard_map/all_to_all | solution.py:270
  133.5 3.5 %collective-permute-start.2 = (bf16[128,256]{1,0:T(8,128)(2,1)S(1)}, bf16[128,256]{1,0:T(8,128)(2,1)S(1)}, u32[]{:S(2)}, u32[]{:S(2)}) collective-permute-start(bf16[128,256]{1,0:T(8,128)(2,1)S(1)} %get-tuple-element.26), channel_id=1, source_target_pairs={{0,1},{1,2},{2,3},{3,4},{4,5},{5,6},{6,7},{7,8},{8,9},{9,10},{10,1... | collective-permute-start | bytes 196616 | tf_op jit(solution)/shard_map/ppermute | solution.py:237
  137.0 1.9 %collective-permute-start.3 = (bf16[128,256]{1,0:T(8,128)(2,1)S(1)}, bf16[128,256]{1,0:T(8,128)(2,1)S(1)}, u32[]{:S(2)}, u32[]{:S(2)}) collective-permute-start(bf16[128,256]{1,0:T(8,128)(2,1)S(1)} %get-tuple-element.25), channel_id=1, source_target_pairs={{1,0},{2,1},{3,2},{4,3},{5,4},{6,5},{7,6},{8,7},{9,8},{10,9},{11,1... | collective-permute-start | bytes 196616 | tf_op jit(solution)/shard_map/ppermute | solution.py:237
  138.9 2.7 %collective-permute-done.2.low_ref = bf16[128,256]{1,0:T(8,128)(2,1)S(1)} collective-permute-done((bf16[128,256]{1,0:T(8,128)(2,1)S(1)}, bf16[128,256]{1,0:T(8,128)(2,1)S(1)}, u32[]{:S(2)}, u32[]{:S(2)}) %collective-permute-start.2) | collective-permute-done | bytes 65568 | tf_op jit(solution)/shard_map/ppermute | solution.py:237
  141.7 3.4 %collective-permute-done.3.high_ref = bf16[128,256]{1,0:T(8,128)(2,1)S(1)} collective-permute-done((bf16[128,256]{1,0:T(8,128)(2,1)S(1)}, bf16[128,256]{1,0:T(8,128)(2,1)S(1)}, u32[]{:S(2)}, u32[]{:S(2)}) %collective-permute-start.3) | collective-permute-done | bytes 65568 | tf_op jit(solution)/shard_map/ppermute | solution.py:237
  145.0 0.0 copy-done.3
  145.0 1.6 %shard_map.131 = bf16[8,128,256]{2,1,0:T(8,128)(2,1)} custom-call(s32[1,12]{1,0:T(1,128)S(1)} %copy-done.3, f32[8,128,256]{2,1,0:T(8,128)S(1)} %get-tuple-element.15.own_ref, bf16[12,144,256]{2,1,0:T(8,128)(2,1)S(1)} %all-to-all-done.2.returned_ref, bf16[128,256]{1,0:T(8,128)(2,1)S(1)} %collective-permute-done.2.low_ref, ...), custom_call_target="tpu_custom_call" | custom-call | flops 1000000 | bytes 3000000 | tf_op jit(solution)/shard_map/pallas_call | solution.py:327
  146.6 1.9 %all-to-all-done.3.spread_ref = bf16[64,24,128]{2,1,0:T(8,128)(2,1)S(1)} async-done(((bf16[64,24,128]{2,1,0:T(8,128)(2,1)}), bf16[64,24,128]{2,1,0:T(8,128)(2,1)S(1)}, u32[]{:S(2)}, u32[]{:S(2)}) %all-to-all-start.3) | async-done | bytes 393248 | tf_op jit(solution)/shard_map/all_to_all | solution.py:270
  148.6 0.8 shard_map.132
  (7 shorter events, 0.1 us)
Async XLA Ops:
  0.6 47.1 %copy-start.10 = (f32[256]{0:T(256)S(1)}, f32[256]{0:T(256)}, u32[]{:S(2)}) copy-start(f32[256]{0:T(256)} %param.16) | copy-start | bytes 3076
  0.6 1.0 copy-start
  1.7 0.7 copy-start.2
  2.3 17.2 %copy-start.1 = (bf16[1024,256]{1,0:T(8,128)(2,1)S(1)}, bf16[1024,256]{1,0:T(8,128)(2,1)}, u32[]{:S(2)}) copy-start(bf16[1024,256]{1,0:T(8,128)(2,1)} %param.9) | copy-start | bytes 1572868
  2.4 45.4 %copy-start.5 = (bf16[1024,256]{1,0:T(8,128)(2,1)S(1)}, bf16[1024,256]{1,0:T(8,128)(2,1)}, u32[]{:S(2)}) copy-start(bf16[1024,256]{1,0:T(8,128)(2,1)} %param.17) | copy-start | bytes 1572868
  2.4 45.4 %copy-start.6 = (bf16[256,256]{1,0:T(8,128)(2,1)S(1)}, bf16[256,256]{1,0:T(8,128)(2,1)}, u32[]{:S(2)}) copy-start(bf16[256,256]{1,0:T(8,128)(2,1)} %w_self_ref.1) | copy-start | bytes 393220
  2.4 45.4 %copy-start.7 = (bf16[256,256]{1,0:T(8,128)(2,1)S(1)}, bf16[256,256]{1,0:T(8,128)(2,1)}, u32[]{:S(2)}) copy-start(bf16[256,256]{1,0:T(8,128)(2,1)} %w_neigh_ref.1) | copy-start | bytes 393220
  2.4 45.4 %copy-start.8 = (s32[8,8]{1,0:T(8,128)S(1)}, s32[8,8]{1,0:T(8,128)}, u32[]{:S(2)}) copy-start(s32[8,8]{1,0:T(8,128)} %pairs_ref.1) | copy-start | bytes 772
  2.4 45.4 %copy-start.9 = (s32[1024]{0:T(1024)S(1)}, s32[1024]{0:T(1024)}, u32[]{:S(2)}) copy-start(s32[1024]{0:T(1024)} %param.12) | copy-start | bytes 12292
  3.9 43.9 %all-to-all-start = ((bf16[12,128,256]{2,1,0:T(8,128)(2,1)}), bf16[12,128,256]{2,1,0:T(8,128)(2,1)S(1)}, u32[]{:S(2)}, u32[]{:S(2)}) async-start(bf16[12,128,256]{2,1,0:T(8,128)(2,1)} %shard_map.128), calls=%async_computation | async-start | bytes 1572864 | tf_op jit(solution)/shard_map/all_to_all | solution.py:309
  19.6 6.0 %collective-permute-start = (bf16[128,256]{1,0:T(8,128)(2,1)S(1)}, bf16[128,256]{1,0:T(8,128)(2,1)S(1)}, u32[]{:S(2)}, u32[]{:S(2)}) collective-permute-start(bf16[128,256]{1,0:T(8,128)(2,1)S(1)} %get-tuple-element.24), channel_id=1, source_target_pairs={{0,1},{1,2},{2,3},{3,4},{4,5},{5,6},{6,7},{7,8},{8,9},{9,10},{10,1... | collective-permute-start | bytes 196616 | tf_op jit(solution)/shard_map/ppermute | solution.py:237
  23.6 5.6 %collective-permute-start.1 = (bf16[128,256]{1,0:T(8,128)(2,1)S(1)}, bf16[128,256]{1,0:T(8,128)(2,1)S(1)}, u32[]{:S(2)}, u32[]{:S(2)}) collective-permute-start(bf16[128,256]{1,0:T(8,128)(2,1)S(1)} %get-tuple-element.23), channel_id=1, source_target_pairs={{1,0},{2,1},{3,2},{4,3},{5,4},{6,5},{7,6},{8,7},{9,8},{10,9},{11,1... | collective-permute-start | bytes 196616 | tf_op jit(solution)/shard_map/ppermute | solution.py:237
  47.7 1.6 %copy-start.4 = (bf16[8,8,128,128]{3,2,1,0:T(8,128)(2,1)S(1)}, bf16[8,8,128,128]{3,2,1,0:T(8,128)(2,1)}, u32[]{:S(2)}) copy-start(bf16[8,8,128,128]{3,2,1,0:T(8,128)(2,1)} %tiles_hbm.1) | copy-start | bytes 6291460
  84.8 60.2 %copy-start.3 = (s32[1,12]{1,0:T(1,128)S(1)}, s32[1,12]{1,0:T(1,128)}, u32[]{:S(2)}) copy-start(s32[1,12]{1,0:T(1,128)} %send_ref.3) | copy-start | bytes 148
  84.8 37.3 %all-to-all-start.2 = ((bf16[12,144,256]{2,1,0:T(8,128)(2,1)}), bf16[12,144,256]{2,1,0:T(8,128)(2,1)S(1)}, u32[]{:S(2)}, u32[]{:S(2)}) async-start(bf16[12,144,256]{2,1,0:T(8,128)(2,1)} %shard_map.130), calls=%async_computation.2 | async-start | bytes 1769472 | tf_op jit(solution)/shard_map/all_to_all | solution.py:325
  123.1 25.5 %all-to-all-start.3 = ((bf16[64,24,128]{2,1,0:T(8,128)(2,1)}), bf16[64,24,128]{2,1,0:T(8,128)(2,1)S(1)}, u32[]{:S(2)}, u32[]{:S(2)}) async-start(bf16[64,24,128]{2,1,0:T(8,128)(2,1)} %broadcast_in_dim.14), calls=%async_computation.3 | async-start | bytes 786432 | tf_op jit(solution)/shard_map/all_to_all | solution.py:270
  133.5 8.2 %collective-permute-start.2 = (bf16[128,256]{1,0:T(8,128)(2,1)S(1)}, bf16[128,256]{1,0:T(8,128)(2,1)S(1)}, u32[]{:S(2)}, u32[]{:S(2)}) collective-permute-start(bf16[128,256]{1,0:T(8,128)(2,1)S(1)} %get-tuple-element.26), channel_id=1, source_target_pairs={{0,1},{1,2},{2,3},{3,4},{4,5},{5,6},{6,7},{7,8},{8,9},{9,10},{10,1... | collective-permute-start | bytes 196616 | tf_op jit(solution)/shard_map/ppermute | solution.py:237
  137.0 8.0 %collective-permute-start.3 = (bf16[128,256]{1,0:T(8,128)(2,1)S(1)}, bf16[128,256]{1,0:T(8,128)(2,1)S(1)}, u32[]{:S(2)}, u32[]{:S(2)}) collective-permute-start(bf16[128,256]{1,0:T(8,128)(2,1)S(1)} %get-tuple-element.25), channel_id=1, source_target_pairs={{1,0},{2,1},{3,2},{4,3},{5,4},{6,5},{7,6},{8,7},{9,8},{10,9},{11,1... | collective-permute-start | bytes 196616 | tf_op jit(solution)/shard_map/ppermute | solution.py:237

commit v4 on v3

--- a/solution.py
+++ b/solution.py
@@ -19,13 +19,19 @@
 CONTRACT_COLS = (((1,), (1,)), ((), ()))
 
 
-def params():
-    return pltpu.CompilerParams(vmem_limit_bytes=32 * 1024 * 1024)
-
-
-def pick_kernel(send_ref, blocks_ref, out_ref):
-    for j in range(out_ref.shape[0]):
-        out_ref[j] = blocks_ref[send_ref[0, j]]
+def params(mebibytes=32):
+    return pltpu.CompilerParams(vmem_limit_bytes=mebibytes * 1024 * 1024)
+
+
+def pick_kernel(send_ref, blocks_ref, out_ref, sems):
+    copies = [
+        pltpu.make_async_copy(blocks_ref.at[send_ref[0, j]], out_ref.at[j], sems.at[j])
+        for j in range(out_ref.shape[0])
+    ]
+    for copy in copies:
+        copy.start()
+    for copy in copies:
+        copy.wait()
 
 
 def merge_kernel(pieces_ref, gbias_ref, slots_ref, merged_ref, piece, sems):
@@ -49,7 +55,24 @@
         copy.wait()
 
 
-def layer_kernel(
+def tile_row(tiles, b):
+    return jnp.concatenate([tiles[b, p] for p in range(tiles.shape[1])], axis=1)
+
+
+def by_degree(values, inverse, b):
+    rows = inverse.shape[1]
+    return jnp.concatenate(
+        [values[:, k : k + rows] * inverse[b] for k in range(0, values.shape[1], rows)], axis=1
+    )
+
+
+def invert_degree(degree_ref, inverse):
+    for b in range(inverse.shape[0]):
+        row = 1.0 / degree_ref[b : b + 1, :].astype(F32)
+        inverse[b] = jnp.broadcast_to(row, inverse.shape[1:]).T
+
+
+def forward_kernel(
     pairs_ref,
     degree_ref,
     w_self_ref,
@@ -62,9 +85,7 @@
     tiles_hbm,
     cot_hbm,
     out_hbm,
-    own_ref,
-    rims_ref,
-    slots_ref,
+    grad_hbm,
     grads_ref,
     gbias_ref,
     table,
@@ -75,7 +96,6 @@
     mean,
     grad_pre,
     inverse,
-    entries,
     sems,
     tile_sems,
 ):
@@ -95,34 +115,22 @@
     ]
     cot_copy = pltpu.make_async_copy(cot_hbm, cot, sems.at[4])
     out_copy = pltpu.make_async_copy(out, out_hbm, sems.at[5])
+    grad_copy = pltpu.make_async_copy(grad_pre, grad_hbm, sems.at[6])
     for copy in copies:
         copy.start()
     for copy in tile_copies:
         copy.start()
     cot_copy.start()
-
-    for b in range(nblocks):
-        row = 1.0 / degree_ref[b : b + 1, :].astype(F32)
-        inverse[b] = jnp.broadcast_to(row, (rows, rows)).T
-    entries[nblocks:] = jnp.zeros((entries.shape[0] - nblocks, rows, width), F32)
-
+    invert_degree(degree_ref, inverse)
     for copy in copies:
         copy.wait()
-
-    def tile_row(b):
-        return jnp.concatenate([tiles[b, p] for p in range(npairs)], axis=1)
-
-    def by_degree(values, b):
-        return jnp.concatenate(
-            [values[:, k : k + rows] * inverse[b] for k in range(0, width, rows)], axis=1
-        )
 
     for b in range(nblocks):
         for p in range(npairs):
             sources[b % 2, pl.ds(p * rows, rows), :] = table[pairs_ref[b, p]]
         tile_copies[b].wait()
-        summed = jnp.dot(tile_row(b), sources[b % 2], preferred_element_type=F32)
-        mean[b] = by_degree(summed, b).astype(BF16)
+        summed = jnp.dot(tile_row(tiles, b), sources[b % 2], preferred_element_type=F32)
+        mean[b] = by_degree(summed, inverse, b).astype(BF16)
 
     cot_copy.wait()
     w_self = w_self_ref[...]
@@ -143,28 +151,9 @@
         grad = (cots * sigma * (1.0 + preact * (1.0 - sigma))).astype(BF16)
         grad_pre[pl.ds(b * rows, step * rows), :] = grad
         gbias = gbias + jnp.sum(grad.astype(F32), axis=0, keepdims=True)
-        own = lax.dot_general(grad, w_self, CONTRACT_COLS, preferred_element_type=F32)
-        entries[b : b + step] = own.reshape(step, rows, width)
+    grad_copy.start()
     out_copy.start()
     gbias_ref[...] = gbias
-
-    for b in range(nblocks):
-        grad = grad_pre[pl.ds(b * rows, rows), :]
-        grad_mean = lax.dot_general(grad, w_neigh, CONTRACT_COLS, preferred_element_type=F32)
-        grad_mean = by_degree(grad_mean, b).astype(BF16)
-        parts = lax.dot_general(
-            tile_row(b), grad_mean, CONTRACT_ROWS, preferred_element_type=F32
-        )
-        for p in range(npairs):
-            entry = pairs_ref[b, p]
-            entries[entry] = entries[entry] + parts[p * rows : (p + 1) * rows]
-
-    own_ref[...] = entries[:nblocks]
-    rims_ref[...] = entries[nblocks : nblocks + 2].astype(BF16)
-    slots_ref[:, :rows, :] = entries[nblocks + 2 :].astype(BF16)
-    slots_ref[:, rows:, :] = jnp.zeros(
-        (slots_ref.shape[0], slots_ref.shape[1] - rows, width), BF16
-    )
 
     grads = grad_pre[...]
     features = table[:nblocks].reshape(nblocks * rows, width)
@@ -175,7 +164,57 @@
     grads_ref[width:, :] = lax.dot_general(
         means, grads, CONTRACT_ROWS, preferred_element_type=F32
     ).astype(BF16)
+    grad_copy.wait()
     out_copy.wait()
+
+
+def backward_kernel(
+    pairs_ref,
+    degree_ref,
+    w_self_ref,
+    w_neigh_ref,
+    grad_ref,
+    tiles_hbm,
+    own_ref,
+    rims_ref,
+    slots_ref,
+    tiles,
+    inverse,
+    entries,
+    tile_sems,
+):
+    nblocks, npairs, rows, _ = tiles.shape
+    width = w_self_ref.shape[0]
+    tile_copies = [
+        pltpu.make_async_copy(tiles_hbm.at[b], tiles.at[b], tile_sems.at[b])
+        for b in range(nblocks)
+    ]
+    for copy in tile_copies:
+        copy.start()
+    invert_degree(degree_ref, inverse)
+    entries[nblocks:] = jnp.zeros((entries.shape[0] - nblocks, rows, width), F32)
+    w_self = w_self_ref[...]
+    w_neigh = w_neigh_ref[...]
+    own = lax.dot_general(grad_ref[...], w_self, CONTRACT_COLS, preferred_element_type=F32)
+    entries[:nblocks] = own.reshape(nblocks, rows, width)
+    for b in range(nblocks):
+        grad = grad_ref[pl.ds(b * rows, rows), :]
+        grad_mean = lax.dot_general(grad, w_neigh, CONTRACT_COLS, preferred_element_type=F32)
+        grad_mean = by_degree(grad_mean, inverse, b).astype(BF16)
+        tile_copies[b].wait()
+        parts = lax.dot_general(
+            tile_row(tiles, b), grad_mean, CONTRACT_ROWS, preferred_element_type=F32
+        )
+        for p in range(npairs):
+            entry = pairs_ref[b, p]
+            entries[entry] = entries[entry] + parts[p * rows : (p + 1) * rows]
+
+    own_ref[...] = entries[:nblocks]
+    rims_ref[...] = entries[nblocks : nblocks + 2].astype(BF16)
+    slots_ref[:, :rows, :] = entries[nblocks + 2 :].astype(BF16)
+    slots_ref[:, rows:, :] = jnp.zeros(
+        (slots_ref.shape[0], slots_ref.shape[1] - rows, width), BF16
+    )
 
 
 def combine_kernel(send_ref, own_ref, returned_ref, low_ref, high_ref, out_ref, total):
@@ -189,27 +228,23 @@
     out_ref[...] = total[...].astype(BF16)
 
 
-def call_layer(
+def call_forward(
     blocks, left, right, received, tiles, cot, pairs, degree, w_self, w_neigh, bias
 ):
     nblocks, npairs, rows, _ = tiles.shape
     width = blocks.shape[2]
-    dom = received.shape[0]
-    entries = nblocks + 2 + dom
-    extra = 2 * width // lax.axis_size("inner") + 8
+    entries = nblocks + 2 + received.shape[0]
     shape = jax.ShapeDtypeStruct
     return pl.pallas_call(
-        layer_kernel,
+        forward_kernel,
         out_shape=(
             shape(blocks.shape, BF16),
-            shape(blocks.shape, F32),
-            shape((2, rows, width), BF16),
-            shape((dom, rows + extra, width), BF16),
+            shape((nblocks * rows, width), BF16),
             shape((2 * width, width), BF16),
             shape((1, width), F32),
         ),
         in_specs=[SMEM] + [VMEM] * 4 + [ANY] * 4 + [HBM] * 2,
-        out_specs=(ANY,) + (VMEM,) * 5,
+        out_specs=(ANY, ANY, VMEM, VMEM),
         scratch_shapes=[
             pltpu.VMEM((entries, rows, width), BF16),
             pltpu.VMEM(tiles.shape, BF16),
@@ -219,15 +254,42 @@
             pltpu.VMEM(blocks.shape, BF16),
             pltpu.VMEM((nblocks * rows, width), BF16),
             pltpu.VMEM((nblocks, rows, rows), F32),
-            pltpu.VMEM((entries, rows, width), F32),
-            pltpu.SemaphoreType.DMA((6,)),
+            pltpu.SemaphoreType.DMA((7,)),
+            pltpu.SemaphoreType.DMA((nblocks,)),
+        ],
+        compiler_params=params(58),
+        cost_estimate=pl.CostEstimate(
+            flops=2 * 10**9, bytes_accessed=6 * 10**6, transcendentals=nblocks * rows * width
+        ),
+    )(pairs, degree, w_self, w_neigh, bias, blocks, left, right, received, tiles, cot)
+
+
+def call_backward(grad, tiles, pairs, degree, w_self, w_neigh):
+    nblocks, _, rows, _ = tiles.shape
+    width = w_self.shape[0]
+    dom = lax.axis_size("dom")
+    extra = 2 * width // lax.axis_size("inner") + 8
+    shape = jax.ShapeDtypeStruct
+    return pl.pallas_call(
+        backward_kernel,
+        out_shape=(
+            shape((nblocks, rows, width), F32),
+            shape((2, rows, width), BF16),
+            shape((dom, rows + extra, width), BF16),
+        ),
+        in_specs=[SMEM] + [VMEM] * 4 + [HBM],
+        out_specs=(VMEM,) * 3,
+        scratch_shapes=[
+            pltpu.VMEM(tiles.shape, BF16),
+            pltpu.VMEM((nblocks, rows, rows), F32),
+            pltpu.VMEM((nblocks + 2 + dom, rows, width), F32),
             pltpu.SemaphoreType.DMA((nblocks,)),
         ],
         compiler_params=params(),
         cost_estimate=pl.CostEstimate(
-            flops=4 * 10**9, bytes_accessed=8 * 10**6, transcendentals=nblocks * rows * width
-        ),
-    )(pairs, degree, w_self, w_neigh, bias, blocks, left, right, received, tiles, cot)
+            flops=2 * 10**9, bytes_accessed=8 * 10**6, transcendentals=0
+        ),
+    )(pairs, degree, w_self, w_neigh, grad, tiles)
 
 
 def neighbours(low_source, high_source, axis):
@@ -302,13 +364,15 @@
     outgoing = pl.pallas_call(
         pick_kernel,
         out_shape=jax.ShapeDtypeStruct((dom_size, rows, width), BF16),
-        in_specs=[SMEM, VMEM],
+        in_specs=[SMEM, HBM],
         out_specs=VMEM,
-        compiler_params=params(),
+        scratch_shapes=[pltpu.SemaphoreType.DMA((dom_size,))],
+        compiler_params=params(58),
     )(send_blocks, blocks)
     received = lax.all_to_all(outgoing, "dom", split_axis=0, concat_axis=0, tiled=True)
     left, right = neighbours(blocks[nblocks - 1], blocks[0], "inner")
-    layer_out, own, rims, slots, grads, gbias = call_layer(
+    degree = in_degree.reshape(nblocks, rows)
+    layer_out, grad_pre, grads, gbias = call_forward(
         blocks,
         left,
         right,
@@ -316,14 +380,16 @@
         tiles,
         cotangent.reshape(nblocks, rows, width),
         pair_source,
-        in_degree.reshape(nblocks, rows),
+        degree,
         w_self,
         w_neigh,
         bias[None, :],
     )
+    own, rims, slots = call_backward(grad_pre, tiles, pair_source, degree, w_self, w_neigh)
     merged = merge_grads(grads, gbias, slots)
     returned = lax.all_to_all(merged, "dom", split_axis=0, concat_axis=0, tiled=True)
     low, high = neighbours(rims[1], rims[0], "inner")
+    extra, low, high = lax.optimization_barrier((returned[:, rows:], low, high))
     grad_features = pl.pallas_call(
         combine_kernel,
         out_shape=jax.ShapeDtypeStruct(blocks.shape, BF16),
@@ -336,7 +402,7 @@
         ),
     )(send_blocks, own, returned, low, high)
     scale = 1.0 / math.sqrt(rows_dev * dom_size * lax.axis_size("inner"))
-    sum_self, sum_neigh, sum_bias = spread_grads(returned[:, rows:], scale)
+    sum_self, sum_neigh, sum_bias = spread_grads(extra, scale)
     return (
         layer_out.reshape(rows_dev, width),
         grad_features.reshape(rows_dev, width),

time: 150 us -> 149 us (level)
  blocking collectives: 26.1 us -> 0 us
  starting transfers between devices: 41.7 us -> 57.1 us
  Pallas kernels: 13.3 us -> 19.8 us
  waiting for transfers between devices: 63.1 us -> 65.1 us
    all_to_all x1 -> x0, blocking collectives: 26.1 us -> none  [merge_grads(): lax.all_to_all(chunks, 'inner', split_axis=0, concat_axis=0, tiled=True)]
    all_to_all x0 -> x1, starting transfers between devices: none -> 14.3 us  [merge_grads(): lax.all_to_all(chunks, 'inner', split_axis=0, concat_axis=0, tiled=True)]
    all_to_all x1, waiting for transfers between devices: 1.91 us -> 13 us  [spread_grads(): lax.all_to_all(spread, 'inner', split_axis=0, concat_axis=0, tiled=True)]
    all_to_all x1, waiting for transfers between devices: 33 us -> 27.5 us  [per_device(): lax.all_to_all(merged, 'dom', split_axis=0, concat_axis=0, tiled=True)]
    pallas_call x1 -> x2, Pallas kernels: 8.56 us -> 13.7 us  [the longest x1 7.8 us: call_forward(): pl.pallas_call(forward_kernel, out_shape=(shape(blocks.shape, BF16), shap...]
    all_to_all x0 -> x1, waiting for transfers between devices: none -> 3.38 us  [merge_grads(): lax.all_to_all(chunks, 'inner', split_axis=0, concat_axis=0, tiled=True)]
    ppermute x2, waiting for transfers between devices: 7 us -> 3.93 us  [neighbours(): lax.ppermute(high_source, axis, backward)]
    ppermute x2, waiting for transfers between devices: 2.75 us -> 0.01 us  [neighbours(): lax.ppermute(low_source, axis, forward)]
  transfers between devices with their start and end apart: 7 -> 8, of which waited for: 6 -> 5; matrix products, arithmetic and copies ran while one was open for 0% -> 1% of each run, Pallas kernels for 1% -> 5%
where the time goes in v4:
time: 149 us; the launch traced here: 148 us
  waiting for transfers between devices  65.1 us (44%)
  starting transfers between devices  57.1 us (38%)
  Pallas kernels  19.8 us (13%)
  local copies, waits for them, and re-layouts  5.32 us (4%)
    all_to_all x1, waiting for transfers between devices, per_device(): lax.all_to_all(merged, 'dom', split_axis=0, concat_axis=0, tiled=True)  27.5 us
    all_to_all x1, waiting for transfers between devices, per_device(): lax.all_to_all(outgoing, 'dom', split_axis=0, concat_axis=0, tiled=True)  17.3 us
    all_to_all x1, starting transfers between devices, per_device(): lax.all_to_all(outgoing, 'dom', split_axis=0, concat_axis=0, tiled=True)  15.7 us
    all_to_all x1, starting transfers between devices, merge_grads(): lax.all_to_all(chunks, 'inner', split_axis=0, concat_axis=0, tiled=True)  14.3 us
    all_to_all x1, waiting for transfers between devices, spread_grads(): lax.all_to_all(spread, 'inner', split_axis=0, concat_axis=0, tiled=True)  13 us
    all_to_all x1, starting transfers between devices, spread_grads(): lax.all_to_all(spread, 'inner', split_axis=0, concat_axis=0, tiled=True)  11.5 us
    pallas_call x1, Pallas kernels, call_forward(): pl.pallas_call(forward_kernel, out_shape=(shape(blocks.shape, BF16), shap...  7.8 us
    ppermute x2, starting transfers between devices, neighbours(): lax.ppermute(low_source, axis, forward)  7.62 us
  transfers between devices with their start and end apart: 8, of which 5 were waited for; matrix products, arithmetic and copies ran while one was open for 1% of the time, Pallas kernels for 5%

profile of v4, /device:TPU:1, one launch (start us, length us, event | category | flops | bytes accessed | tf_op | source)
XLA Modules:
  0.0 148.4 jit_solution(10802728327977086992)
XLA Ops:
  0.6 2.8 %shard_map.128 = bf16[12,128,256]{2,1,0:T(8,128)(2,1)} custom-call(s32[1,12]{1,0:T(1,128)} %send_ref.3, bf16[8,128,256]{2,1,0:T(8,128)(2,1)} %bitcast.15), custom_call_target="tpu_custom_call" | custom-call | tf_op jit(solution)/shard_map/pallas_call | solution.py:364
  3.4 15.7 %all-to-all-start = ((bf16[12,128,256]{2,1,0:T(8,128)(2,1)}), bf16[12,128,256]{2,1,0:T(8,128)(2,1)S(1)}, u32[]{:S(2)}, u32[]{:S(2)}) async-start(bf16[12,128,256]{2,1,0:T(8,128)(2,1)} %shard_map.128), calls=%async_computation | async-start | bytes 1572864 | tf_op jit(solution)/shard_map/all_to_all | solution.py:372
  19.2 0.9 fusion.3
  20.1 4.0 %collective-permute-start = (bf16[128,256]{1,0:T(8,128)(2,1)S(1)}, bf16[128,256]{1,0:T(8,128)(2,1)S(1)}, u32[]{:S(2)}, u32[]{:S(2)}) collective-permute-start(bf16[128,256]{1,0:T(8,128)(2,1)S(1)} %get-tuple-element.32), channel_id=1, source_target_pairs={{0,1},{1,2},{2,3},{3,4},{4,5},{5,6},{6,7},{7,8},{8,9},{9,10},{10,1... | collective-permute-start | bytes 196616 | tf_op jit(solution)/shard_map/ppermute | solution.py:299
  24.1 1.9 %collective-permute-start.1 = (bf16[128,256]{1,0:T(8,128)(2,1)S(1)}, bf16[128,256]{1,0:T(8,128)(2,1)S(1)}, u32[]{:S(2)}, u32[]{:S(2)}) collective-permute-start(bf16[128,256]{1,0:T(8,128)(2,1)S(1)} %get-tuple-element.31), channel_id=1, source_target_pairs={{1,0},{2,1},{3,2},{4,3},{5,4},{6,5},{7,6},{8,7},{9,8},{10,9},{11,1... | collective-permute-start | bytes 196616 | tf_op jit(solution)/shard_map/ppermute | solution.py:299
  26.0 0.0 collective-permute-done.left_hbm
  26.0 0.0 copy-start.9
  26.1 3.9 %collective-permute-done.1.right_hbm = bf16[128,256]{1,0:T(8,128)(2,1)S(1)} collective-permute-done((bf16[128,256]{1,0:T(8,128)(2,1)S(1)}, bf16[128,256]{1,0:T(8,128)(2,1)S(1)}, u32[]{:S(2)}, u32[]{:S(2)}) %collective-permute-start.1) | collective-permute-done | bytes 65568 | tf_op jit(solution)/shard_map/ppermute | solution.py:299
  30.0 0.0 copy-start.10
  30.0 17.3 %all-to-all-done.received_hbm = bf16[12,128,256]{2,1,0:T(8,128)(2,1)S(1)} async-done(((bf16[12,128,256]{2,1,0:T(8,128)(2,1)}), bf16[12,128,256]{2,1,0:T(8,128)(2,1)S(1)}, u32[]{:S(2)}, u32[]{:S(2)}) %all-to-all-start) | async-done | bytes 786464 | tf_op jit(solution)/shard_map/all_to_all | solution.py:372
  47.3 0.0 copy-start.8
  47.3 0.0 copy-done.9
  47.3 0.0 copy-done.10
  47.3 0.9 copy-done.8
  48.2 0.0 copy-start.3
  48.2 0.0 copy-start.4
  48.2 0.0 copy-start.5
  48.2 0.0 copy-start.6
  48.2 7.8 %shard_map.129 = (bf16[8,128,256]{2,1,0:T(8,128)(2,1)}, bf16[1024,256]{1,0:T(8,128)(2,1)}, bf16[512,256]{1,0:T(8,128)(2,1)}, f32[1,256]{1,0:T(1,128)}) custom-call(s32[8,8]{1,0:T(8,128)} %pairs_ref.3, s32[8,128]{1,0:T(8,128)} %bitcast.13, bf16[256,256]{1,0:T(8,128)(2,1)} %w_self_ref.3, bf16[256,256]{1,0:T(8,128)(2,1)} %w_neigh_ref.3, f32[1,256]{1,0:T(1,128)} %bitcast.21, ...), custom_call_target="tpu_custom_call" | custom-call | flops 2000000000 | bytes 6000000 | tf_op jit(solution)/shard_map/pallas_call | solution.py:238
  56.0 14.3 %all-to-all-start.1 = ((bf16[64,8,256]{2,1,0:T(8,128)(2,1)}), bf16[64,8,256]{2,1,0:T(8,128)(2,1)S(1)}, u32[]{:S(2)}, u32[]{:S(2)}) async-start(bf16[64,8,256]{2,1,0:T(8,128)(2,1)} %bitcast.18), calls=%async_computation.1 | async-start | bytes 524288 | tf_op jit(solution)/shard_map/all_to_all | solution.py:306
  70.3 0.0 copy-done.3
  70.3 0.0 copy-done.4
  70.3 0.0 copy-done.5
  70.3 0.0 copy-done.6
  70.3 0.0 copy-start.2
  70.4 1.6 %copy-done.2 = bf16[8,8,128,128]{3,2,1,0:T(8,128)(2,1)S(1)} copy-done((bf16[8,8,128,128]{3,2,1,0:T(8,128)(2,1)S(1)}, bf16[8,8,128,128]{3,2,1,0:T(8,128)(2,1)}, u32[]{:S(2)}) %copy-start.2) | copy-done | bytes 2097176
  71.9 0.0 copy-start.7
  71.9 1.0 copy-done.7
  73.0 0.0 copy-start.1
  73.0 5.9 %shard_map.130 = (f32[8,128,256]{2,1,0:T(8,128)S(1)}, bf16[2,128,256]{2,1,0:T(8,128)(2,1)S(1)}, bf16[12,144,256]{2,1,0:T(8,128)(2,1)}) custom-call(s32[8,8]{1,0:T(8,128)S(1)} %copy-done.5, s32[8,128]{1,0:T(8,128)S(1)} %bitcast.14, bf16[256,256]{1,0:T(8,128)(2,1)S(1)} %copy-done.3, bf16[256,256]{1,0:T(8,128)(2,1)S(1)} %copy-done.4, ...), custom_call_target="tpu_custom_call" | custom-call | flops 2000000000 | bytes 8000000 | tf_op jit(solution)/shard_map/pallas_call | solution.py:273
  78.9 3.4 %all-to-all-done.1.pieces_ref = bf16[64,8,256]{2,1,0:T(8,128)(2,1)S(1)} async-done(((bf16[64,8,256]{2,1,0:T(8,128)(2,1)}), bf16[64,8,256]{2,1,0:T(8,128)(2,1)S(1)}, u32[]{:S(2)}, u32[]{:S(2)}) %all-to-all-start.1) | async-done | bytes 262176 | tf_op jit(solution)/shard_map/all_to_all | solution.py:306
  82.3 0.0 copy-done.1
  82.3 0.9 shard_map.131
  83.2 0.0 copy-start
  83.2 4.2 %all-to-all-start.2 = ((bf16[12,144,256]{2,1,0:T(8,128)(2,1)}), bf16[12,144,256]{2,1,0:T(8,128)(2,1)S(1)}, u32[]{:S(2)}, u32[]{:S(2)}) async-start(bf16[12,144,256]{2,1,0:T(8,128)(2,1)} %shard_map.131), calls=%async_computation.2 | async-start | bytes 1769472 | tf_op jit(solution)/shard_map/all_to_all | solution.py:390
  87.4 3.6 %collective-permute-start.2 = (bf16[128,256]{1,0:T(8,128)(2,1)S(1)}, bf16[128,256]{1,0:T(8,128)(2,1)S(1)}, u32[]{:S(2)}, u32[]{:S(2)}) collective-permute-start(bf16[128,256]{1,0:T(8,128)(2,1)S(1)} %get-tuple-element.34), channel_id=1, source_target_pairs={{0,1},{1,2},{2,3},{3,4},{4,5},{5,6},{6,7},{7,8},{8,9},{9,10},{10,1... | collective-permute-start | bytes 196616 | tf_op jit(solution)/shard_map/ppermute | solution.py:299
  91.0 1.9 %collective-permute-start.3 = (bf16[128,256]{1,0:T(8,128)(2,1)S(1)}, bf16[128,256]{1,0:T(8,128)(2,1)S(1)}, u32[]{:S(2)}, u32[]{:S(2)}) collective-permute-start(bf16[128,256]{1,0:T(8,128)(2,1)S(1)} %get-tuple-element.33), channel_id=1, source_target_pairs={{1,0},{2,1},{3,2},{4,3},{5,4},{6,5},{7,6},{8,7},{9,8},{10,9},{11,1... | collective-permute-start | bytes 196616 | tf_op jit(solution)/shard_map/ppermute | solution.py:299
  92.9 0.1 pad.3.clone
  93.0 27.5 %all-to-all-done.2.returned_ref = bf16[12,144,256]{2,1,0:T(8,128)(2,1)S(1)} async-done(((bf16[12,144,256]{2,1,0:T(8,128)(2,1)}), bf16[12,144,256]{2,1,0:T(8,128)(2,1)S(1)}, u32[]{:S(2)}, u32[]{:S(2)}) %all-to-all-start.2) | async-done | bytes 884768 | tf_op jit(solution)/shard_map/all_to_all | solution.py:390
  120.5 0.0 collective-permute-done.2.low_ref
  120.5 0.0 collective-permute-done.3.high_ref
  120.5 0.1 maximum_maximum_fusion
  120.6 0.8 broadcast_in_dim.14
  121.4 11.5 %all-to-all-start.3 = ((bf16[64,24,128]{2,1,0:T(8,128)(2,1)}), bf16[64,24,128]{2,1,0:T(8,128)(2,1)S(1)}, u32[]{:S(2)}, u32[]{:S(2)}) async-start(bf16[64,24,128]{2,1,0:T(8,128)(2,1)} %broadcast_in_dim.14), calls=%async_computation.3 | async-start | bytes 786432 | tf_op jit(solution)/shard_map/all_to_all | solution.py:332
  133.0 0.0 copy-done
  133.0 1.6 %shard_map.132 = bf16[8,128,256]{2,1,0:T(8,128)(2,1)} custom-call(s32[1,12]{1,0:T(1,128)S(1)} %copy-done, f32[8,128,256]{2,1,0:T(8,128)S(1)} %get-tuple-element.20.own_ref, bf16[12,144,256]{2,1,0:T(8,128)(2,1)S(1)} %all-to-all-done.2.returned_ref, bf16[128,256]{1,0:T(8,128)(2,1)S(1)} %collective-permute-done.2.low_ref, ...), custom_call_target="tpu_custom_call" | custom-call | flops 1000000 | bytes 3000000 | tf_op jit(solution)/shard_map/pallas_call | solution.py:393
  134.6 13.0 %all-to-all-done.3.spread_ref = bf16[64,24,128]{2,1,0:T(8,128)(2,1)S(1)} async-done(((bf16[64,24,128]{2,1,0:T(8,128)(2,1)}), bf16[64,24,128]{2,1,0:T(8,128)(2,1)S(1)}, u32[]{:S(2)}, u32[]{:S(2)}) %all-to-all-start.3) | async-done | bytes 393248 | tf_op jit(solution)/shard_map/all_to_all | solution.py:332
  147.6 0.8 shard_map.133
  (7 shorter events, 0.1 us)
Async XLA Ops:
  3.4 43.9 %all-to-all-start = ((bf16[12,128,256]{2,1,0:T(8,128)(2,1)}), bf16[12,128,256]{2,1,0:T(8,128)(2,1)S(1)}, u32[]{:S(2)}, u32[]{:S(2)}) async-start(bf16[12,128,256]{2,1,0:T(8,128)(2,1)} %shard_map.128), calls=%async_computation | async-start | bytes 1572864 | tf_op jit(solution)/shard_map/all_to_all | solution.py:372
  20.1 6.0 %collective-permute-start = (bf16[128,256]{1,0:T(8,128)(2,1)S(1)}, bf16[128,256]{1,0:T(8,128)(2,1)S(1)}, u32[]{:S(2)}, u32[]{:S(2)}) collective-permute-start(bf16[128,256]{1,0:T(8,128)(2,1)S(1)} %get-tuple-element.32), channel_id=1, source_target_pairs={{0,1},{1,2},{2,3},{3,4},{4,5},{5,6},{6,7},{7,8},{8,9},{9,10},{10,1... | collective-permute-start | bytes 196616 | tf_op jit(solution)/shard_map/ppermute | solution.py:299
  24.1 5.9 %collective-permute-start.1 = (bf16[128,256]{1,0:T(8,128)(2,1)S(1)}, bf16[128,256]{1,0:T(8,128)(2,1)S(1)}, u32[]{:S(2)}, u32[]{:S(2)}) collective-permute-start(bf16[128,256]{1,0:T(8,128)(2,1)S(1)} %get-tuple-element.31), channel_id=1, source_target_pairs={{1,0},{2,1},{3,2},{4,3},{5,4},{6,5},{7,6},{8,7},{9,8},{10,9},{11,1... | collective-permute-start | bytes 196616 | tf_op jit(solution)/shard_map/ppermute | solution.py:299
  26.0 21.3 %copy-start.9 = (bf16[128,256]{1,0:T(8,128)(2,1)}, bf16[128,256]{1,0:T(8,128)(2,1)S(1)}, u32[]{:S(2)}) copy-start(bf16[128,256]{1,0:T(8,128)(2,1)S(1)} %collective-permute-done.left_hbm) | copy-start | bytes 196612
  30.0 17.3 %copy-start.10 = (bf16[128,256]{1,0:T(8,128)(2,1)}, bf16[128,256]{1,0:T(8,128)(2,1)S(1)}, u32[]{:S(2)}) copy-start(bf16[128,256]{1,0:T(8,128)(2,1)S(1)} %collective-permute-done.1.right_hbm) | copy-start | bytes 196612
  47.3 0.9 copy-start.8
  48.2 22.1 %copy-start.3 = (bf16[256,256]{1,0:T(8,128)(2,1)S(1)}, bf16[256,256]{1,0:T(8,128)(2,1)}, u32[]{:S(2)}) copy-start(bf16[256,256]{1,0:T(8,128)(2,1)} %w_self_ref.3) | copy-start | bytes 393220
  48.2 22.1 %copy-start.4 = (bf16[256,256]{1,0:T(8,128)(2,1)S(1)}, bf16[256,256]{1,0:T(8,128)(2,1)}, u32[]{:S(2)}) copy-start(bf16[256,256]{1,0:T(8,128)(2,1)} %w_neigh_ref.3) | copy-start | bytes 393220
  48.2 22.1 %copy-start.5 = (s32[8,8]{1,0:T(8,128)S(1)}, s32[8,8]{1,0:T(8,128)}, u32[]{:S(2)}) copy-start(s32[8,8]{1,0:T(8,128)} %pairs_ref.3) | copy-start | bytes 772
  48.2 22.1 %copy-start.6 = (s32[1024]{0:T(1024)S(1)}, s32[1024]{0:T(1024)}, u32[]{:S(2)}) copy-start(s32[1024]{0:T(1024)} %param.12) | copy-start | bytes 12292
  56.0 26.3 %all-to-all-start.1 = ((bf16[64,8,256]{2,1,0:T(8,128)(2,1)}), bf16[64,8,256]{2,1,0:T(8,128)(2,1)S(1)}, u32[]{:S(2)}, u32[]{:S(2)}) async-start(bf16[64,8,256]{2,1,0:T(8,128)(2,1)} %bitcast.18), calls=%async_computation.1 | async-start | bytes 524288 | tf_op jit(solution)/shard_map/all_to_all | solution.py:306
  70.3 1.6 %copy-start.2 = (bf16[8,8,128,128]{3,2,1,0:T(8,128)(2,1)S(1)}, bf16[8,8,128,128]{3,2,1,0:T(8,128)(2,1)}, u32[]{:S(2)}) copy-start(bf16[8,8,128,128]{3,2,1,0:T(8,128)(2,1)} %tiles_hbm.3) | copy-start | bytes 6291460
  71.9 1.0 copy-start.7
  73.0 9.3 %copy-start.1 = (f32[1,256]{1,0:T(1,128)S(1)}, f32[1,256]{1,0:T(1,128)}, u32[]{:S(2)}) copy-start(f32[1,256]{1,0:T(1,128)} %get-tuple-element.22.gbias_ref) | copy-start | bytes 3076
  83.2 49.8 %copy-start = (s32[1,12]{1,0:T(1,128)S(1)}, s32[1,12]{1,0:T(1,128)}, u32[]{:S(2)}) copy-start(s32[1,12]{1,0:T(1,128)} %send_ref.3) | copy-start | bytes 148
  83.2 37.3 %all-to-all-start.2 = ((bf16[12,144,256]{2,1,0:T(8,128)(2,1)}), bf16[12,144,256]{2,1,0:T(8,128)(2,1)S(1)}, u32[]{:S(2)}, u32[]{:S(2)}) async-start(bf16[12,144,256]{2,1,0:T(8,128)(2,1)} %shard_map.131), calls=%async_computation.2 | async-start | bytes 1769472 | tf_op jit(solution)/shard_map/all_to_all | solution.py:390
  87.4 33.1 %collective-permute-start.2 = (bf16[128,256]{1,0:T(8,128)(2,1)S(1)}, bf16[128,256]{1,0:T(8,128)(2,1)S(1)}, u32[]{:S(2)}, u32[]{:S(2)}) collective-permute-start(bf16[128,256]{1,0:T(8,128)(2,1)S(1)} %get-tuple-element.34), channel_id=1, source_target_pairs={{0,1},{1,2},{2,3},{3,4},{4,5},{5,6},{6,7},{7,8},{8,9},{9,10},{10,1... | collective-permute-start | bytes 196616 | tf_op jit(solution)/shard_map/ppermute | solution.py:299
  91.0 29.5 %collective-permute-start.3 = (bf16[128,256]{1,0:T(8,128)(2,1)S(1)}, bf16[128,256]{1,0:T(8,128)(2,1)S(1)}, u32[]{:S(2)}, u32[]{:S(2)}) collective-permute-start(bf16[128,256]{1,0:T(8,128)(2,1)S(1)} %get-tuple-element.33), channel_id=1, source_target_pairs={{1,0},{2,1},{3,2},{4,3},{5,4},{6,5},{7,6},{8,7},{9,8},{10,9},{11,1... | collective-permute-start | bytes 196616 | tf_op jit(solution)/shard_map/ppermute | solution.py:299
  121.4 26.1 %all-to-all-start.3 = ((bf16[64,24,128]{2,1,0:T(8,128)(2,1)}), bf16[64,24,128]{2,1,0:T(8,128)(2,1)S(1)}, u32[]{:S(2)}, u32[]{:S(2)}) async-start(bf16[64,24,128]{2,1,0:T(8,128)(2,1)} %broadcast_in_dim.14), calls=%async_computation.3 | async-start | bytes 786432 | tf_op jit(solution)/shard_map/all_to_all | solution.py:332

commit v5 on v4

--- a/solution.py
+++ b/solution.py
@@ -34,25 +34,43 @@
         copy.wait()
 
 
-def merge_kernel(pieces_ref, gbias_ref, slots_ref, merged_ref, piece, sems):
-    rows = slots_ref.shape[1] - piece.shape[0]
+def split_bias(bias):
+    high = bias.astype(BF16).astype(F32)
+    return [high, bias - high]
+
+
+def piece_kernel(pieces_ref, gbias_ref, out_ref):
     summed = jnp.sum(pieces_ref[...].astype(F32), axis=0)
-    bias = gbias_ref[...]
-    high = bias.astype(BF16).astype(F32)
-    tail = jnp.concatenate(
-        [high, bias - high, jnp.zeros((6, bias.shape[1]), F32)], axis=0
-    )
-    piece[...] = jnp.concatenate([summed, tail], axis=0).astype(BF16)
-    copies = [
-        pltpu.make_async_copy(
-            piece, merged_ref.at[j, pl.ds(rows, piece.shape[0])], sems.at[j]
-        )
-        for j in range(merged_ref.shape[0])
-    ]
-    for copy in copies:
-        copy.start()
-    for copy in copies:
-        copy.wait()
+    hidden = summed.shape[1]
+    lanes = [summed[:, k : k + LANES] for k in range(0, hidden, LANES)]
+    bias = [gbias_ref[:, k : k + LANES] for k in range(0, hidden, LANES)]
+    tail = split_bias(jnp.concatenate(bias, axis=0))
+    tail.append(jnp.zeros((out_ref.shape[1] // 2 - 2 * len(bias), LANES), F32))
+    piece = jnp.concatenate(lanes + tail, axis=0).astype(BF16)
+    out_ref[...] = jnp.broadcast_to(piece[None], out_ref.shape)
+
+
+def start_kernel(scale, spread_ref, out_ref):
+    rows = out_ref.shape[1]
+    bias_rows = 2
+    summed = jnp.sum(spread_ref[...].astype(F32), axis=0) * scale
+    out_ref[0] = summed[:rows].astype(BF16)
+    tail = summed[rows:]
+    bias = tail[:bias_rows] + tail[bias_rows : 2 * bias_rows]
+    spare = jnp.zeros((rows - 2 * bias_rows, LANES), F32)
+    out_ref[1] = jnp.concatenate(split_bias(bias) + [spare], axis=0).astype(BF16)
+
+
+def double_kernel(shift, place_ref, mine_ref, theirs_ref, out_ref):
+    count = mine_ref.shape[0] - 1
+    bit = lax.bitwise_and(lax.shift_right_logical(place_ref[0], shift), 1)
+    out_ref[pl.ds(bit * count, count)] = mine_ref[:count]
+    out_ref[pl.ds((1 - bit) * count, count)] = theirs_ref[:count]
+    tail = mine_ref[count].astype(F32) + theirs_ref[count].astype(F32)
+    bias_rows = 2
+    bias = tail[:bias_rows] + tail[bias_rows : 2 * bias_rows]
+    spare = jnp.zeros((tail.shape[0] - 2 * bias_rows, LANES), F32)
+    out_ref[2 * count] = jnp.concatenate(split_bias(bias) + [spare], axis=0).astype(BF16)
 
 
 def tile_row(tiles, b):
@@ -79,8 +97,8 @@
     w_neigh_ref,
     bias_ref,
     blocks_hbm,
-    left_hbm,
-    right_hbm,
+    left_ref,
+    right_ref,
     received_hbm,
     tiles_hbm,
     cot_hbm,
@@ -103,24 +121,24 @@
     width = table.shape[2]
     copies = [
         pltpu.make_async_copy(blocks_hbm, table.at[pl.ds(0, nblocks)], sems.at[0]),
-        pltpu.make_async_copy(left_hbm, table.at[nblocks], sems.at[1]),
-        pltpu.make_async_copy(right_hbm, table.at[nblocks + 1], sems.at[2]),
         pltpu.make_async_copy(
-            received_hbm, table.at[pl.ds(nblocks + 2, received_hbm.shape[0])], sems.at[3]
+            received_hbm, table.at[pl.ds(nblocks + 2, received_hbm.shape[0])], sems.at[1]
         ),
     ]
     tile_copies = [
         pltpu.make_async_copy(tiles_hbm.at[b], tiles.at[b], tile_sems.at[b])
         for b in range(nblocks)
     ]
-    cot_copy = pltpu.make_async_copy(cot_hbm, cot, sems.at[4])
-    out_copy = pltpu.make_async_copy(out, out_hbm, sems.at[5])
-    grad_copy = pltpu.make_async_copy(grad_pre, grad_hbm, sems.at[6])
+    cot_copy = pltpu.make_async_copy(cot_hbm, cot, sems.at[2])
+    out_copy = pltpu.make_async_copy(out, out_hbm, sems.at[3])
+    grad_copy = pltpu.make_async_copy(grad_pre, grad_hbm, sems.at[4])
     for copy in copies:
         copy.start()
     for copy in tile_copies:
         copy.start()
     cot_copy.start()
+    table[nblocks] = left_ref[...]
+    table[nblocks + 1] = right_ref[...]
     invert_degree(degree_ref, inverse)
     for copy in copies:
         copy.wait()
@@ -211,10 +229,7 @@
 
     own_ref[...] = entries[:nblocks]
     rims_ref[...] = entries[nblocks : nblocks + 2].astype(BF16)
-    slots_ref[:, :rows, :] = entries[nblocks + 2 :].astype(BF16)
-    slots_ref[:, rows:, :] = jnp.zeros(
-        (slots_ref.shape[0], slots_ref.shape[1] - rows, width), BF16
-    )
+    slots_ref[...] = entries[nblocks + 2 :].astype(BF16)
 
 
 def combine_kernel(send_ref, own_ref, returned_ref, low_ref, high_ref, out_ref, total):
@@ -224,7 +239,7 @@
     total[last] = total[last] + high_ref[...].astype(F32)
     for j in range(returned_ref.shape[0]):
         block = send_ref[0, j]
-        total[block] = total[block] + returned_ref[j, : total.shape[1]].astype(F32)
+        total[block] = total[block] + returned_ref[j].astype(F32)
     out_ref[...] = total[...].astype(BF16)
 
 
@@ -243,7 +258,7 @@
             shape((2 * width, width), BF16),
             shape((1, width), F32),
         ),
-        in_specs=[SMEM] + [VMEM] * 4 + [ANY] * 4 + [HBM] * 2,
+        in_specs=[SMEM] + [VMEM] * 4 + [HBM, VMEM, VMEM, ANY, HBM, HBM],
         out_specs=(ANY, ANY, VMEM, VMEM),
         scratch_shapes=[
             pltpu.VMEM((entries, rows, width), BF16),
@@ -254,7 +269,7 @@
             pltpu.VMEM(blocks.shape, BF16),
             pltpu.VMEM((nblocks * rows, width), BF16),
             pltpu.VMEM((nblocks, rows, rows), F32),
-            pltpu.SemaphoreType.DMA((7,)),
+            pltpu.SemaphoreType.DMA((5,)),
             pltpu.SemaphoreType.DMA((nblocks,)),
         ],
         compiler_params=params(58),
@@ -268,14 +283,13 @@
     nblocks, _, rows, _ = tiles.shape
     width = w_self.shape[0]
     dom = lax.axis_size("dom")
-    extra = 2 * width // lax.axis_size("inner") + 8
     shape = jax.ShapeDtypeStruct
     return pl.pallas_call(
         backward_kernel,
         out_shape=(
             shape((nblocks, rows, width), F32),
             shape((2, rows, width), BF16),
-            shape((dom, rows + extra, width), BF16),
+            shape((dom, rows, width), BF16),
         ),
         in_specs=[SMEM] + [VMEM] * 4 + [HBM],
         out_specs=(VMEM,) * 3,
@@ -299,59 +313,76 @@
     return lax.ppermute(low_source, axis, forward), lax.ppermute(high_source, axis, backward)
 
 
-def merge_grads(grads, gbias, slots):
+def reduce_grads(grads, gbias, scale):
+    dom_size = lax.axis_size("dom")
     inner_size = lax.axis_size("inner")
     hidden = grads.shape[1]
     chunks = grads.reshape(inner_size, grads.shape[0] // inner_size, hidden)
     pieces = lax.all_to_all(chunks, "inner", split_axis=0, concat_axis=0, tiled=True)
+    rows = chunks.shape[1] * chunks.shape[2] // LANES
+    spread = pl.pallas_call(
+        piece_kernel,
+        out_shape=jax.ShapeDtypeStruct((dom_size, 2 * rows, LANES), BF16),
+        in_specs=[VMEM, VMEM],
+        out_specs=VMEM,
+        compiler_params=params(),
+    )(pieces, gbias)
+    spread = lax.all_to_all(spread, "dom", split_axis=0, concat_axis=0, tiled=True)
     return pl.pallas_call(
-        merge_kernel,
-        out_shape=jax.ShapeDtypeStruct(slots.shape, BF16),
-        in_specs=[VMEM, VMEM, ANY],
-        out_specs=ANY,
-        scratch_shapes=[
-            pltpu.VMEM((chunks.shape[1] + 8, hidden), BF16),
-            pltpu.SemaphoreType.DMA((slots.shape[0],)),
-        ],
-        input_output_aliases={2: 0},
+        functools.partial(start_kernel, scale),
+        out_shape=jax.ShapeDtypeStruct((2, rows, LANES), BF16),
+        in_specs=[VMEM],
+        out_specs=VMEM,
         compiler_params=params(),
-    )(pieces, gbias, slots)
-
-
-def spread_grads(extra, scale):
+    )(spread)
+
+
+def gather_grads(state, hidden):
     inner_size = lax.axis_size("inner")
-    hidden = extra.shape[2]
-    rows = extra.shape[1] - 8
-    summed = jnp.sum(extra.astype(F32), axis=0) * scale
-    lanes = [summed[:rows, k : k + LANES] for k in range(0, hidden, LANES)]
-    bias = (summed[rows] + summed[rows + 1]).reshape(-1, LANES)
-    bias_rows = bias.shape[0]
-    spare = jnp.zeros((8 - bias_rows, LANES), F32)
-    piece = jnp.concatenate(lanes + [bias, spare], axis=0).astype(BF16)
-    spread = jnp.broadcast_to(piece[None], (inner_size,) + piece.shape)
-    spread = lax.all_to_all(spread, "inner", split_axis=0, concat_axis=0, tiled=True)
+    shifts = list(reversed(range(inner_size.bit_length() - 1)))
+    index = lax.axis_index("inner").astype(jnp.int32).reshape(1)
+    for shift in shifts:
+        pairs = [(i, i ^ (1 << shift)) for i in range(inner_size)]
+        theirs = lax.ppermute(state, "inner", pairs)
+        count = 2 * (state.shape[0] - 1) + 1
+        state = pl.pallas_call(
+            functools.partial(double_kernel, shift),
+            out_shape=jax.ShapeDtypeStruct((count,) + state.shape[1:], BF16),
+            in_specs=[SMEM, VMEM, VMEM],
+            out_specs=VMEM,
+            compiler_params=params(),
+        )(index, state, theirs)
+    place = []
+    for chunk in range(inner_size):
+        place.append(sum(((chunk >> shift) % 2) << k for k, shift in enumerate(shifts)))
     return pl.pallas_call(
-        functools.partial(unpack_kernel, rows, bias_rows),
+        functools.partial(unpack_kernel, place),
         out_shape=(
             jax.ShapeDtypeStruct((hidden, hidden), F32),
             jax.ShapeDtypeStruct((hidden, hidden), F32),
-            jax.ShapeDtypeStruct((bias_rows, LANES), F32),
+            jax.ShapeDtypeStruct((2, LANES), F32),
         ),
         in_specs=[VMEM],
         out_specs=(VMEM,) * 3,
         compiler_params=params(),
-    )(spread)
-
-
-def unpack_kernel(rows, bias_rows, spread_ref, self_ref, neigh_ref, bias_ref):
-    spread = spread_ref[...].astype(F32)
-    half = spread.shape[0] // 2
-    for k in range(bias_rows):
-        part = spread[:, k * rows : (k + 1) * rows]
-        for ref, first in ((self_ref, 0), (neigh_ref, half)):
-            ref[:, k * LANES : (k + 1) * LANES] = part[first : first + half].reshape(-1, LANES)
-    tail = jnp.sum(spread[:, bias_rows * rows :], axis=0)
-    bias_ref[...] = tail[:bias_rows]
+    )(state)
+
+
+def unpack_kernel(place, state_ref, self_ref, neigh_ref, bias_ref):
+    hidden = self_ref.shape[1]
+    groups = hidden // LANES
+    rows = state_ref.shape[1] // groups
+    half = len(place) // 2
+    for chunk, where in enumerate(place):
+        ref = self_ref if chunk < half else neigh_ref
+        first = (chunk % half) * rows
+        values = state_ref[where].astype(F32)
+        for k in range(groups):
+            ref[first : first + rows, k * LANES : (k + 1) * LANES] = values[
+                k * rows : (k + 1) * rows
+            ]
+    tail = state_ref[len(place)].astype(F32)
+    bias_ref[...] = tail[:groups] + tail[groups : 2 * groups]
 
 
 def per_device(
@@ -386,10 +417,12 @@
         bias[None, :],
     )
     own, rims, slots = call_backward(grad_pre, tiles, pair_source, degree, w_self, w_neigh)
-    merged = merge_grads(grads, gbias, slots)
-    returned = lax.all_to_all(merged, "dom", split_axis=0, concat_axis=0, tiled=True)
     low, high = neighbours(rims[1], rims[0], "inner")
-    extra, low, high = lax.optimization_barrier((returned[:, rows:], low, high))
+    scale = 1.0 / math.sqrt(rows_dev * dom_size * lax.axis_size("inner"))
+    state = reduce_grads(grads, gbias, scale)
+    state, slots, low, high = lax.optimization_barrier((state, slots, low, high))
+    returned = lax.all_to_all(slots, "dom", split_axis=0, concat_axis=0, tiled=True)
+    sum_self, sum_neigh, sum_bias = gather_grads(state, width)
     grad_features = pl.pallas_call(
         combine_kernel,
         out_shape=jax.ShapeDtypeStruct(blocks.shape, BF16),
@@ -401,8 +434,6 @@
             flops=10**6, bytes_accessed=3 * 10**6, transcendentals=0
         ),
     )(send_blocks, own, returned, low, high)
-    scale = 1.0 / math.sqrt(rows_dev * dom_size * lax.axis_size("inner"))
-    sum_self, sum_neigh, sum_bias = spread_grads(extra, scale)
     return (
         layer_out.reshape(rows_dev, width),
         grad_features.reshape(rows_dev, width),

time: 149 us -> 148 us (level)
  waiting for transfers between devices: 65.1 us -> 43.7 us
  starting transfers between devices: 57.1 us -> 78.2 us
    all_to_all x3, waiting for transfers between devices: 43.8 us -> 8.14 us  [the longest x1 4.75 us: reduce_grads(): lax.all_to_all(spread, 'dom', split_axis=0, concat_axis=0, tiled=True)]
    ppermute x0 -> x6, starting transfers between devices: none -> 24.4 us  [gather_grads(): theirs = lax.ppermute(state, 'inner', pairs)]
    ppermute x0 -> x6, waiting for transfers between devices: none -> 14.3 us  [gather_grads(): theirs = lax.ppermute(state, 'inner', pairs)]
    all_to_all x3, starting transfers between devices: 30 us -> 26.6 us  [the longest x1 14.3 us: reduce_grads(): lax.all_to_all(chunks, 'inner', split_axis=0, concat_axis=0, tiled=True)]
  transfers between devices with their start and end apart: 8 -> 14, of which waited for: 5 -> 10; matrix products, arithmetic and copies ran while one was open for 1% -> 1% of each run, Pallas kernels for 5% -> 5%
where the time goes in v5:
time: 148 us; the launch traced here: 147 us
  starting transfers between devices  78.2 us (53%)
  waiting for transfers between devices  43.7 us (30%)
  Pallas kernels  19.8 us (13%)
  local copies, waits for them, and re-layouts  4.46 us (3%)
    ppermute x6, starting transfers between devices, gather_grads(): theirs = lax.ppermute(state, 'inner', pairs)  24.4 us
    all_to_all x1, waiting for transfers between devices, per_device(): lax.all_to_all(outgoing, 'dom', split_axis=0, concat_axis=0, tiled=True)  17.3 us
    all_to_all x1, starting transfers between devices, per_device(): lax.all_to_all(outgoing, 'dom', split_axis=0, concat_axis=0, tiled=True)  15.7 us
    all_to_all x1, starting transfers between devices, reduce_grads(): lax.all_to_all(chunks, 'inner', split_axis=0, concat_axis=0, tiled=True)  14.3 us
    ppermute x6, waiting for transfers between devices, gather_grads(): theirs = lax.ppermute(state, 'inner', pairs)  14.3 us
    all_to_all x1, starting transfers between devices, per_device(): lax.all_to_all(slots, 'dom', split_axis=0, concat_axis=0, tiled=True)  8.18 us
    pallas_call x1, Pallas kernels, call_forward(): pl.pallas_call(forward_kernel, out_shape=(shape(blocks.shape, BF16), shap...  7.79 us
    ppermute x2, starting transfers between devices, neighbours(): lax.ppermute(low_source, axis, forward)  7.6 us
  transfers between devices with their start and end apart: 14, of which 10 were waited for; matrix products, arithmetic and copies ran while one was open for 1% of the time, Pallas kernels for 5%

profile of v5, /device:TPU:1, one launch (start us, length us, event | category | flops | bytes accessed | tf_op | source)
XLA Modules:
  0.0 147.0 jit_solution(12847693135272971079)
XLA Ops:
  0.6 2.8 %shard_map.128 = bf16[12,128,256]{2,1,0:T(8,128)(2,1)} custom-call(s32[1,12]{1,0:T(1,128)} %send_ref.3, bf16[8,128,256]{2,1,0:T(8,128)(2,1)} %bitcast.15), custom_call_target="tpu_custom_call" | custom-call | tf_op jit(solution)/shard_map/pallas_call | solution.py:395
  3.5 15.7 %all-to-all-start = ((bf16[12,128,256]{2,1,0:T(8,128)(2,1)}), bf16[12,128,256]{2,1,0:T(8,128)(2,1)S(1)}, u32[]{:S(2)}, u32[]{:S(2)}) async-start(bf16[12,128,256]{2,1,0:T(8,128)(2,1)} %shard_map.128), calls=%async_computation | async-start | bytes 1572864 | tf_op jit(solution)/shard_map/all_to_all | solution.py:403
  19.2 0.9 fusion
  20.1 4.0 %collective-permute-start = (bf16[128,256]{1,0:T(8,128)(2,1)S(1)}, bf16[128,256]{1,0:T(8,128)(2,1)S(1)}, u32[]{:S(2)}, u32[]{:S(2)}) collective-permute-start(bf16[128,256]{1,0:T(8,128)(2,1)S(1)} %get-tuple-element.34), channel_id=1, source_target_pairs={{0,1},{1,2},{2,3},{3,4},{4,5},{5,6},{6,7},{7,8},{8,9},{9,10},{10,1... | collective-permute-start | bytes 196616 | tf_op jit(solution)/shard_map/ppermute | solution.py:313
  24.1 1.9 %collective-permute-start.1 = (bf16[128,256]{1,0:T(8,128)(2,1)S(1)}, bf16[128,256]{1,0:T(8,128)(2,1)S(1)}, u32[]{:S(2)}, u32[]{:S(2)}) collective-permute-start(bf16[128,256]{1,0:T(8,128)(2,1)S(1)} %get-tuple-element.33), channel_id=1, source_target_pairs={{1,0},{2,1},{3,2},{4,3},{5,4},{6,5},{7,6},{8,7},{9,8},{10,9},{11,1... | collective-permute-start | bytes 196616 | tf_op jit(solution)/shard_map/ppermute | solution.py:313
  26.1 0.0 collective-permute-done.left_ref
  26.1 0.0 copy-start.9
  26.1 3.9 %collective-permute-done.1.right_ref = bf16[128,256]{1,0:T(8,128)(2,1)S(1)} collective-permute-done((bf16[128,256]{1,0:T(8,128)(2,1)S(1)}, bf16[128,256]{1,0:T(8,128)(2,1)S(1)}, u32[]{:S(2)}, u32[]{:S(2)}) %collective-permute-start.1) | collective-permute-done | bytes 65568 | tf_op jit(solution)/shard_map/ppermute | solution.py:313
  30.0 0.0 copy-start.10
  30.0 17.3 %all-to-all-done.received_hbm = bf16[12,128,256]{2,1,0:T(8,128)(2,1)S(1)} async-done(((bf16[12,128,256]{2,1,0:T(8,128)(2,1)}), bf16[12,128,256]{2,1,0:T(8,128)(2,1)S(1)}, u32[]{:S(2)}, u32[]{:S(2)}) %all-to-all-start) | async-done | bytes 786464 | tf_op jit(solution)/shard_map/all_to_all | solution.py:403
  47.3 0.0 copy-start.8
  47.3 0.0 copy-done.9
  47.3 0.0 copy-done.10
  47.4 0.9 copy-done.8
  48.2 0.0 copy-start.3
  48.3 0.0 copy-start.4
  48.3 0.0 copy-start.5
  48.3 0.0 copy-start.6
  48.3 7.8 %shard_map.129 = (bf16[8,128,256]{2,1,0:T(8,128)(2,1)}, bf16[1024,256]{1,0:T(8,128)(2,1)}, bf16[512,256]{1,0:T(8,128)(2,1)}, f32[1,256]{1,0:T(1,128)}) custom-call(s32[8,8]{1,0:T(8,128)} %pairs_ref.3, s32[8,128]{1,0:T(8,128)} %bitcast.13, bf16[256,256]{1,0:T(8,128)(2,1)} %w_self_ref.3, bf16[256,256]{1,0:T(8,128)(2,1)} %w_neigh_ref.3, f32[1,256]{1,0:T(1,128)} %bitcast.20, ...), custom_call_target="tpu_custom_call" | custom-call | flops 2000000000 | bytes 6000000 | tf_op jit(solution)/shard_map/pallas_call | solution.py:253
  56.1 14.3 %all-to-all-start.1 = ((bf16[64,8,256]{2,1,0:T(8,128)(2,1)}), bf16[64,8,256]{2,1,0:T(8,128)(2,1)S(1)}, u32[]{:S(2)}, u32[]{:S(2)}) async-start(bf16[64,8,256]{2,1,0:T(8,128)(2,1)} %bitcast.18), calls=%async_computation.1 | async-start | bytes 524288 | tf_op jit(solution)/shard_map/all_to_all | solution.py:321
  70.3 0.0 copy-done.3
  70.3 0.0 copy-done.4
  70.4 0.0 copy-done.5
  70.4 0.0 copy-done.6
  70.4 0.0 copy-start.2
  70.4 1.6 %copy-done.2 = bf16[8,8,128,128]{3,2,1,0:T(8,128)(2,1)S(1)} copy-done((bf16[8,8,128,128]{3,2,1,0:T(8,128)(2,1)S(1)}, bf16[8,8,128,128]{3,2,1,0:T(8,128)(2,1)}, u32[]{:S(2)}) %copy-start.2) | copy-done | bytes 2097176
  72.0 0.0 copy-start.7
  72.0 1.0 copy-done.7
  73.0 0.0 copy-start.1
  73.0 5.9 %shard_map.130 = (f32[8,128,256]{2,1,0:T(8,128)S(1)}, bf16[2,128,256]{2,1,0:T(8,128)(2,1)S(1)}, bf16[12,128,256]{2,1,0:T(8,128)(2,1)}) custom-call(s32[8,8]{1,0:T(8,128)S(1)} %copy-done.5, s32[8,128]{1,0:T(8,128)S(1)} %bitcast.14, bf16[256,256]{1,0:T(8,128)(2,1)S(1)} %copy-done.3, bf16[256,256]{1,0:T(8,128)(2,1)S(1)} %copy-done.4, ...), custom_call_target="tpu_custom_call" | custom-call | flops 2000000000 | bytes 8000000 | tf_op jit(solution)/shard_map/pallas_call | solution.py:287
  78.9 0.0 copy-start
  78.9 3.4 %all-to-all-done.1.pieces_ref = bf16[64,8,256]{2,1,0:T(8,128)(2,1)S(1)} async-done(((bf16[64,8,256]{2,1,0:T(8,128)(2,1)}), bf16[64,8,256]{2,1,0:T(8,128)(2,1)S(1)}, u32[]{:S(2)}, u32[]{:S(2)}) %all-to-all-start.1) | async-done | bytes 262176 | tf_op jit(solution)/shard_map/all_to_all | solution.py:321
  82.3 0.0 copy-done.1
  82.3 0.7 shard_map.131
  83.1 4.2 %all-to-all-start.2 = ((bf16[12,32,128]{2,1,0:T(8,128)(2,1)}), bf16[12,32,128]{2,1,0:T(8,128)(2,1)S(1)}, u32[]{:S(2)}, u32[]{:S(2)}) async-start(bf16[12,32,128]{2,1,0:T(8,128)(2,1)} %shard_map.131), calls=%async_computation.2 | async-start | bytes 196608 | tf_op jit(solution)/shard_map/all_to_all | solution.py:330
  87.2 3.6 %collective-permute-start.2 = (bf16[128,256]{1,0:T(8,128)(2,1)S(1)}, bf16[128,256]{1,0:T(8,128)(2,1)S(1)}, u32[]{:S(2)}, u32[]{:S(2)}) collective-permute-start(bf16[128,256]{1,0:T(8,128)(2,1)S(1)} %get-tuple-element.36), channel_id=1, source_target_pairs={{0,1},{1,2},{2,3},{3,4},{4,5},{5,6},{6,7},{7,8},{8,9},{9,10},{10,1... | collective-permute-start | bytes 196616 | tf_op jit(solution)/shard_map/ppermute | solution.py:313
  90.8 1.9 %collective-permute-start.3 = (bf16[128,256]{1,0:T(8,128)(2,1)S(1)}, bf16[128,256]{1,0:T(8,128)(2,1)S(1)}, u32[]{:S(2)}, u32[]{:S(2)}) collective-permute-start(bf16[128,256]{1,0:T(8,128)(2,1)S(1)} %get-tuple-element.35), channel_id=1, source_target_pairs={{1,0},{2,1},{3,2},{4,3},{5,4},{6,5},{7,6},{8,7},{9,8},{10,9},{11,1... | collective-permute-start | bytes 196616 | tf_op jit(solution)/shard_map/ppermute | solution.py:313
  92.8 4.7 %all-to-all-done.2.spread_ref = bf16[12,32,128]{2,1,0:T(8,128)(2,1)S(1)} async-done(((bf16[12,32,128]{2,1,0:T(8,128)(2,1)}), bf16[12,32,128]{2,1,0:T(8,128)(2,1)S(1)}, u32[]{:S(2)}, u32[]{:S(2)}) %all-to-all-start.2) | async-done | bytes 98336 | tf_op jit(solution)/shard_map/all_to_all | solution.py:330
  97.5 0.0 collective-permute-done.2.low_ref
  97.5 0.0 collective-permute-done.3.high_ref
  97.6 8.2 %all-to-all-start.3 = ((bf16[12,128,256]{2,1,0:T(8,128)(2,1)}), bf16[12,128,256]{2,1,0:T(8,128)(2,1)S(1)}, u32[]{:S(2)}, u32[]{:S(2)}) async-start(bf16[12,128,256]{2,1,0:T(8,128)(2,1)} %get-tuple-element.26), calls=%async_computation.3 | async-start | bytes 1572864 | tf_op jit(solution)/shard_map/all_to_all | solution.py:424
  105.7 4.0 %collective-permute-start.4 = (bf16[2,16,128]{2,1,0:T(8,128)(2,1)S(1)}, bf16[2,16,128]{2,1,0:T(8,128)(2,1)S(1)}, u32[]{:S(2)}, u32[]{:S(2)}) collective-permute-start(bf16[2,16,128]{2,1,0:T(8,128)(2,1)S(1)} %shard_map.132.mine_ref), channel_id=1, source_target_pairs={{0,32},{1,33},{2,34},{3,35},{4,36},{5,37},{6,38},{7,39},{8,40},{9,... | collective-permute-start | bytes 24584 | tf_op jit(solution)/shard_map/ppermute | solution.py:346
  109.8 2.2 %collective-permute-done.4.theirs_ref = bf16[2,16,128]{2,1,0:T(8,128)(2,1)S(1)} collective-permute-done((bf16[2,16,128]{2,1,0:T(8,128)(2,1)S(1)}, bf16[2,16,128]{2,1,0:T(8,128)(2,1)S(1)}, u32[]{:S(2)}, u32[]{:S(2)}) %collective-permute-start.4) | collective-permute-done | bytes 8224 | tf_op jit(solution)/shard_map/ppermute | solution.py:346
  112.0 2.4 %collective-permute-start.5 = (bf16[3,16,128]{2,1,0:T(8,128)(2,1)S(1)}, bf16[3,16,128]{2,1,0:T(8,128)(2,1)S(1)}, u32[]{:S(2)}, u32[]{:S(2)}) collective-permute-start(bf16[3,16,128]{2,1,0:T(8,128)(2,1)S(1)} %shard_map.134.mine_ref), channel_id=1, source_target_pairs={{0,16},{1,17},{2,18},{3,19},{4,20},{5,21},{6,22},{7,23},{8,24},{9,... | collective-permute-start | bytes 36872 | tf_op jit(solution)/shard_map/ppermute | solution.py:346
  114.3 2.0 %collective-permute-done.5.theirs_ref = bf16[3,16,128]{2,1,0:T(8,128)(2,1)S(1)} collective-permute-done((bf16[3,16,128]{2,1,0:T(8,128)(2,1)S(1)}, bf16[3,16,128]{2,1,0:T(8,128)(2,1)S(1)}, u32[]{:S(2)}, u32[]{:S(2)}) %collective-permute-start.5) | collective-permute-done | bytes 12320 | tf_op jit(solution)/shard_map/ppermute | solution.py:346
  116.4 4.2 %collective-permute-start.6 = (bf16[5,16,128]{2,1,0:T(8,128)(2,1)S(1)}, bf16[5,16,128]{2,1,0:T(8,128)(2,1)S(1)}, u32[]{:S(2)}, u32[]{:S(2)}) collective-permute-start(bf16[5,16,128]{2,1,0:T(8,128)(2,1)S(1)} %shard_map.135.mine_ref), channel_id=1, source_target_pairs={{0,8},{1,9},{2,10},{3,11},{4,12},{5,13},{6,14},{7,15},{8,0},{9,1},... | collective-permute-start | bytes 61448 | tf_op jit(solution)/shard_map/ppermute | solution.py:346
  120.6 4.6 %collective-permute-done.6.theirs_ref = bf16[5,16,128]{2,1,0:T(8,128)(2,1)S(1)} collective-permute-done((bf16[5,16,128]{2,1,0:T(8,128)(2,1)S(1)}, bf16[5,16,128]{2,1,0:T(8,128)(2,1)S(1)}, u32[]{:S(2)}, u32[]{:S(2)}) %collective-permute-start.6) | collective-permute-done | bytes 20512 | tf_op jit(solution)/shard_map/ppermute | solution.py:346
  125.1 3.1 %collective-permute-start.7 = (bf16[9,16,128]{2,1,0:T(8,128)(2,1)S(1)}, bf16[9,16,128]{2,1,0:T(8,128)(2,1)S(1)}, u32[]{:S(2)}, u32[]{:S(2)}) collective-permute-start(bf16[9,16,128]{2,1,0:T(8,128)(2,1)S(1)} %shard_map.136.mine_ref), channel_id=1, source_target_pairs={{0,4},{1,5},{2,6},{3,7},{4,0},{5,1},{6,2},{7,3},{8,12},{9,13},{10,... | collective-permute-start | bytes 110600 | tf_op jit(solution)/shard_map/ppermute | solution.py:346
  128.2 2.8 %collective-permute-done.7.theirs_ref = bf16[9,16,128]{2,1,0:T(8,128)(2,1)S(1)} collective-permute-done((bf16[9,16,128]{2,1,0:T(8,128)(2,1)S(1)}, bf16[9,16,128]{2,1,0:T(8,128)(2,1)S(1)}, u32[]{:S(2)}, u32[]{:S(2)}) %collective-permute-start.7) | collective-permute-done | bytes 36896 | tf_op jit(solution)/shard_map/ppermute | solution.py:346
  131.1 3.4 %collective-permute-start.8 = (bf16[17,16,128]{2,1,0:T(8,128)(2,1)S(1)}, bf16[17,16,128]{2,1,0:T(8,128)(2,1)S(1)}, u32[]{:S(2)}, u32[]{:S(2)}) collective-permute-start(bf16[17,16,128]{2,1,0:T(8,128)(2,1)S(1)} %shard_map.137.mine_ref), channel_id=1, source_target_pairs={{0,2},{1,3},{2,0},{3,1},{4,6},{5,7},{6,4},{7,5},{8,10},{9,11},{10,... | collective-permute-start | bytes 208904 | tf_op jit(solution)/shard_map/ppermute | solution.py:346
  134.4 1.7 %collective-permute-done.8.theirs_ref = bf16[17,16,128]{2,1,0:T(8,128)(2,1)S(1)} collective-permute-done((bf16[17,16,128]{2,1,0:T(8,128)(2,1)S(1)}, bf16[17,16,128]{2,1,0:T(8,128)(2,1)S(1)}, u32[]{:S(2)}, u32[]{:S(2)}) %collective-permute-start.8) | collective-permute-done | bytes 69664 | tf_op jit(solution)/shard_map/ppermute | solution.py:346
  136.1 7.4 %collective-permute-start.9 = (bf16[33,16,128]{2,1,0:T(8,128)(2,1)S(1)}, bf16[33,16,128]{2,1,0:T(8,128)(2,1)S(1)}, u32[]{:S(2)}, u32[]{:S(2)}) collective-permute-start(bf16[33,16,128]{2,1,0:T(8,128)(2,1)S(1)} %shard_map.138.mine_ref), channel_id=1, source_target_pairs={{0,1},{1,0},{2,3},{3,2},{4,5},{5,4},{6,7},{7,6},{8,9},{9,8},{10,11... | collective-permute-start | bytes 405512 | tf_op jit(solution)/shard_map/ppermute | solution.py:346
  143.6 1.0 collective-permute-done.9.theirs_ref
  144.6 0.8 shard_map.140
  145.4 0.0 all-to-all-done.3.returned_ref
  145.4 0.0 copy-done
  145.4 1.6 %shard_map.133 = bf16[8,128,256]{2,1,0:T(8,128)(2,1)} custom-call(s32[1,12]{1,0:T(1,128)S(1)} %copy-done, f32[8,128,256]{2,1,0:T(8,128)S(1)} %get-tuple-element.21.own_ref, bf16[12,128,256]{2,1,0:T(8,128)(2,1)S(1)} %all-to-all-done.3.returned_ref, bf16[128,256]{1,0:T(8,128)(2,1)S(1)} %collective-permute-done.2.low_ref, ...), custom_call_target="tpu_custom_call" | custom-call | flops 1000000 | bytes 3000000 | tf_op jit(solution)/shard_map/pallas_call | solution.py:426
  (8 shorter events, 0.1 us)
Async XLA Ops:
  3.5 43.9 %all-to-all-start = ((bf16[12,128,256]{2,1,0:T(8,128)(2,1)}), bf16[12,128,256]{2,1,0:T(8,128)(2,1)S(1)}, u32[]{:S(2)}, u32[]{:S(2)}) async-start(bf16[12,128,256]{2,1,0:T(8,128)(2,1)} %shard_map.128), calls=%async_computation | async-start | bytes 1572864 | tf_op jit(solution)/shard_map/all_to_all | solution.py:403
  20.1 6.0 %collective-permute-start = (bf16[128,256]{1,0:T(8,128)(2,1)S(1)}, bf16[128,256]{1,0:T(8,128)(2,1)S(1)}, u32[]{:S(2)}, u32[]{:S(2)}) collective-permute-start(bf16[128,256]{1,0:T(8,128)(2,1)S(1)} %get-tuple-element.34), channel_id=1, source_target_pairs={{0,1},{1,2},{2,3},{3,4},{4,5},{5,6},{6,7},{7,8},{8,9},{9,10},{10,1... | collective-permute-start | bytes 196616 | tf_op jit(solution)/shard_map/ppermute | solution.py:313
  24.1 5.9 %collective-permute-start.1 = (bf16[128,256]{1,0:T(8,128)(2,1)S(1)}, bf16[128,256]{1,0:T(8,128)(2,1)S(1)}, u32[]{:S(2)}, u32[]{:S(2)}) collective-permute-start(bf16[128,256]{1,0:T(8,128)(2,1)S(1)} %get-tuple-element.33), channel_id=1, source_target_pairs={{1,0},{2,1},{3,2},{4,3},{5,4},{6,5},{7,6},{8,7},{9,8},{10,9},{11,1... | collective-permute-start | bytes 196616 | tf_op jit(solution)/shard_map/ppermute | solution.py:313
  26.1 21.3 %copy-start.9 = (bf16[128,256]{1,0:T(8,128)(2,1)}, bf16[128,256]{1,0:T(8,128)(2,1)S(1)}, u32[]{:S(2)}) copy-start(bf16[128,256]{1,0:T(8,128)(2,1)S(1)} %collective-permute-done.left_ref) | copy-start | bytes 196612
  30.0 17.3 %copy-start.10 = (bf16[128,256]{1,0:T(8,128)(2,1)}, bf16[128,256]{1,0:T(8,128)(2,1)S(1)}, u32[]{:S(2)}) copy-start(bf16[128,256]{1,0:T(8,128)(2,1)S(1)} %collective-permute-done.1.right_ref) | copy-start | bytes 196612
  47.3 0.9 copy-start.8
  48.2 22.1 %copy-start.3 = (bf16[256,256]{1,0:T(8,128)(2,1)S(1)}, bf16[256,256]{1,0:T(8,128)(2,1)}, u32[]{:S(2)}) copy-start(bf16[256,256]{1,0:T(8,128)(2,1)} %w_self_ref.3) | copy-start | bytes 393220
  48.3 22.1 %copy-start.4 = (bf16[256,256]{1,0:T(8,128)(2,1)S(1)}, bf16[256,256]{1,0:T(8,128)(2,1)}, u32[]{:S(2)}) copy-start(bf16[256,256]{1,0:T(8,128)(2,1)} %w_neigh_ref.3) | copy-start | bytes 393220
  48.3 22.1 %copy-start.5 = (s32[8,8]{1,0:T(8,128)S(1)}, s32[8,8]{1,0:T(8,128)}, u32[]{:S(2)}) copy-start(s32[8,8]{1,0:T(8,128)} %pairs_ref.3) | copy-start | bytes 772
  48.3 22.1 %copy-start.6 = (s32[1024]{0:T(1024)S(1)}, s32[1024]{0:T(1024)}, u32[]{:S(2)}) copy-start(s32[1024]{0:T(1024)} %param.12) | copy-start | bytes 12292
  56.1 26.3 %all-to-all-start.1 = ((bf16[64,8,256]{2,1,0:T(8,128)(2,1)}), bf16[64,8,256]{2,1,0:T(8,128)(2,1)S(1)}, u32[]{:S(2)}, u32[]{:S(2)}) async-start(bf16[64,8,256]{2,1,0:T(8,128)(2,1)} %bitcast.18), calls=%async_computation.1 | async-start | bytes 524288 | tf_op jit(solution)/shard_map/all_to_all | solution.py:321
  70.4 1.6 %copy-start.2 = (bf16[8,8,128,128]{3,2,1,0:T(8,128)(2,1)S(1)}, bf16[8,8,128,128]{3,2,1,0:T(8,128)(2,1)}, u32[]{:S(2)}) copy-start(bf16[8,8,128,128]{3,2,1,0:T(8,128)(2,1)} %tiles_hbm.3) | copy-start | bytes 6291460
  72.0 1.0 copy-start.7
  73.0 9.3 %copy-start.1 = (f32[1,256]{1,0:T(1,128)S(1)}, f32[1,256]{1,0:T(1,128)}, u32[]{:S(2)}) copy-start(f32[1,256]{1,0:T(1,128)} %get-tuple-element.23.gbias_ref) | copy-start | bytes 3076
  78.9 66.4 %copy-start = (s32[1,12]{1,0:T(1,128)S(1)}, s32[1,12]{1,0:T(1,128)}, u32[]{:S(2)}) copy-start(s32[1,12]{1,0:T(1,128)} %send_ref.3) | copy-start | bytes 148
  83.1 14.5 %all-to-all-start.2 = ((bf16[12,32,128]{2,1,0:T(8,128)(2,1)}), bf16[12,32,128]{2,1,0:T(8,128)(2,1)S(1)}, u32[]{:S(2)}, u32[]{:S(2)}) async-start(bf16[12,32,128]{2,1,0:T(8,128)(2,1)} %shard_map.131), calls=%async_computation.2 | async-start | bytes 196608 | tf_op jit(solution)/shard_map/all_to_all | solution.py:330
  87.2 10.3 %collective-permute-start.2 = (bf16[128,256]{1,0:T(8,128)(2,1)S(1)}, bf16[128,256]{1,0:T(8,128)(2,1)S(1)}, u32[]{:S(2)}, u32[]{:S(2)}) collective-permute-start(bf16[128,256]{1,0:T(8,128)(2,1)S(1)} %get-tuple-element.36), channel_id=1, source_target_pairs={{0,1},{1,2},{2,3},{3,4},{4,5},{5,6},{6,7},{7,8},{8,9},{9,10},{10,1... | collective-permute-start | bytes 196616 | tf_op jit(solution)/shard_map/ppermute | solution.py:313
  90.8 6.7 %collective-permute-start.3 = (bf16[128,256]{1,0:T(8,128)(2,1)S(1)}, bf16[128,256]{1,0:T(8,128)(2,1)S(1)}, u32[]{:S(2)}, u32[]{:S(2)}) collective-permute-start(bf16[128,256]{1,0:T(8,128)(2,1)S(1)} %get-tuple-element.35), channel_id=1, source_target_pairs={{1,0},{2,1},{3,2},{4,3},{5,4},{6,5},{7,6},{8,7},{9,8},{10,9},{11,1... | collective-permute-start | bytes 196616 | tf_op jit(solution)/shard_map/ppermute | solution.py:313
  97.6 47.8 %all-to-all-start.3 = ((bf16[12,128,256]{2,1,0:T(8,128)(2,1)}), bf16[12,128,256]{2,1,0:T(8,128)(2,1)S(1)}, u32[]{:S(2)}, u32[]{:S(2)}) async-start(bf16[12,128,256]{2,1,0:T(8,128)(2,1)} %get-tuple-element.26), calls=%async_computation.3 | async-start | bytes 1572864 | tf_op jit(solution)/shard_map/all_to_all | solution.py:424
  105.7 6.2 %collective-permute-start.4 = (bf16[2,16,128]{2,1,0:T(8,128)(2,1)S(1)}, bf16[2,16,128]{2,1,0:T(8,128)(2,1)S(1)}, u32[]{:S(2)}, u32[]{:S(2)}) collective-permute-start(bf16[2,16,128]{2,1,0:T(8,128)(2,1)S(1)} %shard_map.132.mine_ref), channel_id=1, source_target_pairs={{0,32},{1,33},{2,34},{3,35},{4,36},{5,37},{6,38},{7,39},{8,40},{9,... | collective-permute-start | bytes 24584 | tf_op jit(solution)/shard_map/ppermute | solution.py:346
  112.0 4.4 %collective-permute-start.5 = (bf16[3,16,128]{2,1,0:T(8,128)(2,1)S(1)}, bf16[3,16,128]{2,1,0:T(8,128)(2,1)S(1)}, u32[]{:S(2)}, u32[]{:S(2)}) collective-permute-start(bf16[3,16,128]{2,1,0:T(8,128)(2,1)S(1)} %shard_map.134.mine_ref), channel_id=1, source_target_pairs={{0,16},{1,17},{2,18},{3,19},{4,20},{5,21},{6,22},{7,23},{8,24},{9,... | collective-permute-start | bytes 36872 | tf_op jit(solution)/shard_map/ppermute | solution.py:346
  116.4 8.7 %collective-permute-start.6 = (bf16[5,16,128]{2,1,0:T(8,128)(2,1)S(1)}, bf16[5,16,128]{2,1,0:T(8,128)(2,1)S(1)}, u32[]{:S(2)}, u32[]{:S(2)}) collective-permute-start(bf16[5,16,128]{2,1,0:T(8,128)(2,1)S(1)} %shard_map.135.mine_ref), channel_id=1, source_target_pairs={{0,8},{1,9},{2,10},{3,11},{4,12},{5,13},{6,14},{7,15},{8,0},{9,1},... | collective-permute-start | bytes 61448 | tf_op jit(solution)/shard_map/ppermute | solution.py:346
  125.1 5.9 %collective-permute-start.7 = (bf16[9,16,128]{2,1,0:T(8,128)(2,1)S(1)}, bf16[9,16,128]{2,1,0:T(8,128)(2,1)S(1)}, u32[]{:S(2)}, u32[]{:S(2)}) collective-permute-start(bf16[9,16,128]{2,1,0:T(8,128)(2,1)S(1)} %shard_map.136.mine_ref), channel_id=1, source_target_pairs={{0,4},{1,5},{2,6},{3,7},{4,0},{5,1},{6,2},{7,3},{8,12},{9,13},{10,... | collective-permute-start | bytes 110600 | tf_op jit(solution)/shard_map/ppermute | solution.py:346
  131.1 5.1 %collective-permute-start.8 = (bf16[17,16,128]{2,1,0:T(8,128)(2,1)S(1)}, bf16[17,16,128]{2,1,0:T(8,128)(2,1)S(1)}, u32[]{:S(2)}, u32[]{:S(2)}) collective-permute-start(bf16[17,16,128]{2,1,0:T(8,128)(2,1)S(1)} %shard_map.137.mine_ref), channel_id=1, source_target_pairs={{0,2},{1,3},{2,0},{3,1},{4,6},{5,7},{6,4},{7,5},{8,10},{9,11},{10,... | collective-permute-start | bytes 208904 | tf_op jit(solution)/shard_map/ppermute | solution.py:346
  136.1 8.4 %collective-permute-start.9 = (bf16[33,16,128]{2,1,0:T(8,128)(2,1)S(1)}, bf16[33,16,128]{2,1,0:T(8,128)(2,1)S(1)}, u32[]{:S(2)}, u32[]{:S(2)}) collective-permute-start(bf16[33,16,128]{2,1,0:T(8,128)(2,1)S(1)} %shard_map.138.mine_ref), channel_id=1, source_target_pairs={{0,1},{1,0},{2,3},{3,2},{4,5},{5,4},{6,7},{7,6},{8,9},{9,8},{10,11... | collective-permute-start | bytes 405512 | tf_op jit(solution)/shard_map/ppermute | solution.py:346

commit v6 on v5

--- a/solution.py
+++ b/solution.py
@@ -61,16 +61,21 @@
     out_ref[1] = jnp.concatenate(split_bias(bias) + [spare], axis=0).astype(BF16)
 
 
-def double_kernel(shift, place_ref, mine_ref, theirs_ref, out_ref):
+def grow_kernel(low, place_ref, mine_ref, *refs):
+    theirs_refs, out_ref = refs[:-1], refs[-1]
     count = mine_ref.shape[0] - 1
-    bit = lax.bitwise_and(lax.shift_right_logical(place_ref[0], shift), 1)
-    out_ref[pl.ds(bit * count, count)] = mine_ref[:count]
-    out_ref[pl.ds((1 - bit) * count, count)] = theirs_ref[:count]
-    tail = mine_ref[count].astype(F32) + theirs_ref[count].astype(F32)
+    value = lax.bitwise_and(lax.shift_right_logical(place_ref[0], low), len(theirs_refs))
+    out_ref[pl.ds(value * count, count)] = mine_ref[:count]
+    tail = mine_ref[count].astype(F32)
+    for mask, theirs_ref in enumerate(theirs_refs, 1):
+        other = lax.bitwise_xor(value, mask)
+        out_ref[pl.ds(other * count, count)] = theirs_ref[:count]
+        tail = tail + theirs_ref[count].astype(F32)
     bias_rows = 2
     bias = tail[:bias_rows] + tail[bias_rows : 2 * bias_rows]
     spare = jnp.zeros((tail.shape[0] - 2 * bias_rows, LANES), F32)
-    out_ref[2 * count] = jnp.concatenate(split_bias(bias) + [spare], axis=0).astype(BF16)
+    last = out_ref.shape[0] - 1
+    out_ref[last] = jnp.concatenate(split_bias(bias) + [spare], axis=0).astype(BF16)
 
 
 def tile_row(tiles, b):
@@ -299,7 +304,7 @@
             pltpu.VMEM((nblocks + 2 + dom, rows, width), F32),
             pltpu.SemaphoreType.DMA((nblocks,)),
         ],
-        compiler_params=params(),
+        compiler_params=params(58),
         cost_estimate=pl.CostEstimate(
             flops=2 * 10**9, bytes_accessed=8 * 10**6, transcendentals=0
         ),
@@ -339,22 +344,26 @@
 
 def gather_grads(state, hidden):
     inner_size = lax.axis_size("inner")
-    shifts = list(reversed(range(inner_size.bit_length() - 1)))
+    bits = inner_size.bit_length() - 1
+    groups = ((3, 1), (4, 2), (1, 2), (0, 1)) if bits == 6 else ((0, bits),)
     index = lax.axis_index("inner").astype(jnp.int32).reshape(1)
-    for shift in shifts:
-        pairs = [(i, i ^ (1 << shift)) for i in range(inner_size)]
-        theirs = lax.ppermute(state, "inner", pairs)
-        count = 2 * (state.shape[0] - 1) + 1
+    place = [0] * inner_size
+    for low, size in groups:
+        count = state.shape[0] - 1
+        theirs = []
+        for mask in range(1, 1 << size):
+            pairs = [(i, i ^ (mask << low)) for i in range(inner_size)]
+            theirs.append(lax.ppermute(state, "inner", pairs))
+        place = [
+            where + ((chunk >> low) % (1 << size)) * count for chunk, where in enumerate(place)
+        ]
         state = pl.pallas_call(
-            functools.partial(double_kernel, shift),
-            out_shape=jax.ShapeDtypeStruct((count,) + state.shape[1:], BF16),
-            in_specs=[SMEM, VMEM, VMEM],
+            functools.partial(grow_kernel, low),
+            out_shape=jax.ShapeDtypeStruct(((count << size) + 1,) + state.shape[1:], BF16),
+            in_specs=[SMEM] + [VMEM] * (1 + len(theirs)),
             out_specs=VMEM,
             compiler_params=params(),
-        )(index, state, theirs)
-    place = []
-    for chunk in range(inner_size):
-        place.append(sum(((chunk >> shift) % 2) << k for k, shift in enumerate(shifts)))
+        )(index, state, *theirs)
     return pl.pallas_call(
         functools.partial(unpack_kernel, place),
         out_shape=(

time: 148 us -> 151 us (1.020)
  starting transfers between devices: 78.2 us -> 83.3 us
  waiting for transfers between devices: 43.7 us -> 41.8 us
  local copies, waits for them, and re-layouts: 4.46 us -> 2.69 us
    ppermute x6 -> x8, starting transfers between devices: 24.4 us -> 28.6 us  [gather_grads(): theirs.append(lax.ppermute(state, 'inner', pairs))]
    unnamed x22 -> x12, local copies, waits for them, and re-layouts: 3.56 us -> 0.93 us
    ppermute x6 -> x8, waiting for transfers between devices: 14.3 us -> 11.8 us  [gather_grads(): theirs.append(lax.ppermute(state, 'inner', pairs))]
  transfers between devices with their start and end apart: 14 -> 16, of which waited for: 10 -> 8; matrix products, arithmetic and copies ran while one was open for 1% -> 1% of each run, Pallas kernels for 5% -> 5%
where the time goes in v6:
time: 151 us; the launch traced here: 150 us
  starting transfers between devices  83.3 us (55%)
  waiting for transfers between devices  41.8 us (28%)
  Pallas kernels  20.9 us (14%)
  local copies, waits for them, and re-layouts  2.69 us (2%)
    ppermute x8, starting transfers between devices, gather_grads(): theirs.append(lax.ppermute(state, 'inner', pairs))  28.6 us
    all_to_all x1, waiting for transfers between devices, per_device(): lax.all_to_all(outgoing, 'dom', split_axis=0, concat_axis=0, tiled=True)  17.3 us
    all_to_all x1, starting transfers between devices, per_device(): lax.all_to_all(outgoing, 'dom', split_axis=0, concat_axis=0, tiled=True)  15.7 us
    all_to_all x1, starting transfers between devices, reduce_grads(): lax.all_to_all(chunks, 'inner', split_axis=0, concat_axis=0, tiled=True)  14.2 us
    ppermute x8, waiting for transfers between devices, gather_grads(): theirs.append(lax.ppermute(state, 'inner', pairs))  11.8 us
    all_to_all x1, starting transfers between devices, per_device(): lax.all_to_all(slots, 'dom', split_axis=0, concat_axis=0, tiled=True)  9.03 us
    pallas_call x1, Pallas kernels, call_forward(): pl.pallas_call(forward_kernel, out_shape=(shape(blocks.shape, BF16), shap...  7.74 us
    ppermute x2, starting transfers between devices, neighbours(): lax.ppermute(low_source, axis, forward)  7.62 us
  transfers between devices with their start and end apart: 16, of which 8 were waited for; matrix products, arithmetic and copies ran while one was open for 1% of the time, Pallas kernels for 5%

profile of v6, /device:TPU:1, one launch (start us, length us, event | category | flops | bytes accessed | tf_op | source)
XLA Modules:
  0.0 149.6 jit_solution(1268223839928474732)
XLA Ops:
  0.6 2.8 %shard_map.128 = bf16[12,128,256]{2,1,0:T(8,128)(2,1)} custom-call(s32[1,12]{1,0:T(1,128)} %send_ref.3, bf16[8,128,256]{2,1,0:T(8,128)(2,1)} %bitcast.13), custom_call_target="tpu_custom_call" | custom-call | tf_op jit(solution)/shard_map/pallas_call | solution.py:404
  3.5 15.7 %all-to-all-start = ((bf16[12,128,256]{2,1,0:T(8,128)(2,1)}), bf16[12,128,256]{2,1,0:T(8,128)(2,1)S(1)}, u32[]{:S(2)}, u32[]{:S(2)}) async-start(bf16[12,128,256]{2,1,0:T(8,128)(2,1)} %shard_map.128), calls=%async_computation | async-start | bytes 1572864 | tf_op jit(solution)/shard_map/all_to_all | solution.py:412
  19.2 0.9 fusion
  20.1 4.0 %collective-permute-start = (bf16[128,256]{1,0:T(8,128)(2,1)S(1)}, bf16[128,256]{1,0:T(8,128)(2,1)S(1)}, u32[]{:S(2)}, u32[]{:S(2)}) collective-permute-start(bf16[128,256]{1,0:T(8,128)(2,1)S(1)} %get-tuple-element.34), channel_id=1, source_target_pairs={{0,1},{1,2},{2,3},{3,4},{4,5},{5,6},{6,7},{7,8},{8,9},{9,10},{10,1... | collective-permute-start | bytes 196616 | tf_op jit(solution)/shard_map/ppermute | solution.py:318
  24.1 1.9 %collective-permute-start.1 = (bf16[128,256]{1,0:T(8,128)(2,1)S(1)}, bf16[128,256]{1,0:T(8,128)(2,1)S(1)}, u32[]{:S(2)}, u32[]{:S(2)}) collective-permute-start(bf16[128,256]{1,0:T(8,128)(2,1)S(1)} %get-tuple-element.33), channel_id=1, source_target_pairs={{1,0},{2,1},{3,2},{4,3},{5,4},{6,5},{7,6},{8,7},{9,8},{10,9},{11,1... | collective-permute-start | bytes 196616 | tf_op jit(solution)/shard_map/ppermute | solution.py:318
  26.1 0.0 collective-permute-done.left_ref
  26.1 0.0 copy-start.4
  26.1 3.9 %collective-permute-done.1.right_ref = bf16[128,256]{1,0:T(8,128)(2,1)S(1)} collective-permute-done((bf16[128,256]{1,0:T(8,128)(2,1)S(1)}, bf16[128,256]{1,0:T(8,128)(2,1)S(1)}, u32[]{:S(2)}, u32[]{:S(2)}) %collective-permute-start.1) | collective-permute-done | bytes 65568 | tf_op jit(solution)/shard_map/ppermute | solution.py:318
  30.0 0.0 copy-start.5
  30.0 17.3 %all-to-all-done.received_hbm = bf16[12,128,256]{2,1,0:T(8,128)(2,1)S(1)} async-done(((bf16[12,128,256]{2,1,0:T(8,128)(2,1)}), bf16[12,128,256]{2,1,0:T(8,128)(2,1)S(1)}, u32[]{:S(2)}, u32[]{:S(2)}) %all-to-all-start) | async-done | bytes 786464 | tf_op jit(solution)/shard_map/all_to_all | solution.py:412
  47.3 0.0 copy-start.3
  47.3 0.0 copy-done.4
  47.3 0.0 copy-done.5
  47.3 0.9 copy-done.3
  48.2 7.7 %shard_map.129 = (bf16[8,128,256]{2,1,0:T(8,128)(2,1)}, bf16[1024,256]{1,0:T(8,128)(2,1)}, bf16[512,256]{1,0:T(8,128)(2,1)}, f32[1,256]{1,0:T(1,128)}) custom-call(s32[8,8]{1,0:T(8,128)} %pairs_ref.3, s32[8,128]{1,0:T(8,128)} %bitcast.18, bf16[256,256]{1,0:T(8,128)(2,1)} %w_self_ref.3, bf16[256,256]{1,0:T(8,128)(2,1)} %w_neigh_ref.3, f32[1,256]{1,0:T(1,128)} %bitcast.20, ...), custom_call_target="tpu_custom_call" | custom-call | flops 2000000000 | bytes 6000000 | tf_op jit(solution)/shard_map/pallas_call | solution.py:258
  56.0 14.2 %all-to-all-start.1 = ((bf16[64,8,256]{2,1,0:T(8,128)(2,1)}), bf16[64,8,256]{2,1,0:T(8,128)(2,1)S(1)}, u32[]{:S(2)}, u32[]{:S(2)}) async-start(bf16[64,8,256]{2,1,0:T(8,128)(2,1)} %bitcast.16), calls=%async_computation.1 | async-start | bytes 524288 | tf_op jit(solution)/shard_map/all_to_all | solution.py:326
  70.1 0.0 copy-start.2
  70.2 7.1 %shard_map.130 = (f32[8,128,256]{2,1,0:T(8,128)}, bf16[2,128,256]{2,1,0:T(8,128)(2,1)}, bf16[12,128,256]{2,1,0:T(8,128)(2,1)}) custom-call(s32[8,8]{1,0:T(8,128)} %pairs_ref.3, s32[8,128]{1,0:T(8,128)} %bitcast.19, bf16[256,256]{1,0:T(8,128)(2,1)} %w_self_ref.3, bf16[256,256]{1,0:T(8,128)(2,1)} %w_neigh_ref.3, bf16[1024,256]{1,0:T(8,128)(2,1)} %get-tuple-element.20.grad_ref, ...), custom_call_target="tpu_custom_call" | custom-call | flops 2000000000 | bytes 8000000 | tf_op jit(solution)/shard_map/pallas_call | solution.py:292
  77.3 0.0 copy-start
  77.3 0.0 copy-start.1
  77.3 4.9 %all-to-all-done.1.pieces_ref = bf16[64,8,256]{2,1,0:T(8,128)(2,1)S(1)} async-done(((bf16[64,8,256]{2,1,0:T(8,128)(2,1)}), bf16[64,8,256]{2,1,0:T(8,128)(2,1)S(1)}, u32[]{:S(2)}, u32[]{:S(2)}) %all-to-all-start.1) | async-done | bytes 262176 | tf_op jit(solution)/shard_map/all_to_all | solution.py:326
  82.1 0.0 copy-done.2
  82.1 0.7 shard_map.131
  82.9 4.4 %all-to-all-start.2 = ((bf16[12,32,128]{2,1,0:T(8,128)(2,1)}), bf16[12,32,128]{2,1,0:T(8,128)(2,1)S(1)}, u32[]{:S(2)}, u32[]{:S(2)}) async-start(bf16[12,32,128]{2,1,0:T(8,128)(2,1)} %shard_map.131), calls=%async_computation.2 | async-start | bytes 196608 | tf_op jit(solution)/shard_map/all_to_all | solution.py:335
  87.2 0.9 slice_bitcast_fusion
  88.1 3.6 %collective-permute-start.2 = (bf16[128,256]{1,0:T(8,128)(2,1)S(1)}, bf16[128,256]{1,0:T(8,128)(2,1)S(1)}, u32[]{:S(2)}, u32[]{:S(2)}) collective-permute-start(bf16[128,256]{1,0:T(8,128)(2,1)S(1)} %get-tuple-element.36), channel_id=1, source_target_pairs={{0,1},{1,2},{2,3},{3,4},{4,5},{5,6},{6,7},{7,8},{8,9},{9,10},{10,1... | collective-permute-start | bytes 196616 | tf_op jit(solution)/shard_map/ppermute | solution.py:318
  91.7 1.9 %collective-permute-start.3 = (bf16[128,256]{1,0:T(8,128)(2,1)S(1)}, bf16[128,256]{1,0:T(8,128)(2,1)S(1)}, u32[]{:S(2)}, u32[]{:S(2)}) collective-permute-start(bf16[128,256]{1,0:T(8,128)(2,1)S(1)} %get-tuple-element.35), channel_id=1, source_target_pairs={{1,0},{2,1},{3,2},{4,3},{5,4},{6,5},{7,6},{8,7},{9,8},{10,9},{11,1... | collective-permute-start | bytes 196616 | tf_op jit(solution)/shard_map/ppermute | solution.py:318
  93.6 3.9 %all-to-all-done.2.spread_ref = bf16[12,32,128]{2,1,0:T(8,128)(2,1)S(1)} async-done(((bf16[12,32,128]{2,1,0:T(8,128)(2,1)}), bf16[12,32,128]{2,1,0:T(8,128)(2,1)S(1)}, u32[]{:S(2)}, u32[]{:S(2)}) %all-to-all-start.2) | async-done | bytes 98336 | tf_op jit(solution)/shard_map/all_to_all | solution.py:335
  97.5 0.0 collective-permute-done.2.low_ref
  97.6 0.0 collective-permute-done.3.high_ref
  97.6 9.0 %all-to-all-start.3 = ((bf16[12,128,256]{2,1,0:T(8,128)(2,1)}), bf16[12,128,256]{2,1,0:T(8,128)(2,1)S(1)}, u32[]{:S(2)}, u32[]{:S(2)}) async-start(bf16[12,128,256]{2,1,0:T(8,128)(2,1)} %get-tuple-element.26), calls=%async_computation.3 | async-start | bytes 1572864 | tf_op jit(solution)/shard_map/all_to_all | solution.py:433
  106.6 4.2 %collective-permute-start.4 = (bf16[2,16,128]{2,1,0:T(8,128)(2,1)S(1)}, bf16[2,16,128]{2,1,0:T(8,128)(2,1)S(1)}, u32[]{:S(2)}, u32[]{:S(2)}) collective-permute-start(bf16[2,16,128]{2,1,0:T(8,128)(2,1)S(1)} %shard_map.132.mine_ref), channel_id=1, source_target_pairs={{0,8},{1,9},{2,10},{3,11},{4,12},{5,13},{6,14},{7,15},{8,0},{9,1},... | collective-permute-start | bytes 24584 | tf_op jit(solution)/shard_map/ppermute | solution.py:356
  110.8 4.4 %collective-permute-done.4.refs_0_ = bf16[2,16,128]{2,1,0:T(8,128)(2,1)S(1)} collective-permute-done((bf16[2,16,128]{2,1,0:T(8,128)(2,1)S(1)}, bf16[2,16,128]{2,1,0:T(8,128)(2,1)S(1)}, u32[]{:S(2)}, u32[]{:S(2)}) %collective-permute-start.4) | collective-permute-done | bytes 8224 | tf_op jit(solution)/shard_map/ppermute | solution.py:356
  115.2 2.4 %collective-permute-start.5 = (bf16[3,16,128]{2,1,0:T(8,128)(2,1)S(1)}, bf16[3,16,128]{2,1,0:T(8,128)(2,1)S(1)}, u32[]{:S(2)}, u32[]{:S(2)}) collective-permute-start(bf16[3,16,128]{2,1,0:T(8,128)(2,1)S(1)} %shard_map.134.mine_ref), channel_id=1, source_target_pairs={{0,16},{1,17},{2,18},{3,19},{4,20},{5,21},{6,22},{7,23},{8,24},{9,... | collective-permute-start | bytes 36872 | tf_op jit(solution)/shard_map/ppermute | solution.py:356
  117.6 4.0 %collective-permute-start.6 = (bf16[3,16,128]{2,1,0:T(8,128)(2,1)S(1)}, bf16[3,16,128]{2,1,0:T(8,128)(2,1)S(1)}, u32[]{:S(2)}, u32[]{:S(2)}) collective-permute-start(bf16[3,16,128]{2,1,0:T(8,128)(2,1)S(1)} %shard_map.134.mine_ref), channel_id=1, source_target_pairs={{0,32},{1,33},{2,34},{3,35},{4,36},{5,37},{6,38},{7,39},{8,40},{9,... | collective-permute-start | bytes 36872 | tf_op jit(solution)/shard_map/ppermute | solution.py:356
  121.7 3.2 %collective-permute-start.7 = (bf16[3,16,128]{2,1,0:T(8,128)(2,1)S(1)}, bf16[3,16,128]{2,1,0:T(8,128)(2,1)S(1)}, u32[]{:S(2)}, u32[]{:S(2)}) collective-permute-start(bf16[3,16,128]{2,1,0:T(8,128)(2,1)S(1)} %shard_map.134.mine_ref), channel_id=1, source_target_pairs={{0,48},{1,49},{2,50},{3,51},{4,52},{5,53},{6,54},{7,55},{8,56},{9,... | collective-permute-start | bytes 36872 | tf_op jit(solution)/shard_map/ppermute | solution.py:356
  124.8 0.0 collective-permute-done.5.refs_0_
  124.8 0.0 collective-permute-done.6.refs_1_
  124.9 2.8 %collective-permute-done.7.refs_2_ = bf16[3,16,128]{2,1,0:T(8,128)(2,1)S(1)} collective-permute-done((bf16[3,16,128]{2,1,0:T(8,128)(2,1)S(1)}, bf16[3,16,128]{2,1,0:T(8,128)(2,1)S(1)}, u32[]{:S(2)}, u32[]{:S(2)}) %collective-permute-start.7) | collective-permute-done | bytes 12320 | tf_op jit(solution)/shard_map/ppermute | solution.py:356
  127.6 2.4 %collective-permute-start.8 = (bf16[9,16,128]{2,1,0:T(8,128)(2,1)S(1)}, bf16[9,16,128]{2,1,0:T(8,128)(2,1)S(1)}, u32[]{:S(2)}, u32[]{:S(2)}) collective-permute-start(bf16[9,16,128]{2,1,0:T(8,128)(2,1)S(1)} %shard_map.135.mine_ref), channel_id=1, source_target_pairs={{0,2},{1,3},{2,0},{3,1},{4,6},{5,7},{6,4},{7,5},{8,10},{9,11},{10,... | collective-permute-start | bytes 110600 | tf_op jit(solution)/shard_map/ppermute | solution.py:356
  130.0 4.0 %collective-permute-start.9 = (bf16[9,16,128]{2,1,0:T(8,128)(2,1)S(1)}, bf16[9,16,128]{2,1,0:T(8,128)(2,1)S(1)}, u32[]{:S(2)}, u32[]{:S(2)}) collective-permute-start(bf16[9,16,128]{2,1,0:T(8,128)(2,1)S(1)} %shard_map.135.mine_ref), channel_id=1, source_target_pairs={{0,4},{1,5},{2,6},{3,7},{4,0},{5,1},{6,2},{7,3},{8,12},{9,13},{10,... | collective-permute-start | bytes 110600 | tf_op jit(solution)/shard_map/ppermute | solution.py:356
  134.1 2.8 %collective-permute-start.10 = (bf16[9,16,128]{2,1,0:T(8,128)(2,1)S(1)}, bf16[9,16,128]{2,1,0:T(8,128)(2,1)S(1)}, u32[]{:S(2)}, u32[]{:S(2)}) collective-permute-start(bf16[9,16,128]{2,1,0:T(8,128)(2,1)S(1)} %shard_map.135.mine_ref), channel_id=1, source_target_pairs={{0,6},{1,7},{2,4},{3,5},{4,2},{5,3},{6,0},{7,1},{8,14},{9,15},{10,... | collective-permute-start | bytes 110600 | tf_op jit(solution)/shard_map/ppermute | solution.py:356
  136.9 0.0 collective-permute-done.8.refs_0_
  136.9 0.0 collective-permute-done.9.refs_1_
  136.9 3.6 %collective-permute-done.10.refs_2_ = bf16[9,16,128]{2,1,0:T(8,128)(2,1)S(1)} collective-permute-done((bf16[9,16,128]{2,1,0:T(8,128)(2,1)S(1)}, bf16[9,16,128]{2,1,0:T(8,128)(2,1)S(1)}, u32[]{:S(2)}, u32[]{:S(2)}) %collective-permute-start.10) | collective-permute-done | bytes 36896 | tf_op jit(solution)/shard_map/ppermute | solution.py:356
  140.6 5.5 %collective-permute-start.11 = (bf16[33,16,128]{2,1,0:T(8,128)(2,1)S(1)}, bf16[33,16,128]{2,1,0:T(8,128)(2,1)S(1)}, u32[]{:S(2)}, u32[]{:S(2)}) collective-permute-start(bf16[33,16,128]{2,1,0:T(8,128)(2,1)S(1)} %shard_map.136.mine_ref), channel_id=1, source_target_pairs={{0,1},{1,0},{2,3},{3,2},{4,5},{5,4},{6,7},{7,6},{8,9},{9,8},{10,11... | collective-permute-start | bytes 405512 | tf_op jit(solution)/shard_map/ppermute | solution.py:356
  146.2 1.0 collective-permute-done.11.refs_0_
  147.2 0.8 shard_map.138
  148.0 0.0 all-to-all-done.3.returned_ref
  148.0 0.0 copy-done
  148.0 0.0 copy-done.1
  148.0 1.6 %shard_map.133 = bf16[8,128,256]{2,1,0:T(8,128)(2,1)} custom-call(s32[1,12]{1,0:T(1,128)S(1)} %copy-done.1, f32[8,128,256]{2,1,0:T(8,128)S(1)} %copy-done, bf16[12,128,256]{2,1,0:T(8,128)(2,1)S(1)} %all-to-all-done.3.returned_ref, bf16[128,256]{1,0:T(8,128)(2,1)S(1)} %collective-permute-done.2.low_ref, bf16[128,256]{1,0:T(8,128)(2,1)S(1)} %collective-permute-done.3.high_ref), custom_call_target="tpu_custom_call" | custom-call | flops 1000000 | bytes 3000000 | tf_op jit(solution)/shard_map/pallas_call | solution.py:435
  (5 shorter events, 0.1 us)
Async XLA Ops:
  3.5 43.8 %all-to-all-start = ((bf16[12,128,256]{2,1,0:T(8,128)(2,1)}), bf16[12,128,256]{2,1,0:T(8,128)(2,1)S(1)}, u32[]{:S(2)}, u32[]{:S(2)}) async-start(bf16[12,128,256]{2,1,0:T(8,128)(2,1)} %shard_map.128), calls=%async_computation | async-start | bytes 1572864 | tf_op jit(solution)/shard_map/all_to_all | solution.py:412
  20.1 6.0 %collective-permute-start = (bf16[128,256]{1,0:T(8,128)(2,1)S(1)}, bf16[128,256]{1,0:T(8,128)(2,1)S(1)}, u32[]{:S(2)}, u32[]{:S(2)}) collective-permute-start(bf16[128,256]{1,0:T(8,128)(2,1)S(1)} %get-tuple-element.34), channel_id=1, source_target_pairs={{0,1},{1,2},{2,3},{3,4},{4,5},{5,6},{6,7},{7,8},{8,9},{9,10},{10,1... | collective-permute-start | bytes 196616 | tf_op jit(solution)/shard_map/ppermute | solution.py:318
  24.1 5.9 %collective-permute-start.1 = (bf16[128,256]{1,0:T(8,128)(2,1)S(1)}, bf16[128,256]{1,0:T(8,128)(2,1)S(1)}, u32[]{:S(2)}, u32[]{:S(2)}) collective-permute-start(bf16[128,256]{1,0:T(8,128)(2,1)S(1)} %get-tuple-element.33), channel_id=1, source_target_pairs={{1,0},{2,1},{3,2},{4,3},{5,4},{6,5},{7,6},{8,7},{9,8},{10,9},{11,1... | collective-permute-start | bytes 196616 | tf_op jit(solution)/shard_map/ppermute | solution.py:318
  26.1 21.2 %copy-start.4 = (bf16[128,256]{1,0:T(8,128)(2,1)}, bf16[128,256]{1,0:T(8,128)(2,1)S(1)}, u32[]{:S(2)}) copy-start(bf16[128,256]{1,0:T(8,128)(2,1)S(1)} %collective-permute-done.left_ref) | copy-start | bytes 196612
  30.0 17.3 %copy-start.5 = (bf16[128,256]{1,0:T(8,128)(2,1)}, bf16[128,256]{1,0:T(8,128)(2,1)S(1)}, u32[]{:S(2)}) copy-start(bf16[128,256]{1,0:T(8,128)(2,1)S(1)} %collective-permute-done.1.right_ref) | copy-start | bytes 196612
  47.3 0.9 copy-start.3
  56.0 26.2 %all-to-all-start.1 = ((bf16[64,8,256]{2,1,0:T(8,128)(2,1)}), bf16[64,8,256]{2,1,0:T(8,128)(2,1)S(1)}, u32[]{:S(2)}, u32[]{:S(2)}) async-start(bf16[64,8,256]{2,1,0:T(8,128)(2,1)} %bitcast.16), calls=%async_computation.1 | async-start | bytes 524288 | tf_op jit(solution)/shard_map/all_to_all | solution.py:326
  70.1 12.0 %copy-start.2 = (f32[1,256]{1,0:T(1,128)S(1)}, f32[1,256]{1,0:T(1,128)}, u32[]{:S(2)}) copy-start(f32[1,256]{1,0:T(1,128)} %get-tuple-element.23.gbias_ref) | copy-start | bytes 3076
  77.3 70.7 %copy-start = (f32[8,128,256]{2,1,0:T(8,128)S(1)}, f32[8,128,256]{2,1,0:T(8,128)}, u32[]{:S(2)}) copy-start(f32[8,128,256]{2,1,0:T(8,128)} %get-tuple-element.21.own_ref) | copy-start | bytes 3145732
  77.3 70.7 %copy-start.1 = (s32[1,12]{1,0:T(1,128)S(1)}, s32[1,12]{1,0:T(1,128)}, u32[]{:S(2)}) copy-start(s32[1,12]{1,0:T(1,128)} %send_ref.3) | copy-start | bytes 148
  82.9 14.7 %all-to-all-start.2 = ((bf16[12,32,128]{2,1,0:T(8,128)(2,1)}), bf16[12,32,128]{2,1,0:T(8,128)(2,1)S(1)}, u32[]{:S(2)}, u32[]{:S(2)}) async-start(bf16[12,32,128]{2,1,0:T(8,128)(2,1)} %shard_map.131), calls=%async_computation.2 | async-start | bytes 196608 | tf_op jit(solution)/shard_map/all_to_all | solution.py:335
  88.1 9.4 %collective-permute-start.2 = (bf16[128,256]{1,0:T(8,128)(2,1)S(1)}, bf16[128,256]{1,0:T(8,128)(2,1)S(1)}, u32[]{:S(2)}, u32[]{:S(2)}) collective-permute-start(bf16[128,256]{1,0:T(8,128)(2,1)S(1)} %get-tuple-element.36), channel_id=1, source_target_pairs={{0,1},{1,2},{2,3},{3,4},{4,5},{5,6},{6,7},{7,8},{8,9},{9,10},{10,1... | collective-permute-start | bytes 196616 | tf_op jit(solution)/shard_map/ppermute | solution.py:318
  91.7 5.9 %collective-permute-start.3 = (bf16[128,256]{1,0:T(8,128)(2,1)S(1)}, bf16[128,256]{1,0:T(8,128)(2,1)S(1)}, u32[]{:S(2)}, u32[]{:S(2)}) collective-permute-start(bf16[128,256]{1,0:T(8,128)(2,1)S(1)} %get-tuple-element.35), channel_id=1, source_target_pairs={{1,0},{2,1},{3,2},{4,3},{5,4},{6,5},{7,6},{8,7},{9,8},{10,9},{11,1... | collective-permute-start | bytes 196616 | tf_op jit(solution)/shard_map/ppermute | solution.py:318
  97.6 50.4 %all-to-all-start.3 = ((bf16[12,128,256]{2,1,0:T(8,128)(2,1)}), bf16[12,128,256]{2,1,0:T(8,128)(2,1)S(1)}, u32[]{:S(2)}, u32[]{:S(2)}) async-start(bf16[12,128,256]{2,1,0:T(8,128)(2,1)} %get-tuple-element.26), calls=%async_computation.3 | async-start | bytes 1572864 | tf_op jit(solution)/shard_map/all_to_all | solution.py:433
  106.6 8.6 %collective-permute-start.4 = (bf16[2,16,128]{2,1,0:T(8,128)(2,1)S(1)}, bf16[2,16,128]{2,1,0:T(8,128)(2,1)S(1)}, u32[]{:S(2)}, u32[]{:S(2)}) collective-permute-start(bf16[2,16,128]{2,1,0:T(8,128)(2,1)S(1)} %shard_map.132.mine_ref), channel_id=1, source_target_pairs={{0,8},{1,9},{2,10},{3,11},{4,12},{5,13},{6,14},{7,15},{8,0},{9,1},... | collective-permute-start | bytes 24584 | tf_op jit(solution)/shard_map/ppermute | solution.py:356
  115.2 9.6 %collective-permute-start.5 = (bf16[3,16,128]{2,1,0:T(8,128)(2,1)S(1)}, bf16[3,16,128]{2,1,0:T(8,128)(2,1)S(1)}, u32[]{:S(2)}, u32[]{:S(2)}) collective-permute-start(bf16[3,16,128]{2,1,0:T(8,128)(2,1)S(1)} %shard_map.134.mine_ref), channel_id=1, source_target_pairs={{0,16},{1,17},{2,18},{3,19},{4,20},{5,21},{6,22},{7,23},{8,24},{9,... | collective-permute-start | bytes 36872 | tf_op jit(solution)/shard_map/ppermute | solution.py:356
  117.6 7.2 %collective-permute-start.6 = (bf16[3,16,128]{2,1,0:T(8,128)(2,1)S(1)}, bf16[3,16,128]{2,1,0:T(8,128)(2,1)S(1)}, u32[]{:S(2)}, u32[]{:S(2)}) collective-permute-start(bf16[3,16,128]{2,1,0:T(8,128)(2,1)S(1)} %shard_map.134.mine_ref), channel_id=1, source_target_pairs={{0,32},{1,33},{2,34},{3,35},{4,36},{5,37},{6,38},{7,39},{8,40},{9,... | collective-permute-start | bytes 36872 | tf_op jit(solution)/shard_map/ppermute | solution.py:356
  121.7 5.9 %collective-permute-start.7 = (bf16[3,16,128]{2,1,0:T(8,128)(2,1)S(1)}, bf16[3,16,128]{2,1,0:T(8,128)(2,1)S(1)}, u32[]{:S(2)}, u32[]{:S(2)}) collective-permute-start(bf16[3,16,128]{2,1,0:T(8,128)(2,1)S(1)} %shard_map.134.mine_ref), channel_id=1, source_target_pairs={{0,48},{1,49},{2,50},{3,51},{4,52},{5,53},{6,54},{7,55},{8,56},{9,... | collective-permute-start | bytes 36872 | tf_op jit(solution)/shard_map/ppermute | solution.py:356
  127.6 9.3 %collective-permute-start.8 = (bf16[9,16,128]{2,1,0:T(8,128)(2,1)S(1)}, bf16[9,16,128]{2,1,0:T(8,128)(2,1)S(1)}, u32[]{:S(2)}, u32[]{:S(2)}) collective-permute-start(bf16[9,16,128]{2,1,0:T(8,128)(2,1)S(1)} %shard_map.135.mine_ref), channel_id=1, source_target_pairs={{0,2},{1,3},{2,0},{3,1},{4,6},{5,7},{6,4},{7,5},{8,10},{9,11},{10,... | collective-permute-start | bytes 110600 | tf_op jit(solution)/shard_map/ppermute | solution.py:356
  130.0 6.9 %collective-permute-start.9 = (bf16[9,16,128]{2,1,0:T(8,128)(2,1)S(1)}, bf16[9,16,128]{2,1,0:T(8,128)(2,1)S(1)}, u32[]{:S(2)}, u32[]{:S(2)}) collective-permute-start(bf16[9,16,128]{2,1,0:T(8,128)(2,1)S(1)} %shard_map.135.mine_ref), channel_id=1, source_target_pairs={{0,4},{1,5},{2,6},{3,7},{4,0},{5,1},{6,2},{7,3},{8,12},{9,13},{10,... | collective-permute-start | bytes 110600 | tf_op jit(solution)/shard_map/ppermute | solution.py:356
  134.1 6.5 %collective-permute-start.10 = (bf16[9,16,128]{2,1,0:T(8,128)(2,1)S(1)}, bf16[9,16,128]{2,1,0:T(8,128)(2,1)S(1)}, u32[]{:S(2)}, u32[]{:S(2)}) collective-permute-start(bf16[9,16,128]{2,1,0:T(8,128)(2,1)S(1)} %shard_map.135.mine_ref), channel_id=1, source_target_pairs={{0,6},{1,7},{2,4},{3,5},{4,2},{5,3},{6,0},{7,1},{8,14},{9,15},{10,... | collective-permute-start | bytes 110600 | tf_op jit(solution)/shard_map/ppermute | solution.py:356
  140.6 6.5 %collective-permute-start.11 = (bf16[33,16,128]{2,1,0:T(8,128)(2,1)S(1)}, bf16[33,16,128]{2,1,0:T(8,128)(2,1)S(1)}, u32[]{:S(2)}, u32[]{:S(2)}) collective-permute-start(bf16[33,16,128]{2,1,0:T(8,128)(2,1)S(1)} %shard_map.136.mine_ref), channel_id=1, source_target_pairs={{0,1},{1,0},{2,3},{3,2},{4,5},{5,4},{6,7},{7,6},{8,9},{9,8},{10,11... | collective-permute-start | bytes 405512 | tf_op jit(solution)/shard_map/ppermute | solution.py:356

commit v7 on v6

--- a/solution.py
+++ b/solution.py
@@ -148,19 +148,19 @@
     for copy in copies:
         copy.wait()
 
-    for b in range(nblocks):
-        for p in range(npairs):
-            sources[b % 2, pl.ds(p * rows, rows), :] = table[pairs_ref[b, p]]
-        tile_copies[b].wait()
-        summed = jnp.dot(tile_row(tiles, b), sources[b % 2], preferred_element_type=F32)
-        mean[b] = by_degree(summed, inverse, b).astype(BF16)
-
     cot_copy.wait()
     w_self = w_self_ref[...]
     w_neigh = w_neigh_ref[...]
     gbias = jnp.zeros((1, width), F32)
-    step = 2
-    for b in range(0, nblocks, step):
+    def aggregate(b):
+        for p in range(npairs):
+            sources[b % 2, pl.ds(p * rows, rows), :] = table[pairs_ref[b, p]]
+        stacked = sources[b % 2]
+        tile_copies[b].wait()
+        summed = jnp.dot(tile_row(tiles, b), stacked, preferred_element_type=F32)
+        mean[b] = by_degree(summed, inverse, b).astype(BF16)
+
+    def activate(b, gbias):
         features = table[b : b + step].reshape(step * rows, width)
         means = mean[b : b + step].reshape(step * rows, width)
         preact = (
@@ -173,7 +173,13 @@
         cots = cot[b : b + step].reshape(step * rows, width).astype(F32)
         grad = (cots * sigma * (1.0 + preact * (1.0 - sigma))).astype(BF16)
         grad_pre[pl.ds(b * rows, step * rows), :] = grad
-        gbias = gbias + jnp.sum(grad.astype(F32), axis=0, keepdims=True)
+        return gbias + jnp.sum(grad.astype(F32), axis=0, keepdims=True)
+
+    step = 2
+    for b in range(nblocks):
+        aggregate(b)
+    for b in range(0, nblocks, step):
+        gbias = activate(b, gbias)
     grad_copy.start()
     out_copy.start()
     gbias_ref[...] = gbias
@@ -263,7 +269,7 @@
             shape((2 * width, width), BF16),
             shape((1, width), F32),
         ),
-        in_specs=[SMEM] + [VMEM] * 4 + [HBM, VMEM, VMEM, ANY, HBM, HBM],
+        in_specs=[SMEM] + [VMEM] * 4 + [HBM, VMEM, VMEM, HBM, HBM, HBM],
         out_specs=(ANY, ANY, VMEM, VMEM),
         scratch_shapes=[
             pltpu.VMEM((entries, rows, width), BF16),
@@ -342,10 +348,10 @@
     )(spread)
 
 
-def gather_grads(state, hidden):
+def gather_grads(state, hidden, beside):
     inner_size = lax.axis_size("inner")
     bits = inner_size.bit_length() - 1
-    groups = ((3, 1), (4, 2), (1, 2), (0, 1)) if bits == 6 else ((0, bits),)
+    groups = [(low, 1) for low in reversed(range(bits))]
     index = lax.axis_index("inner").astype(jnp.int32).reshape(1)
     place = [0] * inner_size
     for low, size in groups:
@@ -354,6 +360,8 @@
         for mask in range(1, 1 << size):
             pairs = [(i, i ^ (mask << low)) for i in range(inner_size)]
             theirs.append(lax.ppermute(state, "inner", pairs))
+        if low == groups[-1][0]:
+            theirs, beside = lax.optimization_barrier((theirs, beside))
         place = [
             where + ((chunk >> low) % (1 << size)) * count for chunk, where in enumerate(place)
         ]
@@ -364,7 +372,7 @@
             out_specs=VMEM,
             compiler_params=params(),
         )(index, state, *theirs)
-    return pl.pallas_call(
+    unpacked = pl.pallas_call(
         functools.partial(unpack_kernel, place),
         out_shape=(
             jax.ShapeDtypeStruct((hidden, hidden), F32),
@@ -375,6 +383,7 @@
         out_specs=(VMEM,) * 3,
         compiler_params=params(),
     )(state)
+    return unpacked, beside
 
 
 def unpack_kernel(place, state_ref, self_ref, neigh_ref, bias_ref):
@@ -431,7 +440,6 @@
     state = reduce_grads(grads, gbias, scale)
     state, slots, low, high = lax.optimization_barrier((state, slots, low, high))
     returned = lax.all_to_all(slots, "dom", split_axis=0, concat_axis=0, tiled=True)
-    sum_self, sum_neigh, sum_bias = gather_grads(state, width)
     grad_features = pl.pallas_call(
         combine_kernel,
         out_shape=jax.ShapeDtypeStruct(blocks.shape, BF16),
@@ -443,6 +451,7 @@
             flops=10**6, bytes_accessed=3 * 10**6, transcendentals=0
         ),
     )(send_blocks, own, returned, low, high)
+    (sum_self, sum_neigh, sum_bias), grad_features = gather_grads(state, width, grad_features)
     return (
         layer_out.reshape(rows_dev, width),
         grad_features.reshape(rows_dev, width),

time: 151 us -> 148 us (0.980)
  starting transfers between devices: 83.3 us -> 79.1 us
    ppermute x8 -> x6, starting transfers between devices: 28.6 us -> 24.4 us  [gather_grads(): theirs.append(lax.ppermute(state, 'inner', pairs))]
    ppermute x8 -> x6, waiting for transfers between devices: 11.8 us -> 13.3 us  [gather_grads(): theirs.append(lax.ppermute(state, 'inner', pairs))]
  transfers between devices with their start and end apart: 16 -> 14, of which waited for: 8 -> 9; matrix products, arithmetic and copies ran while one was open for 1% -> 1% of each run, Pallas kernels for 5% -> 6%
where the time goes in v7:
time: 148 us; the launch traced here: 147 us
  starting transfers between devices  79.1 us (53%)
  waiting for transfers between devices  43.3 us (29%)
  Pallas kernels  20.9 us (14%)
  local copies, waits for them, and re-layouts  2.68 us (2%)
    ppermute x6, starting transfers between devices, gather_grads(): theirs.append(lax.ppermute(state, 'inner', pairs))  24.4 us
    all_to_all x1, waiting for transfers between devices, per_device(): lax.all_to_all(outgoing, 'dom', split_axis=0, concat_axis=0, tiled=True)  17.3 us
    all_to_all x1, starting transfers between devices, per_device(): lax.all_to_all(outgoing, 'dom', split_axis=0, concat_axis=0, tiled=True)  15.7 us
    all_to_all x1, starting transfers between devices, reduce_grads(): lax.all_to_all(chunks, 'inner', split_axis=0, concat_axis=0, tiled=True)  14.3 us
    ppermute x6, waiting for transfers between devices, gather_grads(): theirs.append(lax.ppermute(state, 'inner', pairs))  13.3 us
    all_to_all x1, starting transfers between devices, per_device(): lax.all_to_all(slots, 'dom', split_axis=0, concat_axis=0, tiled=True)  9.03 us
    pallas_call x1, Pallas kernels, call_forward(): pl.pallas_call(forward_kernel, out_shape=(shape(blocks.shape, BF16), shap...  7.75 us
    ppermute x2, starting transfers between devices, neighbours(): lax.ppermute(low_source, axis, forward)  7.62 us
  transfers between devices with their start and end apart: 14, of which 9 were waited for; matrix products, arithmetic and copies ran while one was open for 1% of the time, Pallas kernels for 6%

profile of v7, /device:TPU:1, one launch (start us, length us, event | category | flops | bytes accessed | tf_op | source)
XLA Modules:
  0.0 146.9 jit_solution(4130195042176708724)
XLA Ops:
  0.6 2.8 %shard_map.128 = bf16[12,128,256]{2,1,0:T(8,128)(2,1)} custom-call(s32[1,12]{1,0:T(1,128)} %send_ref.3, bf16[8,128,256]{2,1,0:T(8,128)(2,1)} %bitcast.13), custom_call_target="tpu_custom_call" | custom-call | tf_op jit(solution)/shard_map/pallas_call | solution.py:413
  3.5 15.7 %all-to-all-start = ((bf16[12,128,256]{2,1,0:T(8,128)(2,1)}), bf16[12,128,256]{2,1,0:T(8,128)(2,1)S(1)}, u32[]{:S(2)}, u32[]{:S(2)}) async-start(bf16[12,128,256]{2,1,0:T(8,128)(2,1)} %shard_map.128), calls=%async_computation | async-start | bytes 1572864 | tf_op jit(solution)/shard_map/all_to_all | solution.py:421
  19.2 0.9 fusion
  20.1 4.0 %collective-permute-start = (bf16[128,256]{1,0:T(8,128)(2,1)S(1)}, bf16[128,256]{1,0:T(8,128)(2,1)S(1)}, u32[]{:S(2)}, u32[]{:S(2)}) collective-permute-start(bf16[128,256]{1,0:T(8,128)(2,1)S(1)} %get-tuple-element.38), channel_id=1, source_target_pairs={{0,1},{1,2},{2,3},{3,4},{4,5},{5,6},{6,7},{7,8},{8,9},{9,10},{10,1... | collective-permute-start | bytes 196616 | tf_op jit(solution)/shard_map/ppermute | solution.py:324
  24.1 1.9 %collective-permute-start.1 = (bf16[128,256]{1,0:T(8,128)(2,1)S(1)}, bf16[128,256]{1,0:T(8,128)(2,1)S(1)}, u32[]{:S(2)}, u32[]{:S(2)}) collective-permute-start(bf16[128,256]{1,0:T(8,128)(2,1)S(1)} %get-tuple-element.37), channel_id=1, source_target_pairs={{1,0},{2,1},{3,2},{4,3},{5,4},{6,5},{7,6},{8,7},{9,8},{10,9},{11,1... | collective-permute-start | bytes 196616 | tf_op jit(solution)/shard_map/ppermute | solution.py:324
  26.1 0.0 collective-permute-done.left_ref
  26.1 0.0 copy-start.4
  26.1 3.9 %collective-permute-done.1.right_ref = bf16[128,256]{1,0:T(8,128)(2,1)S(1)} collective-permute-done((bf16[128,256]{1,0:T(8,128)(2,1)S(1)}, bf16[128,256]{1,0:T(8,128)(2,1)S(1)}, u32[]{:S(2)}, u32[]{:S(2)}) %collective-permute-start.1) | collective-permute-done | bytes 65568 | tf_op jit(solution)/shard_map/ppermute | solution.py:324
  30.0 0.0 copy-start.5
  30.0 17.3 %all-to-all-done.received_hbm = bf16[12,128,256]{2,1,0:T(8,128)(2,1)S(1)} async-done(((bf16[12,128,256]{2,1,0:T(8,128)(2,1)}), bf16[12,128,256]{2,1,0:T(8,128)(2,1)S(1)}, u32[]{:S(2)}, u32[]{:S(2)}) %all-to-all-start) | async-done | bytes 786464 | tf_op jit(solution)/shard_map/all_to_all | solution.py:421
  47.3 0.0 copy-start.3
  47.3 0.0 copy-done.4
  47.3 0.0 copy-done.5
  47.3 0.9 copy-done.3
  48.2 7.8 %shard_map.129 = (bf16[8,128,256]{2,1,0:T(8,128)(2,1)}, bf16[1024,256]{1,0:T(8,128)(2,1)}, bf16[512,256]{1,0:T(8,128)(2,1)}, f32[1,256]{1,0:T(1,128)}) custom-call(s32[8,8]{1,0:T(8,128)} %pairs_ref.3, s32[8,128]{1,0:T(8,128)} %bitcast.18, bf16[256,256]{1,0:T(8,128)(2,1)} %w_self_ref.3, bf16[256,256]{1,0:T(8,128)(2,1)} %w_neigh_ref.3, f32[1,256]{1,0:T(1,128)} %bitcast.20, ...), custom_call_target="tpu_custom_call" | custom-call | flops 2000000000 | bytes 6000000 | tf_op jit(solution)/shard_map/pallas_call | solution.py:264
  56.0 14.3 %all-to-all-start.1 = ((bf16[64,8,256]{2,1,0:T(8,128)(2,1)}), bf16[64,8,256]{2,1,0:T(8,128)(2,1)S(1)}, u32[]{:S(2)}, u32[]{:S(2)}) async-start(bf16[64,8,256]{2,1,0:T(8,128)(2,1)} %bitcast.16), calls=%async_computation.1 | async-start | bytes 524288 | tf_op jit(solution)/shard_map/all_to_all | solution.py:332
  70.3 0.0 copy-start.2
  70.3 7.1 %shard_map.132 = (f32[8,128,256]{2,1,0:T(8,128)}, bf16[2,128,256]{2,1,0:T(8,128)(2,1)}, bf16[12,128,256]{2,1,0:T(8,128)(2,1)}) custom-call(s32[8,8]{1,0:T(8,128)} %pairs_ref.3, s32[8,128]{1,0:T(8,128)} %bitcast.19, bf16[256,256]{1,0:T(8,128)(2,1)} %w_self_ref.3, bf16[256,256]{1,0:T(8,128)(2,1)} %w_neigh_ref.3, bf16[1024,256]{1,0:T(8,128)(2,1)} %get-tuple-element.24.grad_ref, ...), custom_call_target="tpu_custom_call" | custom-call | flops 2000000000 | bytes 8000000 | tf_op jit(solution)/shard_map/pallas_call | solution.py:298
  77.4 0.0 copy-start
  77.4 0.0 copy-start.1
  77.4 4.8 %all-to-all-done.1.pieces_ref = bf16[64,8,256]{2,1,0:T(8,128)(2,1)S(1)} async-done(((bf16[64,8,256]{2,1,0:T(8,128)(2,1)}), bf16[64,8,256]{2,1,0:T(8,128)(2,1)S(1)}, u32[]{:S(2)}, u32[]{:S(2)}) %all-to-all-start.1) | async-done | bytes 262176 | tf_op jit(solution)/shard_map/all_to_all | solution.py:332
  82.3 0.0 copy-done.2
  82.3 0.7 shard_map.130
  83.0 4.2 %all-to-all-start.2 = ((bf16[12,32,128]{2,1,0:T(8,128)(2,1)}), bf16[12,32,128]{2,1,0:T(8,128)(2,1)S(1)}, u32[]{:S(2)}, u32[]{:S(2)}) async-start(bf16[12,32,128]{2,1,0:T(8,128)(2,1)} %shard_map.130), calls=%async_computation.2 | async-start | bytes 196608 | tf_op jit(solution)/shard_map/all_to_all | solution.py:341
  87.2 0.9 slice_bitcast_fusion
  88.1 3.6 %collective-permute-start.2 = (bf16[128,256]{1,0:T(8,128)(2,1)S(1)}, bf16[128,256]{1,0:T(8,128)(2,1)S(1)}, u32[]{:S(2)}, u32[]{:S(2)}) collective-permute-start(bf16[128,256]{1,0:T(8,128)(2,1)S(1)} %get-tuple-element.40), channel_id=1, source_target_pairs={{0,1},{1,2},{2,3},{3,4},{4,5},{5,6},{6,7},{7,8},{8,9},{9,10},{10,1... | collective-permute-start | bytes 196616 | tf_op jit(solution)/shard_map/ppermute | solution.py:324
  91.6 1.9 %collective-permute-start.3 = (bf16[128,256]{1,0:T(8,128)(2,1)S(1)}, bf16[128,256]{1,0:T(8,128)(2,1)S(1)}, u32[]{:S(2)}, u32[]{:S(2)}) collective-permute-start(bf16[128,256]{1,0:T(8,128)(2,1)S(1)} %get-tuple-element.39), channel_id=1, source_target_pairs={{1,0},{2,1},{3,2},{4,3},{5,4},{6,5},{7,6},{8,7},{9,8},{10,9},{11,1... | collective-permute-start | bytes 196616 | tf_op jit(solution)/shard_map/ppermute | solution.py:324
  93.6 3.9 %all-to-all-done.2.spread_ref = bf16[12,32,128]{2,1,0:T(8,128)(2,1)S(1)} async-done(((bf16[12,32,128]{2,1,0:T(8,128)(2,1)}), bf16[12,32,128]{2,1,0:T(8,128)(2,1)S(1)}, u32[]{:S(2)}, u32[]{:S(2)}) %all-to-all-start.2) | async-done | bytes 98336 | tf_op jit(solution)/shard_map/all_to_all | solution.py:341
  97.5 0.0 collective-permute-done.2.low_ref
  97.5 0.0 collective-permute-done.3.high_ref
  97.5 9.0 %all-to-all-start.3 = ((bf16[12,128,256]{2,1,0:T(8,128)(2,1)}), bf16[12,128,256]{2,1,0:T(8,128)(2,1)S(1)}, u32[]{:S(2)}, u32[]{:S(2)}) async-start(bf16[12,128,256]{2,1,0:T(8,128)(2,1)} %get-tuple-element.29), calls=%async_computation.3 | async-start | bytes 1572864 | tf_op jit(solution)/shard_map/all_to_all | solution.py:442
  106.6 4.0 %collective-permute-start.4 = (bf16[2,16,128]{2,1,0:T(8,128)(2,1)S(1)}, bf16[2,16,128]{2,1,0:T(8,128)(2,1)S(1)}, u32[]{:S(2)}, u32[]{:S(2)}) collective-permute-start(bf16[2,16,128]{2,1,0:T(8,128)(2,1)S(1)} %shard_map.131.mine_ref), channel_id=1, source_target_pairs={{0,32},{1,33},{2,34},{3,35},{4,36},{5,37},{6,38},{7,39},{8,40},{9,... | collective-permute-start | bytes 24584 | tf_op jit(solution)/shard_map/ppermute | solution.py:362
  110.6 2.2 %collective-permute-done.4.refs_0_ = bf16[2,16,128]{2,1,0:T(8,128)(2,1)S(1)} collective-permute-done((bf16[2,16,128]{2,1,0:T(8,128)(2,1)S(1)}, bf16[2,16,128]{2,1,0:T(8,128)(2,1)S(1)}, u32[]{:S(2)}, u32[]{:S(2)}) %collective-permute-start.4) | collective-permute-done | bytes 8224 | tf_op jit(solution)/shard_map/ppermute | solution.py:362
  112.8 2.4 %collective-permute-start.5 = (bf16[3,16,128]{2,1,0:T(8,128)(2,1)S(1)}, bf16[3,16,128]{2,1,0:T(8,128)(2,1)S(1)}, u32[]{:S(2)}, u32[]{:S(2)}) collective-permute-start(bf16[3,16,128]{2,1,0:T(8,128)(2,1)S(1)} %shard_map.133.mine_ref), channel_id=1, source_target_pairs={{0,16},{1,17},{2,18},{3,19},{4,20},{5,21},{6,22},{7,23},{8,24},{9,... | collective-permute-start | bytes 36872 | tf_op jit(solution)/shard_map/ppermute | solution.py:362
  115.2 2.0 %collective-permute-done.5.refs_0_ = bf16[3,16,128]{2,1,0:T(8,128)(2,1)S(1)} collective-permute-done((bf16[3,16,128]{2,1,0:T(8,128)(2,1)S(1)}, bf16[3,16,128]{2,1,0:T(8,128)(2,1)S(1)}, u32[]{:S(2)}, u32[]{:S(2)}) %collective-permute-start.5) | collective-permute-done | bytes 12320 | tf_op jit(solution)/shard_map/ppermute | solution.py:362
  117.2 4.2 %collective-permute-start.6 = (bf16[5,16,128]{2,1,0:T(8,128)(2,1)S(1)}, bf16[5,16,128]{2,1,0:T(8,128)(2,1)S(1)}, u32[]{:S(2)}, u32[]{:S(2)}) collective-permute-start(bf16[5,16,128]{2,1,0:T(8,128)(2,1)S(1)} %shard_map.134.mine_ref), channel_id=1, source_target_pairs={{0,8},{1,9},{2,10},{3,11},{4,12},{5,13},{6,14},{7,15},{8,0},{9,1},... | collective-permute-start | bytes 61448 | tf_op jit(solution)/shard_map/ppermute | solution.py:362
  121.4 4.6 %collective-permute-done.6.refs_0_ = bf16[5,16,128]{2,1,0:T(8,128)(2,1)S(1)} collective-permute-done((bf16[5,16,128]{2,1,0:T(8,128)(2,1)S(1)}, bf16[5,16,128]{2,1,0:T(8,128)(2,1)S(1)}, u32[]{:S(2)}, u32[]{:S(2)}) %collective-permute-start.6) | collective-permute-done | bytes 20512 | tf_op jit(solution)/shard_map/ppermute | solution.py:362
  126.0 3.1 %collective-permute-start.7 = (bf16[9,16,128]{2,1,0:T(8,128)(2,1)S(1)}, bf16[9,16,128]{2,1,0:T(8,128)(2,1)S(1)}, u32[]{:S(2)}, u32[]{:S(2)}) collective-permute-start(bf16[9,16,128]{2,1,0:T(8,128)(2,1)S(1)} %shard_map.135.mine_ref), channel_id=1, source_target_pairs={{0,4},{1,5},{2,6},{3,7},{4,0},{5,1},{6,2},{7,3},{8,12},{9,13},{10,... | collective-permute-start | bytes 110600 | tf_op jit(solution)/shard_map/ppermute | solution.py:362
  129.0 2.8 %collective-permute-done.7.refs_0_ = bf16[9,16,128]{2,1,0:T(8,128)(2,1)S(1)} collective-permute-done((bf16[9,16,128]{2,1,0:T(8,128)(2,1)S(1)}, bf16[9,16,128]{2,1,0:T(8,128)(2,1)S(1)}, u32[]{:S(2)}, u32[]{:S(2)}) %collective-permute-start.7) | collective-permute-done | bytes 36896 | tf_op jit(solution)/shard_map/ppermute | solution.py:362
  131.9 3.4 %collective-permute-start.8 = (bf16[17,16,128]{2,1,0:T(8,128)(2,1)S(1)}, bf16[17,16,128]{2,1,0:T(8,128)(2,1)S(1)}, u32[]{:S(2)}, u32[]{:S(2)}) collective-permute-start(bf16[17,16,128]{2,1,0:T(8,128)(2,1)S(1)} %shard_map.136.mine_ref), channel_id=1, source_target_pairs={{0,2},{1,3},{2,0},{3,1},{4,6},{5,7},{6,4},{7,5},{8,10},{9,11},{10,... | collective-permute-start | bytes 208904 | tf_op jit(solution)/shard_map/ppermute | solution.py:362
  135.2 1.7 %collective-permute-done.8.refs_0_ = bf16[17,16,128]{2,1,0:T(8,128)(2,1)S(1)} collective-permute-done((bf16[17,16,128]{2,1,0:T(8,128)(2,1)S(1)}, bf16[17,16,128]{2,1,0:T(8,128)(2,1)S(1)}, u32[]{:S(2)}, u32[]{:S(2)}) %collective-permute-start.8) | collective-permute-done | bytes 69664 | tf_op jit(solution)/shard_map/ppermute | solution.py:362
  136.9 7.4 %collective-permute-start.9 = (bf16[33,16,128]{2,1,0:T(8,128)(2,1)S(1)}, bf16[33,16,128]{2,1,0:T(8,128)(2,1)S(1)}, u32[]{:S(2)}, u32[]{:S(2)}) collective-permute-start(bf16[33,16,128]{2,1,0:T(8,128)(2,1)S(1)} %shard_map.137.mine_ref), channel_id=1, source_target_pairs={{0,1},{1,0},{2,3},{3,2},{4,5},{5,4},{6,7},{7,6},{8,9},{9,8},{10,11... | collective-permute-start | bytes 405512 | tf_op jit(solution)/shard_map/ppermute | solution.py:362
  144.4 0.0 all-to-all-done.3.returned_ref
  144.4 0.0 copy-done
  144.4 0.0 copy-done.1
  144.4 1.6 %shard_map.138 = bf16[8,128,256]{2,1,0:T(8,128)(2,1)} custom-call(s32[1,12]{1,0:T(1,128)S(1)} %copy-done.1, f32[8,128,256]{2,1,0:T(8,128)S(1)} %copy-done, bf16[12,128,256]{2,1,0:T(8,128)(2,1)S(1)} %all-to-all-done.3.returned_ref, bf16[128,256]{1,0:T(8,128)(2,1)S(1)} %collective-permute-done.2.low_ref, bf16[128,256]{1,0:T(8,128)(2,1)S(1)} %collective-permute-done.3.high_ref), custom_call_target="tpu_custom_call" | custom-call | flops 1000000 | bytes 3000000 | tf_op jit(solution)/shard_map/pallas_call | solution.py:443
  146.0 0.0 collective-permute-done.9.refs_0_
  146.0 0.8 shard_map.140
  (7 shorter events, 0.1 us)
Async XLA Ops:
  3.5 43.9 %all-to-all-start = ((bf16[12,128,256]{2,1,0:T(8,128)(2,1)}), bf16[12,128,256]{2,1,0:T(8,128)(2,1)S(1)}, u32[]{:S(2)}, u32[]{:S(2)}) async-start(bf16[12,128,256]{2,1,0:T(8,128)(2,1)} %shard_map.128), calls=%async_computation | async-start | bytes 1572864 | tf_op jit(solution)/shard_map/all_to_all | solution.py:421
  20.1 6.0 %collective-permute-start = (bf16[128,256]{1,0:T(8,128)(2,1)S(1)}, bf16[128,256]{1,0:T(8,128)(2,1)S(1)}, u32[]{:S(2)}, u32[]{:S(2)}) collective-permute-start(bf16[128,256]{1,0:T(8,128)(2,1)S(1)} %get-tuple-element.38), channel_id=1, source_target_pairs={{0,1},{1,2},{2,3},{3,4},{4,5},{5,6},{6,7},{7,8},{8,9},{9,10},{10,1... | collective-permute-start | bytes 196616 | tf_op jit(solution)/shard_map/ppermute | solution.py:324
  24.1 5.9 %collective-permute-start.1 = (bf16[128,256]{1,0:T(8,128)(2,1)S(1)}, bf16[128,256]{1,0:T(8,128)(2,1)S(1)}, u32[]{:S(2)}, u32[]{:S(2)}) collective-permute-start(bf16[128,256]{1,0:T(8,128)(2,1)S(1)} %get-tuple-element.37), channel_id=1, source_target_pairs={{1,0},{2,1},{3,2},{4,3},{5,4},{6,5},{7,6},{8,7},{9,8},{10,9},{11,1... | collective-permute-start | bytes 196616 | tf_op jit(solution)/shard_map/ppermute | solution.py:324
  26.1 21.3 %copy-start.4 = (bf16[128,256]{1,0:T(8,128)(2,1)}, bf16[128,256]{1,0:T(8,128)(2,1)S(1)}, u32[]{:S(2)}) copy-start(bf16[128,256]{1,0:T(8,128)(2,1)S(1)} %collective-permute-done.left_ref) | copy-start | bytes 196612
  30.0 17.3 %copy-start.5 = (bf16[128,256]{1,0:T(8,128)(2,1)}, bf16[128,256]{1,0:T(8,128)(2,1)S(1)}, u32[]{:S(2)}) copy-start(bf16[128,256]{1,0:T(8,128)(2,1)S(1)} %collective-permute-done.1.right_ref) | copy-start | bytes 196612
  47.3 0.9 copy-start.3
  56.0 26.3 %all-to-all-start.1 = ((bf16[64,8,256]{2,1,0:T(8,128)(2,1)}), bf16[64,8,256]{2,1,0:T(8,128)(2,1)S(1)}, u32[]{:S(2)}, u32[]{:S(2)}) async-start(bf16[64,8,256]{2,1,0:T(8,128)(2,1)} %bitcast.16), calls=%async_computation.1 | async-start | bytes 524288 | tf_op jit(solution)/shard_map/all_to_all | solution.py:332
  70.3 12.0 %copy-start.2 = (f32[1,256]{1,0:T(1,128)S(1)}, f32[1,256]{1,0:T(1,128)}, u32[]{:S(2)}) copy-start(f32[1,256]{1,0:T(1,128)} %get-tuple-element.23.gbias_ref) | copy-start | bytes 3076
  77.4 67.0 %copy-start = (f32[8,128,256]{2,1,0:T(8,128)S(1)}, f32[8,128,256]{2,1,0:T(8,128)}, u32[]{:S(2)}) copy-start(f32[8,128,256]{2,1,0:T(8,128)} %get-tuple-element.28.own_ref) | copy-start | bytes 3145732
  77.4 67.0 %copy-start.1 = (s32[1,12]{1,0:T(1,128)S(1)}, s32[1,12]{1,0:T(1,128)}, u32[]{:S(2)}) copy-start(s32[1,12]{1,0:T(1,128)} %send_ref.3) | copy-start | bytes 148
  83.0 14.5 %all-to-all-start.2 = ((bf16[12,32,128]{2,1,0:T(8,128)(2,1)}), bf16[12,32,128]{2,1,0:T(8,128)(2,1)S(1)}, u32[]{:S(2)}, u32[]{:S(2)}) async-start(bf16[12,32,128]{2,1,0:T(8,128)(2,1)} %shard_map.130), calls=%async_computation.2 | async-start | bytes 196608 | tf_op jit(solution)/shard_map/all_to_all | solution.py:341
  88.1 9.4 %collective-permute-start.2 = (bf16[128,256]{1,0:T(8,128)(2,1)S(1)}, bf16[128,256]{1,0:T(8,128)(2,1)S(1)}, u32[]{:S(2)}, u32[]{:S(2)}) collective-permute-start(bf16[128,256]{1,0:T(8,128)(2,1)S(1)} %get-tuple-element.40), channel_id=1, source_target_pairs={{0,1},{1,2},{2,3},{3,4},{4,5},{5,6},{6,7},{7,8},{8,9},{9,10},{10,1... | collective-permute-start | bytes 196616 | tf_op jit(solution)/shard_map/ppermute | solution.py:324
  91.6 5.9 %collective-permute-start.3 = (bf16[128,256]{1,0:T(8,128)(2,1)S(1)}, bf16[128,256]{1,0:T(8,128)(2,1)S(1)}, u32[]{:S(2)}, u32[]{:S(2)}) collective-permute-start(bf16[128,256]{1,0:T(8,128)(2,1)S(1)} %get-tuple-element.39), channel_id=1, source_target_pairs={{1,0},{2,1},{3,2},{4,3},{5,4},{6,5},{7,6},{8,7},{9,8},{10,9},{11,1... | collective-permute-start | bytes 196616 | tf_op jit(solution)/shard_map/ppermute | solution.py:324
  97.5 46.9 %all-to-all-start.3 = ((bf16[12,128,256]{2,1,0:T(8,128)(2,1)}), bf16[12,128,256]{2,1,0:T(8,128)(2,1)S(1)}, u32[]{:S(2)}, u32[]{:S(2)}) async-start(bf16[12,128,256]{2,1,0:T(8,128)(2,1)} %get-tuple-element.29), calls=%async_computation.3 | async-start | bytes 1572864 | tf_op jit(solution)/shard_map/all_to_all | solution.py:442
  106.6 6.2 %collective-permute-start.4 = (bf16[2,16,128]{2,1,0:T(8,128)(2,1)S(1)}, bf16[2,16,128]{2,1,0:T(8,128)(2,1)S(1)}, u32[]{:S(2)}, u32[]{:S(2)}) collective-permute-start(bf16[2,16,128]{2,1,0:T(8,128)(2,1)S(1)} %shard_map.131.mine_ref), channel_id=1, source_target_pairs={{0,32},{1,33},{2,34},{3,35},{4,36},{5,37},{6,38},{7,39},{8,40},{9,... | collective-permute-start | bytes 24584 | tf_op jit(solution)/shard_map/ppermute | solution.py:362
  112.8 4.4 %collective-permute-start.5 = (bf16[3,16,128]{2,1,0:T(8,128)(2,1)S(1)}, bf16[3,16,128]{2,1,0:T(8,128)(2,1)S(1)}, u32[]{:S(2)}, u32[]{:S(2)}) collective-permute-start(bf16[3,16,128]{2,1,0:T(8,128)(2,1)S(1)} %shard_map.133.mine_ref), channel_id=1, source_target_pairs={{0,16},{1,17},{2,18},{3,19},{4,20},{5,21},{6,22},{7,23},{8,24},{9,... | collective-permute-start | bytes 36872 | tf_op jit(solution)/shard_map/ppermute | solution.py:362
  117.2 8.7 %collective-permute-start.6 = (bf16[5,16,128]{2,1,0:T(8,128)(2,1)S(1)}, bf16[5,16,128]{2,1,0:T(8,128)(2,1)S(1)}, u32[]{:S(2)}, u32[]{:S(2)}) collective-permute-start(bf16[5,16,128]{2,1,0:T(8,128)(2,1)S(1)} %shard_map.134.mine_ref), channel_id=1, source_target_pairs={{0,8},{1,9},{2,10},{3,11},{4,12},{5,13},{6,14},{7,15},{8,0},{9,1},... | collective-permute-start | bytes 61448 | tf_op jit(solution)/shard_map/ppermute | solution.py:362
  126.0 5.9 %collective-permute-start.7 = (bf16[9,16,128]{2,1,0:T(8,128)(2,1)S(1)}, bf16[9,16,128]{2,1,0:T(8,128)(2,1)S(1)}, u32[]{:S(2)}, u32[]{:S(2)}) collective-permute-start(bf16[9,16,128]{2,1,0:T(8,128)(2,1)S(1)} %shard_map.135.mine_ref), channel_id=1, source_target_pairs={{0,4},{1,5},{2,6},{3,7},{4,0},{5,1},{6,2},{7,3},{8,12},{9,13},{10,... | collective-permute-start | bytes 110600 | tf_op jit(solution)/shard_map/ppermute | solution.py:362
  131.9 5.1 %collective-permute-start.8 = (bf16[17,16,128]{2,1,0:T(8,128)(2,1)S(1)}, bf16[17,16,128]{2,1,0:T(8,128)(2,1)S(1)}, u32[]{:S(2)}, u32[]{:S(2)}) collective-permute-start(bf16[17,16,128]{2,1,0:T(8,128)(2,1)S(1)} %shard_map.136.mine_ref), channel_id=1, source_target_pairs={{0,2},{1,3},{2,0},{3,1},{4,6},{5,7},{6,4},{7,5},{8,10},{9,11},{10,... | collective-permute-start | bytes 208904 | tf_op jit(solution)/shard_map/ppermute | solution.py:362
  136.9 9.1 %collective-permute-start.9 = (bf16[33,16,128]{2,1,0:T(8,128)(2,1)S(1)}, bf16[33,16,128]{2,1,0:T(8,128)(2,1)S(1)}, u32[]{:S(2)}, u32[]{:S(2)}) collective-permute-start(bf16[33,16,128]{2,1,0:T(8,128)(2,1)S(1)} %shard_map.137.mine_ref), channel_id=1, source_target_pairs={{0,1},{1,0},{2,3},{3,2},{4,5},{5,4},{6,7},{7,6},{8,9},{9,8},{10,11... | collective-permute-start | bytes 405512 | tf_op jit(solution)/shard_map/ppermute | solution.py:362

commit v8 on v7

--- a/solution.py
+++ b/solution.py
@@ -6,9 +6,12 @@
 from jax import lax
 from jax.experimental import pallas as pl
 from jax.experimental.pallas import tpu as pltpu
+from jax.sharding import Mesh
 from jax.sharding import PartitionSpec as P
 
 LANES = 128
+INNER = ("hi", "mid", "lo")
+ALL = ("dom",) + INNER
 VMEM = pl.BlockSpec(memory_space=pltpu.VMEM)
 SMEM = pl.BlockSpec(memory_space=pltpu.SMEM)
 ANY = pl.BlockSpec(memory_space=pl.ANY)
@@ -45,20 +48,22 @@
     lanes = [summed[:, k : k + LANES] for k in range(0, hidden, LANES)]
     bias = [gbias_ref[:, k : k + LANES] for k in range(0, hidden, LANES)]
     tail = split_bias(jnp.concatenate(bias, axis=0))
-    tail.append(jnp.zeros((out_ref.shape[1] // 2 - 2 * len(bias), LANES), F32))
+    tail.append(jnp.zeros((8 - 2 * len(bias), LANES), F32))
     piece = jnp.concatenate(lanes + tail, axis=0).astype(BF16)
     out_ref[...] = jnp.broadcast_to(piece[None], out_ref.shape)
 
 
 def start_kernel(scale, spread_ref, out_ref):
-    rows = out_ref.shape[1]
+    count, rows = out_ref.shape[0] - 1, out_ref.shape[1]
     bias_rows = 2
-    summed = jnp.sum(spread_ref[...].astype(F32), axis=0) * scale
-    out_ref[0] = summed[:rows].astype(BF16)
-    tail = summed[rows:]
+    spread = spread_ref[...].astype(F32)
+    spread = spread.reshape((spread.shape[0] // count, count) + spread.shape[1:])
+    summed = jnp.sum(spread, axis=0) * scale
+    out_ref[:count] = summed[:, :rows].astype(BF16)
+    tail = jnp.sum(summed[:, rows:], axis=0)
     bias = tail[:bias_rows] + tail[bias_rows : 2 * bias_rows]
     spare = jnp.zeros((rows - 2 * bias_rows, LANES), F32)
-    out_ref[1] = jnp.concatenate(split_bias(bias) + [spare], axis=0).astype(BF16)
+    out_ref[count] = jnp.concatenate(split_bias(bias) + [spare], axis=0).astype(BF16)
 
 
 def grow_kernel(low, place_ref, mine_ref, *refs):
@@ -325,23 +330,24 @@
 
 
 def reduce_grads(grads, gbias, scale):
-    dom_size = lax.axis_size("dom")
-    inner_size = lax.axis_size("inner")
+    twins = lax.axis_size("mid")
+    peers = lax.axis_size("dom") * twins
+    inner_size = lax.axis_size(INNER)
     hidden = grads.shape[1]
     chunks = grads.reshape(inner_size, grads.shape[0] // inner_size, hidden)
-    pieces = lax.all_to_all(chunks, "inner", split_axis=0, concat_axis=0, tiled=True)
+    pieces = lax.all_to_all(chunks, INNER, split_axis=0, concat_axis=0, tiled=True)
     rows = chunks.shape[1] * chunks.shape[2] // LANES
     spread = pl.pallas_call(
         piece_kernel,
-        out_shape=jax.ShapeDtypeStruct((dom_size, 2 * rows, LANES), BF16),
+        out_shape=jax.ShapeDtypeStruct((peers, rows + 8, LANES), BF16),
         in_specs=[VMEM, VMEM],
         out_specs=VMEM,
         compiler_params=params(),
     )(pieces, gbias)
-    spread = lax.all_to_all(spread, "dom", split_axis=0, concat_axis=0, tiled=True)
+    spread = lax.all_to_all(spread, ("dom", "mid"), split_axis=0, concat_axis=0, tiled=True)
     return pl.pallas_call(
         functools.partial(start_kernel, scale),
-        out_shape=jax.ShapeDtypeStruct((2, rows, LANES), BF16),
+        out_shape=jax.ShapeDtypeStruct((twins + 1, rows, LANES), BF16),
         in_specs=[VMEM],
         out_specs=VMEM,
         compiler_params=params(),
@@ -349,17 +355,17 @@
 
 
 def gather_grads(state, hidden, beside):
-    inner_size = lax.axis_size("inner")
+    inner_size = lax.axis_size(INNER)
     bits = inner_size.bit_length() - 1
-    groups = [(low, 1) for low in reversed(range(bits))]
-    index = lax.axis_index("inner").astype(jnp.int32).reshape(1)
-    place = [0] * inner_size
+    groups = [(low, 1) for low in reversed(range(bits)) if low != 1]
+    index = lax.axis_index(INNER).astype(jnp.int32).reshape(1)
+    place = [(chunk >> 1) % 2 for chunk in range(inner_size)]
     for low, size in groups:
         count = state.shape[0] - 1
         theirs = []
         for mask in range(1, 1 << size):
             pairs = [(i, i ^ (mask << low)) for i in range(inner_size)]
-            theirs.append(lax.ppermute(state, "inner", pairs))
+            theirs.append(lax.ppermute(state, INNER, pairs))
         if low == groups[-1][0]:
             theirs, beside = lax.optimization_barrier((theirs, beside))
         place = [
@@ -419,7 +425,7 @@
         compiler_params=params(58),
     )(send_blocks, blocks)
     received = lax.all_to_all(outgoing, "dom", split_axis=0, concat_axis=0, tiled=True)
-    left, right = neighbours(blocks[nblocks - 1], blocks[0], "inner")
+    left, right = neighbours(blocks[nblocks - 1], blocks[0], INNER)
     degree = in_degree.reshape(nblocks, rows)
     layer_out, grad_pre, grads, gbias = call_forward(
         blocks,
@@ -435,8 +441,8 @@
         bias[None, :],
     )
     own, rims, slots = call_backward(grad_pre, tiles, pair_source, degree, w_self, w_neigh)
-    low, high = neighbours(rims[1], rims[0], "inner")
-    scale = 1.0 / math.sqrt(rows_dev * dom_size * lax.axis_size("inner"))
+    low, high = neighbours(rims[1], rims[0], INNER)
+    scale = 1.0 / math.sqrt(rows_dev * dom_size * lax.axis_size(INNER))
     state = reduce_grads(grads, gbias, scale)
     state, slots, low, high = lax.optimization_barrier((state, slots, low, high))
     returned = lax.all_to_all(slots, "dom", split_axis=0, concat_axis=0, tiled=True)
@@ -462,20 +468,21 @@
 
 
 def solution(mesh):
+    devices = mesh.devices.reshape(mesh.shape["dom"], -1, 2, 2)
     return jax.shard_map(
         per_device,
-        mesh=mesh,
+        mesh=Mesh(devices, ALL),
         in_specs=(
-            P(("dom", "inner"), None),
-            P(("dom", "inner"), None, None, None),
-            P(("dom", "inner"), None),
-            P(("dom", "inner")),
-            P(("dom", "inner"), None),
+            P(ALL, None),
+            P(ALL, None, None, None),
+            P(ALL, None),
+            P(ALL),
+            P(ALL, None),
             P(),
             P(),
             P(),
-            P(("dom", "inner"), None),
-        ),
-        out_specs=(P(("dom", "inner"), None), P(("dom", "inner"), None), P(), P(), P()),
+            P(ALL, None),
+        ),
+        out_specs=(P(ALL, None), P(ALL, None), P(), P(), P()),
         check_vma=False,
     )

time: 148 us -> 151 us (1.020)
  blocking collectives: 0 us -> 26.3 us
  starting transfers between devices: 79.1 us -> 61.8 us
  waiting for transfers between devices: 43.3 us -> 37.2 us
    all_to_all x0 -> x1, blocking collectives: none -> 26.3 us  [reduce_grads(): lax.all_to_all(chunks, INNER, split_axis=0, concat_axis=0, tiled=True)]
    all_to_all x2 -> x1, starting transfers between devices: 18.5 us -> 5.26 us  [reduce_grads(): lax.all_to_all(spread, ('dom', 'mid'), split_axis=0, concat_axis=0, tiled...]
    all_to_all x2 -> x1, waiting for transfers between devices: 8.73 us -> 0.01 us  [reduce_grads(): lax.all_to_all(spread, ('dom', 'mid'), split_axis=0, concat_axis=0, tiled...]
    ppermute x6 -> x5, starting transfers between devices: 24.4 us -> 20.2 us  [gather_grads(): theirs.append(lax.ppermute(state, INNER, pairs))]
    ppermute x2, waiting for transfers between devices: 3.96 us -> 7.53 us  [neighbours(): lax.ppermute(high_source, axis, backward)]
    ppermute x6 -> x5, waiting for transfers between devices: 13.3 us -> 12.4 us  [gather_grads(): theirs.append(lax.ppermute(state, INNER, pairs))]
  transfers between devices with their start and end apart: 14 -> 12, of which waited for: 9 -> 7; matrix products, arithmetic and copies ran while one was open for 1% -> 1% of each run, Pallas kernels for 6% -> 6%
where the time goes in v8:
time: 151 us
  starting transfers between devices  61.8 us (41%)
  waiting for transfers between devices  37.2 us (25%)
  blocking collectives  26.3 us (17%)
  Pallas kernels  21 us (14%)
  local copies, waits for them, and re-layouts  3.42 us (2%)
    all_to_all x1, blocking collectives, reduce_grads(): lax.all_to_all(chunks, INNER, split_axis=0, concat_axis=0, tiled=True)  26.3 us
    ppermute x5, starting transfers between devices, gather_grads(): theirs.append(lax.ppermute(state, INNER, pairs))  20.2 us
    all_to_all x1, waiting for transfers between devices, per_device(): lax.all_to_all(outgoing, 'dom', split_axis=0, concat_axis=0, tiled=True)  17.3 us
    all_to_all x1, starting transfers between devices, per_device(): lax.all_to_all(outgoing, 'dom', split_axis=0, concat_axis=0, tiled=True)  15.7 us
    ppermute x5, waiting for transfers between devices, gather_grads(): theirs.append(lax.ppermute(state, INNER, pairs))  12.4 us
    all_to_all x1, starting transfers between devices, per_device(): lax.all_to_all(slots, 'dom', split_axis=0, concat_axis=0, tiled=True)  8.81 us
    ppermute x2, starting transfers between devices, neighbours(): lax.ppermute(low_source, axis, forward)  7.99 us
    pallas_call x1, Pallas kernels, call_forward(): pl.pallas_call(forward_kernel, out_shape=(shape(blocks.shape, BF16), shap...  7.75 us
  transfers between devices with their start and end apart: 12, of which 7 were waited for; matrix products, arithmetic and copies ran while one was open for 1% of the time, Pallas kernels for 6%

profile of v8, /device:TPU:1, one launch (start us, length us, event | category | flops | bytes accessed | tf_op | source)
XLA Modules:
  0.0 150.6 jit_solution(10901851752049086232)
XLA Ops:
  0.6 2.8 %shard_map.128 = bf16[12,128,256]{2,1,0:T(8,128)(2,1)} custom-call(s32[1,12]{1,0:T(1,128)} %send_ref.3, bf16[8,128,256]{2,1,0:T(8,128)(2,1)} %bitcast.13), custom_call_target="tpu_custom_call" | custom-call | tf_op jit(solution)/shard_map/pallas_call | solution.py:419
  3.4 15.7 %all-to-all-start = ((bf16[12,128,256]{2,1,0:T(8,128)(2,1)}), bf16[12,128,256]{2,1,0:T(8,128)(2,1)S(1)}, u32[]{:S(2)}, u32[]{:S(2)}) async-start(bf16[12,128,256]{2,1,0:T(8,128)(2,1)} %shard_map.128), calls=%async_computation | async-start | bytes 1572864 | tf_op jit(solution)/shard_map/all_to_all | solution.py:427
  19.2 0.9 fusion
  20.1 4.0 %collective-permute-start = (bf16[128,256]{1,0:T(8,128)(2,1)S(1)}, bf16[128,256]{1,0:T(8,128)(2,1)S(1)}, u32[]{:S(2)}, u32[]{:S(2)}) collective-permute-start(bf16[128,256]{1,0:T(8,128)(2,1)S(1)} %get-tuple-element.38), channel_id=1, source_target_pairs={{0,1},{1,2},{2,3},{3,4},{4,5},{5,6},{6,7},{7,8},{8,9},{9,10},{10,1... | collective-permute-start | bytes 196616 | tf_op jit(solution)/shard_map/ppermute | solution.py:329
  24.1 1.9 %collective-permute-start.1 = (bf16[128,256]{1,0:T(8,128)(2,1)S(1)}, bf16[128,256]{1,0:T(8,128)(2,1)S(1)}, u32[]{:S(2)}, u32[]{:S(2)}) collective-permute-start(bf16[128,256]{1,0:T(8,128)(2,1)S(1)} %get-tuple-element.37), channel_id=1, source_target_pairs={{1,0},{2,1},{3,2},{4,3},{5,4},{6,5},{7,6},{8,7},{9,8},{10,9},{11,1... | collective-permute-start | bytes 196616 | tf_op jit(solution)/shard_map/ppermute | solution.py:329
  26.0 0.0 collective-permute-done.left_ref
  26.0 0.0 copy-start.4
  26.1 3.9 %collective-permute-done.1.right_ref = bf16[128,256]{1,0:T(8,128)(2,1)S(1)} collective-permute-done((bf16[128,256]{1,0:T(8,128)(2,1)S(1)}, bf16[128,256]{1,0:T(8,128)(2,1)S(1)}, u32[]{:S(2)}, u32[]{:S(2)}) %collective-permute-start.1) | collective-permute-done | bytes 65568 | tf_op jit(solution)/shard_map/ppermute | solution.py:329
  30.0 0.0 copy-start.5
  30.0 17.3 %all-to-all-done.received_hbm = bf16[12,128,256]{2,1,0:T(8,128)(2,1)S(1)} async-done(((bf16[12,128,256]{2,1,0:T(8,128)(2,1)}), bf16[12,128,256]{2,1,0:T(8,128)(2,1)S(1)}, u32[]{:S(2)}, u32[]{:S(2)}) %all-to-all-start) | async-done | bytes 786464 | tf_op jit(solution)/shard_map/all_to_all | solution.py:427
  47.3 0.0 copy-start.3
  47.3 0.0 copy-done.4
  47.3 0.0 copy-done.5
  47.3 0.9 copy-done.3
  48.2 7.8 %shard_map.129 = (bf16[8,128,256]{2,1,0:T(8,128)(2,1)}, bf16[1024,256]{1,0:T(8,128)(2,1)}, bf16[512,256]{1,0:T(8,128)(2,1)}, f32[1,256]{1,0:T(1,128)}) custom-call(s32[8,8]{1,0:T(8,128)} %pairs_ref.3, s32[8,128]{1,0:T(8,128)} %bitcast.18, bf16[256,256]{1,0:T(8,128)(2,1)} %w_self_ref.3, bf16[256,256]{1,0:T(8,128)(2,1)} %w_neigh_ref.3, f32[1,256]{1,0:T(1,128)} %bitcast.20, ...), custom_call_target="tpu_custom_call" | custom-call | flops 2000000000 | bytes 6000000 | tf_op jit(solution)/shard_map/pallas_call | solution.py:269
  55.9 26.3 %all_to_all.20.pieces_ref = bf16[64,8,256]{2,1,0:T(8,128)(2,1)S(1)} all-to-all(bf16[64,8,256]{2,1,0:T(8,128)(2,1)} %bitcast.16), channel_id=1, replica_groups=mesh['dom'=12,'hi'=16,'mid'=2,'lo'=2] {'hi','mid','lo'}, dimensions={0} | all-to-all | bytes 524288 | tf_op jit(solution)/shard_map/all_to_all | solution.py:338
  82.3 0.0 copy-start.2
  82.3 0.7 copy-done.2
  82.9 0.7 shard_map.130
  83.7 5.3 %all-to-all-start.2 = ((bf16[24,24,128]{2,1,0:T(8,128)(2,1)}), bf16[24,24,128]{2,1,0:T(8,128)(2,1)S(1)}, u32[]{:S(2)}, u32[]{:S(2)}) async-start(bf16[24,24,128]{2,1,0:T(8,128)(2,1)} %shard_map.130), calls=%async_computation.2 | async-start | bytes 294912 | tf_op jit(solution)/shard_map/all_to_all | solution.py:347
  88.9 7.1 %shard_map.132 = (f32[8,128,256]{2,1,0:T(8,128)}, bf16[2,128,256]{2,1,0:T(8,128)(2,1)}, bf16[12,128,256]{2,1,0:T(8,128)(2,1)}) custom-call(s32[8,8]{1,0:T(8,128)} %pairs_ref.3, s32[8,128]{1,0:T(8,128)} %bitcast.19, bf16[256,256]{1,0:T(8,128)(2,1)} %w_self_ref.3, bf16[256,256]{1,0:T(8,128)(2,1)} %w_neigh_ref.3, bf16[1024,256]{1,0:T(8,128)(2,1)} %get-tuple-element.24.grad_ref, ...), custom_call_target="tpu_custom_call" | custom-call | flops 2000000000 | bytes 8000000 | tf_op jit(solution)/shard_map/pallas_call | solution.py:303
  96.1 0.0 copy-start
  96.1 0.0 copy-start.1
  96.1 1.0 slice_bitcast_fusion
  97.1 3.9 %collective-permute-start.2 = (bf16[128,256]{1,0:T(8,128)(2,1)S(1)}, bf16[128,256]{1,0:T(8,128)(2,1)S(1)}, u32[]{:S(2)}, u32[]{:S(2)}) collective-permute-start(bf16[128,256]{1,0:T(8,128)(2,1)S(1)} %get-tuple-element.40), channel_id=1, source_target_pairs={{0,1},{1,2},{2,3},{3,4},{4,5},{5,6},{6,7},{7,8},{8,9},{9,10},{10,1... | collective-permute-start | bytes 196616 | tf_op jit(solution)/shard_map/ppermute | solution.py:329
  101.0 1.9 %collective-permute-start.3 = (bf16[128,256]{1,0:T(8,128)(2,1)S(1)}, bf16[128,256]{1,0:T(8,128)(2,1)S(1)}, u32[]{:S(2)}, u32[]{:S(2)}) collective-permute-start(bf16[128,256]{1,0:T(8,128)(2,1)S(1)} %get-tuple-element.39), channel_id=1, source_target_pairs={{1,0},{2,1},{3,2},{4,3},{5,4},{6,5},{7,6},{8,7},{9,8},{10,9},{11,1... | collective-permute-start | bytes 196616 | tf_op jit(solution)/shard_map/ppermute | solution.py:329
  102.9 0.0 all-to-all-done.2.spread_ref
  103.0 0.0 collective-permute-done.2.low_ref
  103.0 3.6 %collective-permute-done.3.high_ref = bf16[128,256]{1,0:T(8,128)(2,1)S(1)} collective-permute-done((bf16[128,256]{1,0:T(8,128)(2,1)S(1)}, bf16[128,256]{1,0:T(8,128)(2,1)S(1)}, u32[]{:S(2)}, u32[]{:S(2)}) %collective-permute-start.3) | collective-permute-done | bytes 65568 | tf_op jit(solution)/shard_map/ppermute | solution.py:329
  106.6 8.8 %all-to-all-start.3 = ((bf16[12,128,256]{2,1,0:T(8,128)(2,1)}), bf16[12,128,256]{2,1,0:T(8,128)(2,1)S(1)}, u32[]{:S(2)}, u32[]{:S(2)}) async-start(bf16[12,128,256]{2,1,0:T(8,128)(2,1)} %get-tuple-element.29), calls=%async_computation.3 | async-start | bytes 1572864 | tf_op jit(solution)/shard_map/all_to_all | solution.py:448
  115.4 4.0 %collective-permute-start.4 = (bf16[3,16,128]{2,1,0:T(8,128)(2,1)S(1)}, bf16[3,16,128]{2,1,0:T(8,128)(2,1)S(1)}, u32[]{:S(2)}, u32[]{:S(2)}) collective-permute-start(bf16[3,16,128]{2,1,0:T(8,128)(2,1)S(1)} %shard_map.131.mine_ref), channel_id=1, source_target_pairs={{0,32},{1,33},{2,34},{3,35},{4,36},{5,37},{6,38},{7,39},{8,40},{9,... | collective-permute-start | bytes 36872 | tf_op jit(solution)/shard_map/ppermute | solution.py:368
  119.4 2.2 %collective-permute-done.4.refs_0_ = bf16[3,16,128]{2,1,0:T(8,128)(2,1)S(1)} collective-permute-done((bf16[3,16,128]{2,1,0:T(8,128)(2,1)S(1)}, bf16[3,16,128]{2,1,0:T(8,128)(2,1)S(1)}, u32[]{:S(2)}, u32[]{:S(2)}) %collective-permute-start.4) | collective-permute-done | bytes 12320 | tf_op jit(solution)/shard_map/ppermute | solution.py:368
  121.7 2.4 %collective-permute-start.5 = (bf16[5,16,128]{2,1,0:T(8,128)(2,1)S(1)}, bf16[5,16,128]{2,1,0:T(8,128)(2,1)S(1)}, u32[]{:S(2)}, u32[]{:S(2)}) collective-permute-start(bf16[5,16,128]{2,1,0:T(8,128)(2,1)S(1)} %shard_map.133.mine_ref), channel_id=1, source_target_pairs={{0,16},{1,17},{2,18},{3,19},{4,20},{5,21},{6,22},{7,23},{8,24},{9,... | collective-permute-start | bytes 61448 | tf_op jit(solution)/shard_map/ppermute | solution.py:368
  124.1 2.1 %collective-permute-done.5.refs_0_ = bf16[5,16,128]{2,1,0:T(8,128)(2,1)S(1)} collective-permute-done((bf16[5,16,128]{2,1,0:T(8,128)(2,1)S(1)}, bf16[5,16,128]{2,1,0:T(8,128)(2,1)S(1)}, u32[]{:S(2)}, u32[]{:S(2)}) %collective-permute-start.5) | collective-permute-done | bytes 20512 | tf_op jit(solution)/shard_map/ppermute | solution.py:368
  126.2 4.2 %collective-permute-start.6 = (bf16[9,16,128]{2,1,0:T(8,128)(2,1)S(1)}, bf16[9,16,128]{2,1,0:T(8,128)(2,1)S(1)}, u32[]{:S(2)}, u32[]{:S(2)}) collective-permute-start(bf16[9,16,128]{2,1,0:T(8,128)(2,1)S(1)} %shard_map.134.mine_ref), channel_id=1, source_target_pairs={{0,8},{1,9},{2,10},{3,11},{4,12},{5,13},{6,14},{7,15},{8,0},{9,1},... | collective-permute-start | bytes 110600 | tf_op jit(solution)/shard_map/ppermute | solution.py:368
  130.4 4.7 %collective-permute-done.6.refs_0_ = bf16[9,16,128]{2,1,0:T(8,128)(2,1)S(1)} collective-permute-done((bf16[9,16,128]{2,1,0:T(8,128)(2,1)S(1)}, bf16[9,16,128]{2,1,0:T(8,128)(2,1)S(1)}, u32[]{:S(2)}, u32[]{:S(2)}) %collective-permute-start.6) | collective-permute-done | bytes 36896 | tf_op jit(solution)/shard_map/ppermute | solution.py:368
  135.1 3.7 %collective-permute-start.7 = (bf16[17,16,128]{2,1,0:T(8,128)(2,1)S(1)}, bf16[17,16,128]{2,1,0:T(8,128)(2,1)S(1)}, u32[]{:S(2)}, u32[]{:S(2)}) collective-permute-start(bf16[17,16,128]{2,1,0:T(8,128)(2,1)S(1)} %shard_map.135.mine_ref), channel_id=1, source_target_pairs={{0,4},{1,5},{2,6},{3,7},{4,0},{5,1},{6,2},{7,3},{8,12},{9,13},{10,... | collective-permute-start | bytes 208904 | tf_op jit(solution)/shard_map/ppermute | solution.py:368
  138.8 3.3 %collective-permute-done.7.refs_0_ = bf16[17,16,128]{2,1,0:T(8,128)(2,1)S(1)} collective-permute-done((bf16[17,16,128]{2,1,0:T(8,128)(2,1)S(1)}, bf16[17,16,128]{2,1,0:T(8,128)(2,1)S(1)}, u32[]{:S(2)}, u32[]{:S(2)}) %collective-permute-start.7) | collective-permute-done | bytes 69664 | tf_op jit(solution)/shard_map/ppermute | solution.py:368
  142.2 5.9 %collective-permute-start.8 = (bf16[33,16,128]{2,1,0:T(8,128)(2,1)S(1)}, bf16[33,16,128]{2,1,0:T(8,128)(2,1)S(1)}, u32[]{:S(2)}, u32[]{:S(2)}) collective-permute-start(bf16[33,16,128]{2,1,0:T(8,128)(2,1)S(1)} %shard_map.136.mine_ref), channel_id=1, source_target_pairs={{0,1},{1,0},{2,3},{3,2},{4,5},{5,4},{6,7},{7,6},{8,9},{9,8},{10,11... | collective-permute-start | bytes 405512 | tf_op jit(solution)/shard_map/ppermute | solution.py:368
  148.1 0.0 all-to-all-done.3.returned_ref
  148.1 0.0 copy-done
  148.1 0.0 copy-done.1
  148.1 1.6 %shard_map.137 = bf16[8,128,256]{2,1,0:T(8,128)(2,1)} custom-call(s32[1,12]{1,0:T(1,128)S(1)} %copy-done.1, f32[8,128,256]{2,1,0:T(8,128)S(1)} %copy-done, bf16[12,128,256]{2,1,0:T(8,128)(2,1)S(1)} %all-to-all-done.3.returned_ref, bf16[128,256]{1,0:T(8,128)(2,1)S(1)} %collective-permute-done.2.low_ref, bf16[128,256]{1,0:T(8,128)(2,1)S(1)} %collective-permute-done.3.high_ref), custom_call_target="tpu_custom_call" | custom-call | flops 1000000 | bytes 3000000 | tf_op jit(solution)/shard_map/pallas_call | solution.py:449
  149.7 0.0 collective-permute-done.8.refs_0_
  149.8 0.8 shard_map.139
  (6 shorter events, 0.1 us)
Async XLA Ops:
  3.4 43.8 %all-to-all-start = ((bf16[12,128,256]{2,1,0:T(8,128)(2,1)}), bf16[12,128,256]{2,1,0:T(8,128)(2,1)S(1)}, u32[]{:S(2)}, u32[]{:S(2)}) async-start(bf16[12,128,256]{2,1,0:T(8,128)(2,1)} %shard_map.128), calls=%async_computation | async-start | bytes 1572864 | tf_op jit(solution)/shard_map/all_to_all | solution.py:427
  20.1 6.0 %collective-permute-start = (bf16[128,256]{1,0:T(8,128)(2,1)S(1)}, bf16[128,256]{1,0:T(8,128)(2,1)S(1)}, u32[]{:S(2)}, u32[]{:S(2)}) collective-permute-start(bf16[128,256]{1,0:T(8,128)(2,1)S(1)} %get-tuple-element.38), channel_id=1, source_target_pairs={{0,1},{1,2},{2,3},{3,4},{4,5},{5,6},{6,7},{7,8},{8,9},{9,10},{10,1... | collective-permute-start | bytes 196616 | tf_op jit(solution)/shard_map/ppermute | solution.py:329
  24.1 5.9 %collective-permute-start.1 = (bf16[128,256]{1,0:T(8,128)(2,1)S(1)}, bf16[128,256]{1,0:T(8,128)(2,1)S(1)}, u32[]{:S(2)}, u32[]{:S(2)}) collective-permute-start(bf16[128,256]{1,0:T(8,128)(2,1)S(1)} %get-tuple-element.37), channel_id=1, source_target_pairs={{1,0},{2,1},{3,2},{4,3},{5,4},{6,5},{7,6},{8,7},{9,8},{10,9},{11,1... | collective-permute-start | bytes 196616 | tf_op jit(solution)/shard_map/ppermute | solution.py:329
  26.0 21.2 %copy-start.4 = (bf16[128,256]{1,0:T(8,128)(2,1)}, bf16[128,256]{1,0:T(8,128)(2,1)S(1)}, u32[]{:S(2)}) copy-start(bf16[128,256]{1,0:T(8,128)(2,1)S(1)} %collective-permute-done.left_ref) | copy-start | bytes 196612
  30.0 17.3 %copy-start.5 = (bf16[128,256]{1,0:T(8,128)(2,1)}, bf16[128,256]{1,0:T(8,128)(2,1)S(1)}, u32[]{:S(2)}) copy-start(bf16[128,256]{1,0:T(8,128)(2,1)S(1)} %collective-permute-done.1.right_ref) | copy-start | bytes 196612
  47.3 0.9 copy-start.3
  82.3 0.7 copy-start.2
  83.7 19.3 %all-to-all-start.2 = ((bf16[24,24,128]{2,1,0:T(8,128)(2,1)}), bf16[24,24,128]{2,1,0:T(8,128)(2,1)S(1)}, u32[]{:S(2)}, u32[]{:S(2)}) async-start(bf16[24,24,128]{2,1,0:T(8,128)(2,1)} %shard_map.130), calls=%async_computation.2 | async-start | bytes 294912 | tf_op jit(solution)/shard_map/all_to_all | solution.py:347
  96.1 52.0 %copy-start = (f32[8,128,256]{2,1,0:T(8,128)S(1)}, f32[8,128,256]{2,1,0:T(8,128)}, u32[]{:S(2)}) copy-start(f32[8,128,256]{2,1,0:T(8,128)} %get-tuple-element.28.own_ref) | copy-start | bytes 3145732
  96.1 52.0 %copy-start.1 = (s32[1,12]{1,0:T(1,128)S(1)}, s32[1,12]{1,0:T(1,128)}, u32[]{:S(2)}) copy-start(s32[1,12]{1,0:T(1,128)} %send_ref.3) | copy-start | bytes 148
  97.1 5.9 %collective-permute-start.2 = (bf16[128,256]{1,0:T(8,128)(2,1)S(1)}, bf16[128,256]{1,0:T(8,128)(2,1)S(1)}, u32[]{:S(2)}, u32[]{:S(2)}) collective-permute-start(bf16[128,256]{1,0:T(8,128)(2,1)S(1)} %get-tuple-element.40), channel_id=1, source_target_pairs={{0,1},{1,2},{2,3},{3,4},{4,5},{5,6},{6,7},{7,8},{8,9},{9,10},{10,1... | collective-permute-start | bytes 196616 | tf_op jit(solution)/shard_map/ppermute | solution.py:329
  101.0 5.6 %collective-permute-start.3 = (bf16[128,256]{1,0:T(8,128)(2,1)S(1)}, bf16[128,256]{1,0:T(8,128)(2,1)S(1)}, u32[]{:S(2)}, u32[]{:S(2)}) collective-permute-start(bf16[128,256]{1,0:T(8,128)(2,1)S(1)} %get-tuple-element.39), channel_id=1, source_target_pairs={{1,0},{2,1},{3,2},{4,3},{5,4},{6,5},{7,6},{8,7},{9,8},{10,9},{11,1... | collective-permute-start | bytes 196616 | tf_op jit(solution)/shard_map/ppermute | solution.py:329
  106.6 41.5 %all-to-all-start.3 = ((bf16[12,128,256]{2,1,0:T(8,128)(2,1)}), bf16[12,128,256]{2,1,0:T(8,128)(2,1)S(1)}, u32[]{:S(2)}, u32[]{:S(2)}) async-start(bf16[12,128,256]{2,1,0:T(8,128)(2,1)} %get-tuple-element.29), calls=%async_computation.3 | async-start | bytes 1572864 | tf_op jit(solution)/shard_map/all_to_all | solution.py:448
  115.4 6.2 %collective-permute-start.4 = (bf16[3,16,128]{2,1,0:T(8,128)(2,1)S(1)}, bf16[3,16,128]{2,1,0:T(8,128)(2,1)S(1)}, u32[]{:S(2)}, u32[]{:S(2)}) collective-permute-start(bf16[3,16,128]{2,1,0:T(8,128)(2,1)S(1)} %shard_map.131.mine_ref), channel_id=1, source_target_pairs={{0,32},{1,33},{2,34},{3,35},{4,36},{5,37},{6,38},{7,39},{8,40},{9,... | collective-permute-start | bytes 36872 | tf_op jit(solution)/shard_map/ppermute | solution.py:368
  121.7 4.5 %collective-permute-start.5 = (bf16[5,16,128]{2,1,0:T(8,128)(2,1)S(1)}, bf16[5,16,128]{2,1,0:T(8,128)(2,1)S(1)}, u32[]{:S(2)}, u32[]{:S(2)}) collective-permute-start(bf16[5,16,128]{2,1,0:T(8,128)(2,1)S(1)} %shard_map.133.mine_ref), channel_id=1, source_target_pairs={{0,16},{1,17},{2,18},{3,19},{4,20},{5,21},{6,22},{7,23},{8,24},{9,... | collective-permute-start | bytes 61448 | tf_op jit(solution)/shard_map/ppermute | solution.py:368
  126.2 8.9 %collective-permute-start.6 = (bf16[9,16,128]{2,1,0:T(8,128)(2,1)S(1)}, bf16[9,16,128]{2,1,0:T(8,128)(2,1)S(1)}, u32[]{:S(2)}, u32[]{:S(2)}) collective-permute-start(bf16[9,16,128]{2,1,0:T(8,128)(2,1)S(1)} %shard_map.134.mine_ref), channel_id=1, source_target_pairs={{0,8},{1,9},{2,10},{3,11},{4,12},{5,13},{6,14},{7,15},{8,0},{9,1},... | collective-permute-start | bytes 110600 | tf_op jit(solution)/shard_map/ppermute | solution.py:368
  135.1 7.0 %collective-permute-start.7 = (bf16[17,16,128]{2,1,0:T(8,128)(2,1)S(1)}, bf16[17,16,128]{2,1,0:T(8,128)(2,1)S(1)}, u32[]{:S(2)}, u32[]{:S(2)}) collective-permute-start(bf16[17,16,128]{2,1,0:T(8,128)(2,1)S(1)} %shard_map.135.mine_ref), channel_id=1, source_target_pairs={{0,4},{1,5},{2,6},{3,7},{4,0},{5,1},{6,2},{7,3},{8,12},{9,13},{10,... | collective-permute-start | bytes 208904 | tf_op jit(solution)/shard_map/ppermute | solution.py:368
  142.2 7.6 %collective-permute-start.8 = (bf16[33,16,128]{2,1,0:T(8,128)(2,1)S(1)}, bf16[33,16,128]{2,1,0:T(8,128)(2,1)S(1)}, u32[]{:S(2)}, u32[]{:S(2)}) collective-permute-start(bf16[33,16,128]{2,1,0:T(8,128)(2,1)S(1)} %shard_map.136.mine_ref), channel_id=1, source_target_pairs={{0,1},{1,0},{2,3},{3,2},{4,5},{5,4},{6,7},{7,6},{8,9},{9,8},{10,11... | collective-permute-start | bytes 405512 | tf_op jit(solution)/shard_map/ppermute | solution.py:368

commit v9 on v8

--- a/solution.py
+++ b/solution.py
@@ -329,13 +329,14 @@
     return lax.ppermute(low_source, axis, forward), lax.ppermute(high_source, axis, backward)
 
 
-def reduce_grads(grads, gbias, scale):
+def reduce_grads(grads, gbias, scale, beside):
     twins = lax.axis_size("mid")
     peers = lax.axis_size("dom") * twins
     inner_size = lax.axis_size(INNER)
     hidden = grads.shape[1]
     chunks = grads.reshape(inner_size, grads.shape[0] // inner_size, hidden)
     pieces = lax.all_to_all(chunks, INNER, split_axis=0, concat_axis=0, tiled=True)
+    pieces, beside = lax.optimization_barrier((pieces, beside))
     rows = chunks.shape[1] * chunks.shape[2] // LANES
     spread = pl.pallas_call(
         piece_kernel,
@@ -345,13 +346,14 @@
         compiler_params=params(),
     )(pieces, gbias)
     spread = lax.all_to_all(spread, ("dom", "mid"), split_axis=0, concat_axis=0, tiled=True)
-    return pl.pallas_call(
+    state = pl.pallas_call(
         functools.partial(start_kernel, scale),
         out_shape=jax.ShapeDtypeStruct((twins + 1, rows, LANES), BF16),
         in_specs=[VMEM],
         out_specs=VMEM,
         compiler_params=params(),
     )(spread)
+    return state, beside
 
 
 def gather_grads(state, hidden, beside):
@@ -441,9 +443,9 @@
         bias[None, :],
     )
     own, rims, slots = call_backward(grad_pre, tiles, pair_source, degree, w_self, w_neigh)
+    scale = 1.0 / math.sqrt(rows_dev * dom_size * lax.axis_size(INNER))
+    state, (own, rims, slots) = reduce_grads(grads, gbias, scale, (own, rims, slots))
     low, high = neighbours(rims[1], rims[0], INNER)
-    scale = 1.0 / math.sqrt(rows_dev * dom_size * lax.axis_size(INNER))
-    state = reduce_grads(grads, gbias, scale)
     state, slots, low, high = lax.optimization_barrier((state, slots, low, high))
     returned = lax.all_to_all(slots, "dom", split_axis=0, concat_axis=0, tiled=True)
     grad_features = pl.pallas_call(

time: 151 us -> 144 us (0.954)
  blocking collectives: 26.3 us -> 0 us
  starting transfers between devices: 61.8 us -> 74.7 us
  waiting for transfers between devices: 37.2 us -> 43.6 us
    all_to_all x1 -> x0, blocking collectives: 26.3 us -> none  [reduce_grads(): lax.all_to_all(chunks, INNER, split_axis=0, concat_axis=0, tiled=True)]
    all_to_all x0 -> x1, starting transfers between devices: none -> 14.3 us  [reduce_grads(): lax.all_to_all(chunks, INNER, split_axis=0, concat_axis=0, tiled=True)]
    all_to_all x0 -> x1, waiting for transfers between devices: none -> 4.85 us  [reduce_grads(): lax.all_to_all(chunks, INNER, split_axis=0, concat_axis=0, tiled=True)]
    all_to_all x1, waiting for transfers between devices: 0.01 us -> 4.14 us  [reduce_grads(): lax.all_to_all(spread, ('dom', 'mid'), split_axis=0, concat_axis=0, tiled...]
    ppermute x2, waiting for transfers between devices: 7.53 us -> 3.96 us  [neighbours(): lax.ppermute(high_source, axis, backward)]
  transfers between devices with their start and end apart: 12 -> 13, of which waited for: 7 -> 8; matrix products, arithmetic and copies ran while one was open for 1% -> 1% of each run, Pallas kernels for 6% -> 6%
where the time goes in v9:
time: 144 us; the launch traced here: 143 us
  starting transfers between devices  74.7 us (52%)
  waiting for transfers between devices  43.6 us (30%)
  Pallas kernels  21 us (15%)
  local copies, waits for them, and re-layouts  2.67 us (2%)
    ppermute x5, starting transfers between devices, gather_grads(): theirs.append(lax.ppermute(state, INNER, pairs))  19.3 us
    all_to_all x1, waiting for transfers between devices, per_device(): lax.all_to_all(outgoing, 'dom', split_axis=0, concat_axis=0, tiled=True)  17.3 us
    all_to_all x1, starting transfers between devices, per_device(): lax.all_to_all(outgoing, 'dom', split_axis=0, concat_axis=0, tiled=True)  15.7 us
    all_to_all x1, starting transfers between devices, reduce_grads(): lax.all_to_all(chunks, INNER, split_axis=0, concat_axis=0, tiled=True)  14.3 us
    ppermute x5, waiting for transfers between devices, gather_grads(): theirs.append(lax.ppermute(state, INNER, pairs))  13.3 us
    all_to_all x1, starting transfers between devices, per_device(): lax.all_to_all(slots, 'dom', split_axis=0, concat_axis=0, tiled=True)  8.25 us
    ppermute x2, starting transfers between devices, neighbours(): lax.ppermute(low_source, axis, forward)  7.99 us
    pallas_call x1, Pallas kernels, call_forward(): pl.pallas_call(forward_kernel, out_shape=(shape(blocks.shape, BF16), shap...  7.75 us
  transfers between devices with their start and end apart: 13, of which 8 were waited for; matrix products, arithmetic and copies ran while one was open for 1% of the time, Pallas kernels for 6%

profile of v9, /device:TPU:1, one launch (start us, length us, event | category | flops | bytes accessed | tf_op | source)
XLA Modules:
  0.0 142.7 jit_solution(17299483454273409600)
XLA Ops:
  0.6 2.8 %shard_map.128 = bf16[12,128,256]{2,1,0:T(8,128)(2,1)} custom-call(s32[1,12]{1,0:T(1,128)} %send_ref.3, bf16[8,128,256]{2,1,0:T(8,128)(2,1)} %bitcast.13), custom_call_target="tpu_custom_call" | custom-call | tf_op jit(solution)/shard_map/pallas_call | solution.py:421
  3.5 15.7 %all-to-all-start = ((bf16[12,128,256]{2,1,0:T(8,128)(2,1)}), bf16[12,128,256]{2,1,0:T(8,128)(2,1)S(1)}, u32[]{:S(2)}, u32[]{:S(2)}) async-start(bf16[12,128,256]{2,1,0:T(8,128)(2,1)} %shard_map.128), calls=%async_computation | async-start | bytes 1572864 | tf_op jit(solution)/shard_map/all_to_all | solution.py:429
  19.2 0.9 fusion
  20.1 4.0 %collective-permute-start = (bf16[128,256]{1,0:T(8,128)(2,1)S(1)}, bf16[128,256]{1,0:T(8,128)(2,1)S(1)}, u32[]{:S(2)}, u32[]{:S(2)}) collective-permute-start(bf16[128,256]{1,0:T(8,128)(2,1)S(1)} %get-tuple-element.46), channel_id=1, source_target_pairs={{0,1},{1,2},{2,3},{3,4},{4,5},{5,6},{6,7},{7,8},{8,9},{9,10},{10,1... | collective-permute-start | bytes 196616 | tf_op jit(solution)/shard_map/ppermute | solution.py:329
  24.1 1.9 %collective-permute-start.1 = (bf16[128,256]{1,0:T(8,128)(2,1)S(1)}, bf16[128,256]{1,0:T(8,128)(2,1)S(1)}, u32[]{:S(2)}, u32[]{:S(2)}) collective-permute-start(bf16[128,256]{1,0:T(8,128)(2,1)S(1)} %get-tuple-element.45), channel_id=1, source_target_pairs={{1,0},{2,1},{3,2},{4,3},{5,4},{6,5},{7,6},{8,7},{9,8},{10,9},{11,1... | collective-permute-start | bytes 196616 | tf_op jit(solution)/shard_map/ppermute | solution.py:329
  26.0 0.0 collective-permute-done.left_ref
  26.1 0.0 copy-start.4
  26.1 3.9 %collective-permute-done.1.right_ref = bf16[128,256]{1,0:T(8,128)(2,1)S(1)} collective-permute-done((bf16[128,256]{1,0:T(8,128)(2,1)S(1)}, bf16[128,256]{1,0:T(8,128)(2,1)S(1)}, u32[]{:S(2)}, u32[]{:S(2)}) %collective-permute-start.1) | collective-permute-done | bytes 65568 | tf_op jit(solution)/shard_map/ppermute | solution.py:329
  30.0 0.0 copy-start.5
  30.0 17.3 %all-to-all-done.received_hbm = bf16[12,128,256]{2,1,0:T(8,128)(2,1)S(1)} async-done(((bf16[12,128,256]{2,1,0:T(8,128)(2,1)}), bf16[12,128,256]{2,1,0:T(8,128)(2,1)S(1)}, u32[]{:S(2)}, u32[]{:S(2)}) %all-to-all-start) | async-done | bytes 786464 | tf_op jit(solution)/shard_map/all_to_all | solution.py:429
  47.3 0.0 copy-start.3
  47.3 0.0 copy-done.4
  47.3 0.0 copy-done.5
  47.3 0.9 copy-done.3
  48.2 7.8 %shard_map.129 = (bf16[8,128,256]{2,1,0:T(8,128)(2,1)}, bf16[1024,256]{1,0:T(8,128)(2,1)}, bf16[512,256]{1,0:T(8,128)(2,1)}, f32[1,256]{1,0:T(1,128)}) custom-call(s32[8,8]{1,0:T(8,128)} %pairs_ref.3, s32[8,128]{1,0:T(8,128)} %bitcast.18, bf16[256,256]{1,0:T(8,128)(2,1)} %w_self_ref.3, bf16[256,256]{1,0:T(8,128)(2,1)} %w_neigh_ref.3, f32[1,256]{1,0:T(1,128)} %bitcast.20, ...), custom_call_target="tpu_custom_call" | custom-call | flops 2000000000 | bytes 6000000 | tf_op jit(solution)/shard_map/pallas_call | solution.py:269
  56.0 14.3 %all-to-all-start.1 = ((bf16[64,8,256]{2,1,0:T(8,128)(2,1)}), bf16[64,8,256]{2,1,0:T(8,128)(2,1)S(1)}, u32[]{:S(2)}, u32[]{:S(2)}) async-start(bf16[64,8,256]{2,1,0:T(8,128)(2,1)} %bitcast.16), calls=%async_computation.1 | async-start | bytes 524288 | tf_op jit(solution)/shard_map/all_to_all | solution.py:338
  70.3 0.0 copy-start.2
  70.3 7.1 %shard_map.130 = (f32[8,128,256]{2,1,0:T(8,128)}, bf16[2,128,256]{2,1,0:T(8,128)(2,1)}, bf16[12,128,256]{2,1,0:T(8,128)(2,1)}) custom-call(s32[8,8]{1,0:T(8,128)} %pairs_ref.3, s32[8,128]{1,0:T(8,128)} %bitcast.19, bf16[256,256]{1,0:T(8,128)(2,1)} %w_self_ref.3, bf16[256,256]{1,0:T(8,128)(2,1)} %w_neigh_ref.3, bf16[1024,256]{1,0:T(8,128)(2,1)} %get-tuple-element.27.grad_ref, ...), custom_call_target="tpu_custom_call" | custom-call | flops 2000000000 | bytes 8000000 | tf_op jit(solution)/shard_map/pallas_call | solution.py:303
  77.4 0.0 copy-start
  77.4 0.0 copy-start.1
  77.4 4.9 %all-to-all-done.1.pieces_ref = bf16[64,8,256]{2,1,0:T(8,128)(2,1)S(1)} async-done(((bf16[64,8,256]{2,1,0:T(8,128)(2,1)}), bf16[64,8,256]{2,1,0:T(8,128)(2,1)S(1)}, u32[]{:S(2)}, u32[]{:S(2)}) %all-to-all-start.1) | async-done | bytes 262176 | tf_op jit(solution)/shard_map/all_to_all | solution.py:338
  82.3 0.0 copy-done.2
  82.3 0.7 shard_map.131
  83.0 5.3 %all-to-all-start.2 = ((bf16[24,24,128]{2,1,0:T(8,128)(2,1)}), bf16[24,24,128]{2,1,0:T(8,128)(2,1)S(1)}, u32[]{:S(2)}, u32[]{:S(2)}) async-start(bf16[24,24,128]{2,1,0:T(8,128)(2,1)} %shard_map.131), calls=%async_computation.2 | async-start | bytes 294912 | tf_op jit(solution)/shard_map/all_to_all | solution.py:348
  88.3 0.9 slice_bitcast_fusion
  89.2 3.9 %collective-permute-start.2 = (bf16[128,256]{1,0:T(8,128)(2,1)S(1)}, bf16[128,256]{1,0:T(8,128)(2,1)S(1)}, u32[]{:S(2)}, u32[]{:S(2)}) collective-permute-start(bf16[128,256]{1,0:T(8,128)(2,1)S(1)} %get-tuple-element.48), channel_id=1, source_target_pairs={{0,1},{1,2},{2,3},{3,4},{4,5},{5,6},{6,7},{7,8},{8,9},{9,10},{10,1... | collective-permute-start | bytes 196616 | tf_op jit(solution)/shard_map/ppermute | solution.py:329
  93.1 1.9 %collective-permute-start.3 = (bf16[128,256]{1,0:T(8,128)(2,1)S(1)}, bf16[128,256]{1,0:T(8,128)(2,1)S(1)}, u32[]{:S(2)}, u32[]{:S(2)}) collective-permute-start(bf16[128,256]{1,0:T(8,128)(2,1)S(1)} %get-tuple-element.47), channel_id=1, source_target_pairs={{1,0},{2,1},{3,2},{4,3},{5,4},{6,5},{7,6},{8,7},{9,8},{10,9},{11,1... | collective-permute-start | bytes 196616 | tf_op jit(solution)/shard_map/ppermute | solution.py:329
  95.1 4.1 %all-to-all-done.2.spread_ref = bf16[24,24,128]{2,1,0:T(8,128)(2,1)S(1)} async-done(((bf16[24,24,128]{2,1,0:T(8,128)(2,1)}), bf16[24,24,128]{2,1,0:T(8,128)(2,1)S(1)}, u32[]{:S(2)}, u32[]{:S(2)}) %all-to-all-start.2) | async-done | bytes 147488 | tf_op jit(solution)/shard_map/all_to_all | solution.py:348
  99.2 0.0 collective-permute-done.2.low_ref
  99.2 0.0 collective-permute-done.3.high_ref
  99.3 8.3 %all-to-all-start.3 = ((bf16[12,128,256]{2,1,0:T(8,128)(2,1)}), bf16[12,128,256]{2,1,0:T(8,128)(2,1)S(1)}, u32[]{:S(2)}, u32[]{:S(2)}) async-start(bf16[12,128,256]{2,1,0:T(8,128)(2,1)} %get-tuple-element.37), calls=%async_computation.3 | async-start | bytes 1572864 | tf_op jit(solution)/shard_map/all_to_all | solution.py:450
  107.5 4.0 %collective-permute-start.4 = (bf16[3,16,128]{2,1,0:T(8,128)(2,1)S(1)}, bf16[3,16,128]{2,1,0:T(8,128)(2,1)S(1)}, u32[]{:S(2)}, u32[]{:S(2)}) collective-permute-start(bf16[3,16,128]{2,1,0:T(8,128)(2,1)S(1)} %shard_map.132.mine_ref), channel_id=1, source_target_pairs={{0,32},{1,33},{2,34},{3,35},{4,36},{5,37},{6,38},{7,39},{8,40},{9,... | collective-permute-start | bytes 36872 | tf_op jit(solution)/shard_map/ppermute | solution.py:370
  111.6 2.2 %collective-permute-done.4.refs_0_ = bf16[3,16,128]{2,1,0:T(8,128)(2,1)S(1)} collective-permute-done((bf16[3,16,128]{2,1,0:T(8,128)(2,1)S(1)}, bf16[3,16,128]{2,1,0:T(8,128)(2,1)S(1)}, u32[]{:S(2)}, u32[]{:S(2)}) %collective-permute-start.4) | collective-permute-done | bytes 12320 | tf_op jit(solution)/shard_map/ppermute | solution.py:370
  113.8 2.4 %collective-permute-start.5 = (bf16[5,16,128]{2,1,0:T(8,128)(2,1)S(1)}, bf16[5,16,128]{2,1,0:T(8,128)(2,1)S(1)}, u32[]{:S(2)}, u32[]{:S(2)}) collective-permute-start(bf16[5,16,128]{2,1,0:T(8,128)(2,1)S(1)} %shard_map.133.mine_ref), channel_id=1, source_target_pairs={{0,16},{1,17},{2,18},{3,19},{4,20},{5,21},{6,22},{7,23},{8,24},{9,... | collective-permute-start | bytes 61448 | tf_op jit(solution)/shard_map/ppermute | solution.py:370
  116.2 2.4 %collective-permute-done.5.refs_0_ = bf16[5,16,128]{2,1,0:T(8,128)(2,1)S(1)} collective-permute-done((bf16[5,16,128]{2,1,0:T(8,128)(2,1)S(1)}, bf16[5,16,128]{2,1,0:T(8,128)(2,1)S(1)}, u32[]{:S(2)}, u32[]{:S(2)}) %collective-permute-start.5) | collective-permute-done | bytes 20512 | tf_op jit(solution)/shard_map/ppermute | solution.py:370
  118.6 3.9 %collective-permute-start.6 = (bf16[9,16,128]{2,1,0:T(8,128)(2,1)S(1)}, bf16[9,16,128]{2,1,0:T(8,128)(2,1)S(1)}, u32[]{:S(2)}, u32[]{:S(2)}) collective-permute-start(bf16[9,16,128]{2,1,0:T(8,128)(2,1)S(1)} %shard_map.134.mine_ref), channel_id=1, source_target_pairs={{0,8},{1,9},{2,10},{3,11},{4,12},{5,13},{6,14},{7,15},{8,0},{9,1},... | collective-permute-start | bytes 110600 | tf_op jit(solution)/shard_map/ppermute | solution.py:370
  122.5 5.0 %collective-permute-done.6.refs_0_ = bf16[9,16,128]{2,1,0:T(8,128)(2,1)S(1)} collective-permute-done((bf16[9,16,128]{2,1,0:T(8,128)(2,1)S(1)}, bf16[9,16,128]{2,1,0:T(8,128)(2,1)S(1)}, u32[]{:S(2)}, u32[]{:S(2)}) %collective-permute-start.6) | collective-permute-done | bytes 36896 | tf_op jit(solution)/shard_map/ppermute | solution.py:370
  127.5 3.4 %collective-permute-start.7 = (bf16[17,16,128]{2,1,0:T(8,128)(2,1)S(1)}, bf16[17,16,128]{2,1,0:T(8,128)(2,1)S(1)}, u32[]{:S(2)}, u32[]{:S(2)}) collective-permute-start(bf16[17,16,128]{2,1,0:T(8,128)(2,1)S(1)} %shard_map.135.mine_ref), channel_id=1, source_target_pairs={{0,4},{1,5},{2,6},{3,7},{4,0},{5,1},{6,2},{7,3},{8,12},{9,13},{10,... | collective-permute-start | bytes 208904 | tf_op jit(solution)/shard_map/ppermute | solution.py:370
  130.9 3.6 %collective-permute-done.7.refs_0_ = bf16[17,16,128]{2,1,0:T(8,128)(2,1)S(1)} collective-permute-done((bf16[17,16,128]{2,1,0:T(8,128)(2,1)S(1)}, bf16[17,16,128]{2,1,0:T(8,128)(2,1)S(1)}, u32[]{:S(2)}, u32[]{:S(2)}) %collective-permute-start.7) | collective-permute-done | bytes 69664 | tf_op jit(solution)/shard_map/ppermute | solution.py:370
  134.6 5.7 %collective-permute-start.8 = (bf16[33,16,128]{2,1,0:T(8,128)(2,1)S(1)}, bf16[33,16,128]{2,1,0:T(8,128)(2,1)S(1)}, u32[]{:S(2)}, u32[]{:S(2)}) collective-permute-start(bf16[33,16,128]{2,1,0:T(8,128)(2,1)S(1)} %shard_map.136.mine_ref), channel_id=1, source_target_pairs={{0,1},{1,0},{2,3},{3,2},{4,5},{5,4},{6,7},{7,6},{8,9},{9,8},{10,11... | collective-permute-start | bytes 405512 | tf_op jit(solution)/shard_map/ppermute | solution.py:370
  140.2 0.0 all-to-all-done.3.returned_ref
  140.2 0.0 copy-done
  140.2 0.0 copy-done.1
  140.2 1.6 %shard_map.137 = bf16[8,128,256]{2,1,0:T(8,128)(2,1)} custom-call(s32[1,12]{1,0:T(1,128)S(1)} %copy-done.1, f32[8,128,256]{2,1,0:T(8,128)S(1)} %copy-done, bf16[12,128,256]{2,1,0:T(8,128)(2,1)S(1)} %all-to-all-done.3.returned_ref, bf16[128,256]{1,0:T(8,128)(2,1)S(1)} %collective-permute-done.2.low_ref, bf16[128,256]{1,0:T(8,128)(2,1)S(1)} %collective-permute-done.3.high_ref), custom_call_target="tpu_custom_call" | custom-call | flops 1000000 | bytes 3000000 | tf_op jit(solution)/shard_map/pallas_call | solution.py:451
  141.9 0.0 collective-permute-done.8.refs_0_
  141.9 0.8 shard_map.139
  (6 shorter events, 0.1 us)
Async XLA Ops:
  3.5 43.9 %all-to-all-start = ((bf16[12,128,256]{2,1,0:T(8,128)(2,1)}), bf16[12,128,256]{2,1,0:T(8,128)(2,1)S(1)}, u32[]{:S(2)}, u32[]{:S(2)}) async-start(bf16[12,128,256]{2,1,0:T(8,128)(2,1)} %shard_map.128), calls=%async_computation | async-start | bytes 1572864 | tf_op jit(solution)/shard_map/all_to_all | solution.py:429
  20.1 6.0 %collective-permute-start = (bf16[128,256]{1,0:T(8,128)(2,1)S(1)}, bf16[128,256]{1,0:T(8,128)(2,1)S(1)}, u32[]{:S(2)}, u32[]{:S(2)}) collective-permute-start(bf16[128,256]{1,0:T(8,128)(2,1)S(1)} %get-tuple-element.46), channel_id=1, source_target_pairs={{0,1},{1,2},{2,3},{3,4},{4,5},{5,6},{6,7},{7,8},{8,9},{9,10},{10,1... | collective-permute-start | bytes 196616 | tf_op jit(solution)/shard_map/ppermute | solution.py:329
  24.1 5.9 %collective-permute-start.1 = (bf16[128,256]{1,0:T(8,128)(2,1)S(1)}, bf16[128,256]{1,0:T(8,128)(2,1)S(1)}, u32[]{:S(2)}, u32[]{:S(2)}) collective-permute-start(bf16[128,256]{1,0:T(8,128)(2,1)S(1)} %get-tuple-element.45), channel_id=1, source_target_pairs={{1,0},{2,1},{3,2},{4,3},{5,4},{6,5},{7,6},{8,7},{9,8},{10,9},{11,1... | collective-permute-start | bytes 196616 | tf_op jit(solution)/shard_map/ppermute | solution.py:329
  26.1 21.3 %copy-start.4 = (bf16[128,256]{1,0:T(8,128)(2,1)}, bf16[128,256]{1,0:T(8,128)(2,1)S(1)}, u32[]{:S(2)}) copy-start(bf16[128,256]{1,0:T(8,128)(2,1)S(1)} %collective-permute-done.left_ref) | copy-start | bytes 196612
  30.0 17.3 %copy-start.5 = (bf16[128,256]{1,0:T(8,128)(2,1)}, bf16[128,256]{1,0:T(8,128)(2,1)S(1)}, u32[]{:S(2)}) copy-start(bf16[128,256]{1,0:T(8,128)(2,1)S(1)} %collective-permute-done.1.right_ref) | copy-start | bytes 196612
  47.3 0.9 copy-start.3
  56.0 26.3 %all-to-all-start.1 = ((bf16[64,8,256]{2,1,0:T(8,128)(2,1)}), bf16[64,8,256]{2,1,0:T(8,128)(2,1)S(1)}, u32[]{:S(2)}, u32[]{:S(2)}) async-start(bf16[64,8,256]{2,1,0:T(8,128)(2,1)} %bitcast.16), calls=%async_computation.1 | async-start | bytes 524288 | tf_op jit(solution)/shard_map/all_to_all | solution.py:338
  70.3 12.0 %copy-start.2 = (f32[1,256]{1,0:T(1,128)S(1)}, f32[1,256]{1,0:T(1,128)}, u32[]{:S(2)}) copy-start(f32[1,256]{1,0:T(1,128)} %get-tuple-element.32.gbias_ref) | copy-start | bytes 3076
  77.4 62.8 %copy-start = (f32[8,128,256]{2,1,0:T(8,128)S(1)}, f32[8,128,256]{2,1,0:T(8,128)}, u32[]{:S(2)}) copy-start(f32[8,128,256]{2,1,0:T(8,128)} %get-tuple-element.36.own_ref) | copy-start | bytes 3145732
  77.4 62.8 %copy-start.1 = (s32[1,12]{1,0:T(1,128)S(1)}, s32[1,12]{1,0:T(1,128)}, u32[]{:S(2)}) copy-start(s32[1,12]{1,0:T(1,128)} %send_ref.3) | copy-start | bytes 148
  83.0 16.2 %all-to-all-start.2 = ((bf16[24,24,128]{2,1,0:T(8,128)(2,1)}), bf16[24,24,128]{2,1,0:T(8,128)(2,1)S(1)}, u32[]{:S(2)}, u32[]{:S(2)}) async-start(bf16[24,24,128]{2,1,0:T(8,128)(2,1)} %shard_map.131), calls=%async_computation.2 | async-start | bytes 294912 | tf_op jit(solution)/shard_map/all_to_all | solution.py:348
  89.2 10.1 %collective-permute-start.2 = (bf16[128,256]{1,0:T(8,128)(2,1)S(1)}, bf16[128,256]{1,0:T(8,128)(2,1)S(1)}, u32[]{:S(2)}, u32[]{:S(2)}) collective-permute-start(bf16[128,256]{1,0:T(8,128)(2,1)S(1)} %get-tuple-element.48), channel_id=1, source_target_pairs={{0,1},{1,2},{2,3},{3,4},{4,5},{5,6},{6,7},{7,8},{8,9},{9,10},{10,1... | collective-permute-start | bytes 196616 | tf_op jit(solution)/shard_map/ppermute | solution.py:329
  93.1 6.1 %collective-permute-start.3 = (bf16[128,256]{1,0:T(8,128)(2,1)S(1)}, bf16[128,256]{1,0:T(8,128)(2,1)S(1)}, u32[]{:S(2)}, u32[]{:S(2)}) collective-permute-start(bf16[128,256]{1,0:T(8,128)(2,1)S(1)} %get-tuple-element.47), channel_id=1, source_target_pairs={{1,0},{2,1},{3,2},{4,3},{5,4},{6,5},{7,6},{8,7},{9,8},{10,9},{11,1... | collective-permute-start | bytes 196616 | tf_op jit(solution)/shard_map/ppermute | solution.py:329
  99.3 40.9 %all-to-all-start.3 = ((bf16[12,128,256]{2,1,0:T(8,128)(2,1)}), bf16[12,128,256]{2,1,0:T(8,128)(2,1)S(1)}, u32[]{:S(2)}, u32[]{:S(2)}) async-start(bf16[12,128,256]{2,1,0:T(8,128)(2,1)} %get-tuple-element.37), calls=%async_computation.3 | async-start | bytes 1572864 | tf_op jit(solution)/shard_map/all_to_all | solution.py:450
  107.5 6.2 %collective-permute-start.4 = (bf16[3,16,128]{2,1,0:T(8,128)(2,1)S(1)}, bf16[3,16,128]{2,1,0:T(8,128)(2,1)S(1)}, u32[]{:S(2)}, u32[]{:S(2)}) collective-permute-start(bf16[3,16,128]{2,1,0:T(8,128)(2,1)S(1)} %shard_map.132.mine_ref), channel_id=1, source_target_pairs={{0,32},{1,33},{2,34},{3,35},{4,36},{5,37},{6,38},{7,39},{8,40},{9,... | collective-permute-start | bytes 36872 | tf_op jit(solution)/shard_map/ppermute | solution.py:370
  113.8 4.8 %collective-permute-start.5 = (bf16[5,16,128]{2,1,0:T(8,128)(2,1)S(1)}, bf16[5,16,128]{2,1,0:T(8,128)(2,1)S(1)}, u32[]{:S(2)}, u32[]{:S(2)}) collective-permute-start(bf16[5,16,128]{2,1,0:T(8,128)(2,1)S(1)} %shard_map.133.mine_ref), channel_id=1, source_target_pairs={{0,16},{1,17},{2,18},{3,19},{4,20},{5,21},{6,22},{7,23},{8,24},{9,... | collective-permute-start | bytes 61448 | tf_op jit(solution)/shard_map/ppermute | solution.py:370
  118.6 8.9 %collective-permute-start.6 = (bf16[9,16,128]{2,1,0:T(8,128)(2,1)S(1)}, bf16[9,16,128]{2,1,0:T(8,128)(2,1)S(1)}, u32[]{:S(2)}, u32[]{:S(2)}) collective-permute-start(bf16[9,16,128]{2,1,0:T(8,128)(2,1)S(1)} %shard_map.134.mine_ref), channel_id=1, source_target_pairs={{0,8},{1,9},{2,10},{3,11},{4,12},{5,13},{6,14},{7,15},{8,0},{9,1},... | collective-permute-start | bytes 110600 | tf_op jit(solution)/shard_map/ppermute | solution.py:370
  127.5 7.0 %collective-permute-start.7 = (bf16[17,16,128]{2,1,0:T(8,128)(2,1)S(1)}, bf16[17,16,128]{2,1,0:T(8,128)(2,1)S(1)}, u32[]{:S(2)}, u32[]{:S(2)}) collective-permute-start(bf16[17,16,128]{2,1,0:T(8,128)(2,1)S(1)} %shard_map.135.mine_ref), channel_id=1, source_target_pairs={{0,4},{1,5},{2,6},{3,7},{4,0},{5,1},{6,2},{7,3},{8,12},{9,13},{10,... | collective-permute-start | bytes 208904 | tf_op jit(solution)/shard_map/ppermute | solution.py:370
  134.6 7.3 %collective-permute-start.8 = (bf16[33,16,128]{2,1,0:T(8,128)(2,1)S(1)}, bf16[33,16,128]{2,1,0:T(8,128)(2,1)S(1)}, u32[]{:S(2)}, u32[]{:S(2)}) collective-permute-start(bf16[33,16,128]{2,1,0:T(8,128)(2,1)S(1)} %shard_map.136.mine_ref), channel_id=1, source_target_pairs={{0,1},{1,0},{2,3},{3,2},{4,5},{5,4},{6,7},{7,6},{8,9},{9,8},{10,11... | collective-permute-start | bytes 405512 | tf_op jit(solution)/shard_map/ppermute | solution.py:370
